TPU v7x, 256 devices: a whole 4x4x8 slice. The times are simulated.
256 devices in a mesh: grp: 8 (over z), brick: 32 (over x, y, core).
Axes of the slice: x: 4, y: 4, z: 8, core: 2. Of those that a mesh axis runs over, the one named last changes fastest.
Arguments:
- store: bfloat16 [768, 256, 256], P(('grp', 'brick')), may hold values from -0.005859375 to 0.005859375
- crossing: int32 [256, 16], P('grp'), may hold values from 0 to 95, as said below
- phi: bfloat16 [64, 256, 16, 1024], P('grp', 'brick'), may hold values from -6 to 6
- rows_index: int32 [256, 16, 256], P(('grp', 'brick')), may hold values from 0 to 1023
- cols_index: int32 [256, 16, 256], P(('grp', 'brick')), may hold values from 0 to 1023
Outputs:
- hamiltonian: float32 [768, 256, 256], P(('grp', 'brick'))
Inputs may be any that keep to these rules, and one draw needn't show every extreme that they name: `crossing`: each row lists 16 different blocks of its group; block k of a group is held by the device with brick index k // 3 of that group. A row names at most 1 block held by one device, and exactly 1 of some device.
All inputs are finite; a program needn't handle non-finite values.
Results may differ from a plain program's by a relative error of at most 0.0029.
Values may be sent and summed in bfloat16 or wider, within the bound.
No kernel may reach another device: no remote copies, remote signals or barrier semaphores. Data moves between devices by JAX's collectives and lax.ppermute only.
A program may use at most 128 MiB of HBM per device.

v0:
```python
import math

import jax
import jax.numpy as jnp
from jax import lax
from jax.sharding import PartitionSpec as P

CAP = 1


GRAD_WEIGHT = 0.5


def extended(block, sides, width):
    for axis, dim in sides:
        count = lax.axis_size(axis)
        forward = [(i, i + 1) for i in range(count - 1)]
        forward.append((count - 1, 0))
        backward = [(target, source) for source, target in forward]
        low = lax.ppermute(
            lax.slice_in_dim(block, block.shape[dim] - width, None, axis=dim), axis, forward
        )
        high = lax.ppermute(lax.slice_in_dim(block, 0, width, axis=dim), axis, backward)
        block = jnp.concatenate([low, block, high], axis=dim)
    return block


def owner_rank(owners):
    count = owners.shape[-1]
    same_owner = owners[..., :, None] == owners[..., None, :]
    before = jnp.arange(count)[None, :] < jnp.arange(count)[:, None]
    return jnp.sum(same_owner & before, axis=-1)


def flux_of(padded):
    centre = padded[1:-1, 1:-1]
    grad_x = (padded[2:, 1:-1] - padded[:-2, 1:-1]) * 0.5
    grad_y = (padded[1:-1, 2:] - padded[1:-1, :-2]) * 0.5
    grad_z = (jnp.roll(centre, -1, 2) - jnp.roll(centre, 1, 2)) * 0.5
    sigma = grad_x * grad_x + grad_y * grad_y + grad_z * grad_z
    factor = 2.0 * GRAD_WEIGHT / (1.0 + sigma)
    return (factor * grad_x, factor * grad_y, factor * grad_z)


def along_z(field):
    return (jnp.roll(field, -1, 2) - jnp.roll(field, 1, 2)) * 0.5


def local(store, crossing, phi, rows_index, cols_index):
    brick_count = lax.axis_size("brick")
    position = lax.axis_index("brick")
    own_count = store.shape[0]
    width = store.shape[1]
    owners = crossing // own_count
    local_ids = crossing % own_count
    ranks = owner_rank(owners)
    slot_iota = jnp.arange(CAP, dtype=jnp.int32)
    chosen = (owners == position)[:, None, :] & (ranks[:, None, :] == slot_iota[None, :, None])
    filled = jnp.any(chosen, axis=-1)
    send_ids = jnp.sum(jnp.where(chosen, local_ids[:, None, :], 0), axis=-1)
    my_row = lax.dynamic_index_in_dim(crossing, position, 0, keepdims=False)
    my_owner = my_row // own_count
    my_slot = my_owner * CAP + owner_rank(my_owner)
    piece = lax.all_gather(store, "brick", axis=0, tiled=True)
    count = piece.shape[0]
    select = (my_row[:, None] == jnp.arange(count, dtype=jnp.int32)[None, :]).astype(piece.dtype)
    picked = jnp.einsum("jn,nab->jab", select, piece, preferred_element_type=jnp.float32)
    blocks = picked.astype(jnp.bfloat16)
    size_x, size_y, size_z = (phi.shape[0], phi.shape[1], phi.shape[2])
    points = size_x * size_y * size_z
    table = phi.reshape(points, phi.shape[3]).T
    row_tables = table[rows_index[0]]
    col_tables = table[cols_index[0]]

    def collocate(operands):
        block, left, right = operands
        product = jnp.dot(block, right, preferred_element_type=jnp.float32)
        return jnp.sum(left.astype(jnp.float32) * product, axis=0)

    density = jnp.sum(lax.map(collocate, (blocks, row_tables, col_tables)), axis=0).reshape(
        size_x, size_y, size_z
    )
    padded = extended(density, (("grp", 0), ("brick", 1)), 1)
    flux_x, flux_y, flux_z = flux_of(padded)
    stacked = jnp.stack([flux_x, flux_y])
    outer = extended(stacked, (("grp", 1), ("brick", 2)), 1)
    diverge = (
        (outer[0, 2:, 1:-1] - outer[0, :-2, 1:-1]) * 0.5
        + (outer[1, 1:-1, 2:] - outer[1, 1:-1, :-2]) * 0.5
        + along_z(flux_z)
    )
    potential = density / jnp.sqrt(1.0 + density * density) - diverge
    scaled = potential.reshape(points) * (1.0 / math.sqrt(points))

    def integrate(operands):
        left, right = operands
        weighted = (right.astype(jnp.float32) * scaled[None, :]).astype(jnp.bfloat16)
        return lax.dot_general(
            left, weighted, (((1,), (1,)), ((), ())), preferred_element_type=jnp.float32
        )

    partial_value = lax.map(integrate, (row_tables, col_tables))
    returning = (
        jnp.zeros((brick_count * CAP, width, width), jnp.float32).at[my_slot].set(partial_value)
    )
    returning = returning.reshape(brick_count, CAP, width, width)
    arrived = lax.all_to_all(returning, "brick", split_axis=0, concat_axis=0, tiled=True)
    onehot = (
        filled[:, :, None]
        & (send_ids[:, :, None] == jnp.arange(own_count, dtype=jnp.int32)[None, None, :])
    ).astype(jnp.float32)
    return jnp.einsum("dck,dcab->kab", onehot, arrived, precision=lax.Precision.HIGHEST)


def solution(mesh):
    in_specs = (
        P(("grp", "brick"), None, None),
        P("grp", None),
        P("grp", "brick", None, None),
        P(("grp", "brick"), None, None),
        P(("grp", "brick"), None, None),
    )
    out_specs = P(("grp", "brick"), None, None)
    return jax.shard_map(local, mesh=mesh, in_specs=in_specs, out_specs=out_specs, check_vma=False)
```

profile of v0, /device:TPU:12, one launch (start us, length us, event | category | flops | bytes accessed | tf_op | source)
XLA Modules:
  0.0 345.5 jit_solution(12163844893791678848)
XLA Ops:
  6.5 0.7 all-gather.2.cloned.1.call-update
  7.3 2.9 copy.28
  10.2 0.7 fusion.30
  10.9 0.7 fusion.31
  11.6 18.3 %gather_fusion = bf16[4096,1024]{1,0:T(8,128)(2,1)} fusion(bf16[1024,1024]{1,0:T(8,128)(2,1)S(1)} %bitcast.86, s32[4096]{0:T(1024)S(1)} %broadcast_clamp_fusion.1), kind=kCustom, calls=%fused_computation | custom fusion | bytes 16793600 | tf_op jit(solution)/shard_map/gather | solution.py:72
  29.9 18.3 %gather_fusion.1 = bf16[4096,1024]{1,0:T(8,128)(2,1)} fusion(bf16[1024,1024]{1,0:T(8,128)(2,1)S(1)} %bitcast.87, s32[4096]{0:T(1024)S(1)} %broadcast_clamp_fusion), kind=kCustom, calls=%fused_computation.1 | custom fusion | bytes 16793600 | tf_op jit(solution)/shard_map/gather | solution.py:73
  48.2 0.2 fusion.50
  48.4 0.2 fusion.40
  48.8 30.5 %all-gather.2.cloned.1.call-done = bf16[96,256,256]{2,1,0:T(8,128)(2,1)} async-done(((bf16[3,256,256]{2,1,0:T(8,128)(2,1)}), bf16[96,256,256]{2,1,0:T(8,128)(2,1)}) %all-gather.2.cloned.1.call-update) | async-done | bytes 12582928 | tf_op jit(solution)/shard_map/all_gather | solution.py:64
  79.3 11.4 %fusion.19 = bf16[16,256,256]{2,0,1:T(8,128)(2,1)S(1)} fusion(bf16[96,256,256]{2,1,0:T(8,128)(2,1)} %all-gather.2.cloned.1.call-done, s32[16]{0:T(128)S(1)} %get-tuple-element.83), kind=kOutput, calls=%fused_computation.24 | convolution fusion | flops 202376704 | bytes 14680128 | tf_op jit(solution)/shard_map/jn,nab->jab/dot_general | solution.py:67
  90.7 0.7 copy.30
  91.4 26.5 %while.20 = (s32[]{:T(128)}, f32[16,1024]{1,0:T(8,128)S(1)}, bf16[16,256,1024]{2,1,0:T(8,128)(2,1)}, bf16[16,256,256]{2,1,0:T(8,128)(2,1)S(1)}, bf16[16,256,1024]{2,1,0:T(8,128)(2,1)}, /*index=5*/s32[]{:T(128)}, s32[]{:T(128)}) while((s32[]{:T(128)}, f32[16,1024]{1,0:T(8,128)S(1)}, bf16[16,256,1024]{2,1,0:T(8,128)(2,1)}, ...), condition=%wide.region_6.7_spmd, body=%wide.region_4.6_spmd.sunk | while | flops 135003136 | bytes 1193553 | solution.py:80
  91.4 1.5 fusion.66
  93.0 1.5 fusion.66
  94.7 1.5 fusion.66
  96.4 1.5 fusion.66
  98.0 1.5 fusion.66
  99.7 1.5 fusion.66
  101.3 1.5 fusion.66
  103.0 1.5 fusion.66
  104.6 1.5 fusion.66
  106.3 1.5 fusion.66
  108.0 1.5 fusion.66
  109.6 1.5 fusion.66
  111.3 1.5 fusion.66
  112.9 1.5 fusion.66
  114.6 1.5 fusion.66
  116.2 1.5 fusion.66
  118.1 1.6 collective-permute-start.1
  119.7 1.8 collective-permute-start
  121.6 1.4 collective-permute-done.1
  123.0 0.3 collective-permute-done
  123.4 0.9 collective-permute-start.2
  124.3 1.3 collective-permute-done.2
  125.6 1.7 collective-permute-done.3
  127.5 3.1 collective-permute-start.4
  130.7 1.3 collective-permute-done.4
  132.0 3.5 %collective-permute-done.5 = f32[2,1,8,16]{3,2,1,0:T(8,128)S(1)} collective-permute-done((f32[2,1,8,16]{3,2,1,0:T(8,128)S(1)}, f32[2,1,8,16]{3,2,1,0:T(8,128)S(1)}, u32[]{:S(2)}, u32[]{:S(2)}) %collective-permute-start.5) | collective-permute-done | bytes 1056 | tf_op jit(solution)/shard_map/ppermute | solution.py:20
  135.6 0.5 collective-permute-start.7
  136.2 0.7 collective-permute-done.6
  137.0 3.6 %collective-permute-done.7 = f32[2,10,1,16]{3,2,1,0:T(1,128)S(1)} collective-permute-done((f32[2,10,1,16]{3,2,1,0:T(1,128)S(1)}, f32[2,10,1,16]{3,2,1,0:T(1,128)S(1)}, u32[]{:S(2)}, u32[]{:S(2)}) %collective-permute-start.7) | collective-permute-done | bytes 1312 | tf_op jit(solution)/shard_map/ppermute | solution.py:20
  140.6 36.0 %while.21 = (s32[]{:T(128)}, f32[16,256,256]{2,1,0:T(8,128)}, bf16[16,256,1024]{2,1,0:T(8,128)(2,1)}, bf16[16,256,1024]{2,1,0:T(8,128)(2,1)}, f32[1024]{0:T(1024)S(1)}, /*index=5*/s32[]{:T(128)}) while((s32[]{:T(128)}, f32[16,256,256]{2,1,0:T(8,128)}, bf16[16,256,1024]{2,1,0:T(8,128)(2,1)}, bf16[16,256,1024]{2,1,0:T(8,128)(2,1)}, ...), condition=%wide.region_9.10_spmd, body=%wide.region_8.9_spmd.sunk | while | flops 135004160 | bytes 1316421 | solution.py:102
  140.6 2.3 fusion.69
  142.9 2.2 fusion.69
  145.2 2.3 fusion.69
  147.4 2.2 fusion.69
  149.7 2.2 fusion.69
  151.9 2.2 fusion.69
  154.2 2.2 fusion.69
  156.4 2.3 fusion.69
  158.7 2.3 fusion.69
  160.9 2.3 fusion.69
  163.2 2.3 fusion.69
  165.4 2.2 fusion.69
  167.7 2.3 fusion.69
  169.9 2.2 fusion.69
  172.2 2.2 fusion.69
  174.4 2.2 fusion.69
  176.7 4.2 %broadcast_in_dim.14 = f32[32,256,256]{2,1,0:T(8,128)} broadcast(f32[]{:T(128)} %constant.71.clone.1), dimensions={} | broadcast | bytes 8388612 | tf_op jit(solution)/shard_map/broadcast_in_dim | solution.py:104
  180.9 7.9 %scatter_fusion = f32[32,256,256]{2,1,0:T(8,128)} fusion(f32[32,256,256]{2,1,0:T(8,128)} %broadcast_in_dim.14, s32[16]{0:T(128)S(1)} %fusion.47, f32[16,256,256]{2,1,0:T(8,128)} %get-tuple-element.60), kind=kCustom, calls=%fused_computation.2 | custom fusion | bytes 12582976 | tf_op jit(solution)/shard_map/scatter | solution.py:104
  188.8 12.5 %all-to-all-start = ((f32[32,1,256,256]{3,2,1,0:T(8,128)}), f32[32,1,256,256]{3,2,1,0:T(8,128)}, u32[]{:S(2)}, u32[]{:S(2)}) async-start(f32[32,1,256,256]{3,2,1,0:T(8,128)} %bitcast.88), calls=%async_computation | async-start | bytes 16777216 | tf_op jit(solution)/shard_map/all_to_all | solution.py:107
  201.6 125.6 %all-to-all-done = f32[32,1,256,256]{3,2,1,0:T(8,128)} async-done(((f32[32,1,256,256]{3,2,1,0:T(8,128)}), f32[32,1,256,256]{3,2,1,0:T(8,128)}, u32[]{:S(2)}, u32[]{:S(2)}) %all-to-all-start) | async-done | bytes 8388640 | tf_op jit(solution)/shard_map/all_to_all | solution.py:107
  327.2 10.4 %fusion.16 = f32[3,256,256]{2,0,1:T(4,128)S(1)} fusion(f32[32,1,256,256]{3,2,1,0:T(8,128)} %all-to-all-done, s32[32]{0:T(128)S(1)} %fusion.33, pred[32]{0:T(512)(128)(4,1)S(1)} %get-tuple-element.104), kind=kOutput, calls=%fused_computation.21 | convolution fusion | flops 75497664 | bytes 9175200 | tf_op jit(solution)/shard_map/dck,dcab->kab/dot_general | solution.py:112
  337.6 1.0 copy.33
  (58 shorter events, 3.3 us)
Async XLA Ops:
  6.5 72.8 %all-gather.2.cloned.1.call-start = ((), (), s32[]{:S(2)}) async-start(), calls=%async_computation.1 | async-start | bytes 12976128 | tf_op jit(solution)/shard_map/all_gather | solution.py:64
  29.9 18.3 %copy-start = (s32[32,16]{0,1:T(8,128)S(1)}, s32[32,16]{0,1:T(8,128)}, u32[]{:S(2)}) copy-start(s32[32,16]{0,1:T(8,128)} %param.10) | copy-start | bytes 6148
  118.1 4.9 %collective-permute-start.1 = (f32[1,8,16]{2,1,0:T(8,128)S(1)}, f32[1,8,16]{2,1,0:T(8,128)S(1)}, u32[]{:S(2)}, u32[]{:S(2)}) collective-permute-start(f32[1,8,16]{2,1,0:T(8,128)S(1)} %slice.110), channel_id=1, source_target_pairs={{0,32},{32,64},{64,96},{96,128},{128,160},{160,192},{192,224},{224... | collective-permute-start | bytes 1544 | tf_op jit(solution)/shard_map/ppermute | solution.py:20
  119.7 3.6 %collective-permute-start = (f32[1,8,16]{2,1,0:T(8,128)S(1)}, f32[1,8,16]{2,1,0:T(8,128)S(1)}, u32[]{:S(2)}, u32[]{:S(2)}) collective-permute-start(f32[1,8,16]{2,1,0:T(8,128)S(1)} %slice.107), channel_id=1, source_target_pairs={{32,0},{64,32},{96,64},{128,96},{160,128},{192,160},{224,192},{0,2... | collective-permute-start | bytes 1544 | tf_op jit(solution)/shard_map/ppermute | solution.py:23
  123.4 2.2 collective-permute-start.2
  124.2 3.0 collective-permute-start.3
  127.5 4.5 %collective-permute-start.4 = (f32[2,1,8,16]{3,2,1,0:T(8,128)S(1)}, f32[2,1,8,16]{3,2,1,0:T(8,128)S(1)}, u32[]{:S(2)}, u32[]{:S(2)}) collective-permute-start(f32[2,1,8,16]{3,2,1,0:T(8,128)S(1)} %get-tuple-element.113), channel_id=1, source_target_pairs={{32,0},{64,32},{96,64},{128,96},{160,128},{192,160},{224,192},{0,2... | collective-permute-start | bytes 3080 | tf_op jit(solution)/shard_map/ppermute | solution.py:23
  130.6 4.9 %collective-permute-start.5 = (f32[2,1,8,16]{3,2,1,0:T(8,128)S(1)}, f32[2,1,8,16]{3,2,1,0:T(8,128)S(1)}, u32[]{:S(2)}, u32[]{:S(2)}) collective-permute-start(f32[2,1,8,16]{3,2,1,0:T(8,128)S(1)} %get-tuple-element.112), channel_id=1, source_target_pairs={{0,32},{32,64},{64,96},{96,128},{128,160},{160,192},{192,224},{224... | collective-permute-start | bytes 3080 | tf_op jit(solution)/shard_map/ppermute | solution.py:20
  135.5 1.5 collective-permute-start.6
  135.6 4.9 %collective-permute-start.7 = (f32[2,10,1,16]{3,2,1,0:T(1,128)S(1)}, f32[2,10,1,16]{3,2,1,0:T(1,128)S(1)}, u32[]{:S(2)}, u32[]{:S(2)}) collective-permute-start(f32[2,10,1,16]{3,2,1,0:T(1,128)S(1)} %get-tuple-element.111), channel_id=1, source_target_pairs={{0,1},{1,2},{2,3},{3,4},{4,5},{5,6},{6,7},{7,8},{8,9},{9,10},{10,1... | collective-permute-start | bytes 3848 | tf_op jit(solution)/shard_map/ppermute | solution.py:20
  188.8 138.3 %all-to-all-start = ((f32[32,1,256,256]{3,2,1,0:T(8,128)}), f32[32,1,256,256]{3,2,1,0:T(8,128)}, u32[]{:S(2)}, u32[]{:S(2)}) async-start(f32[32,1,256,256]{3,2,1,0:T(8,128)} %bitcast.88), calls=%async_computation | async-start | bytes 16777216 | tf_op jit(solution)/shard_map/all_to_all | solution.py:107
Sparse Core Ops, SparseCore 0:
  9.9 69.3 all-gather.1
where the time goes:
time: 347 us; the launch traced here: 345 us
  waiting for transfers between devices  171 us (49%)
  matrix products  82.1 us (24%)
  local copies, waits for them, and re-layouts  55.7 us (16%)
  starting transfers between devices  20.5 us (6%)
  between operations  13.6 us (4%)
    all_to_all x1, waiting for transfers between devices, local(): lax.all_to_all(returning, 'brick', split_axis=0, concat_axis=0, tiled=True)  126 us
    dot_general x16, matrix products, integrate(): lax.dot_general(left, weighted, (((1,), (1,)), ((), ())), preferred_eleme...  36 us
    all_gather x1, waiting for transfers between devices, local(): piece = lax.all_gather(store, 'brick', axis=0, tiled=True)  30.5 us
    dot_general x16, matrix products, collocate(): product = jnp.dot(block, right, preferred_element_type=jnp.float32)  24.3 us
    gather x1, local copies, waits for them, and re-layouts, local(): col_tables = table[cols_index[0]]  18.3 us
    gather x1, local copies, waits for them, and re-layouts, local(): row_tables = table[rows_index[0]]  18.3 us
    all_to_all x1, starting transfers between devices, local(): lax.all_to_all(returning, 'brick', split_axis=0, concat_axis=0, tiled=True)  12.5 us
    dot_general x1, matrix products, local(): jnp.einsum('jn,nab->jab', select, piece, preferred_element_type=jnp.float32)  11.4 us
  transfers between devices with their start and end apart: 10, of which 10 were waited for; matrix products, arithmetic and copies ran while one was open for 12% of the time, Pallas kernels for 0%

commit v1 on v0

v1 whole, which is shorter than its diff:
```python
import math

import jax
import jax.numpy as jnp
from jax import lax
from jax.experimental import pallas as pl
from jax.experimental.pallas import tpu as pltpu
from jax.sharding import PartitionSpec as P

GRAD_WEIGHT = 0.5
MIB = 1024 * 1024


def params(mib=40):
    return pltpu.CompilerParams(vmem_limit_bytes=mib * MIB)


def pick_blocks(ids, store, group=4):
    count = ids.shape[0]
    own, rows, cols = store.shape

    def kernel(ids_ref, store_ref, out_ref):
        base = pl.program_id(0) * group
        for i in range(group):
            out_ref[i] = store_ref[ids_ref[base + i]]

    return pl.pallas_call(
        kernel,
        out_shape=jax.ShapeDtypeStruct((count, rows, cols), store.dtype),
        grid_spec=pltpu.PrefetchScalarGridSpec(
            num_scalar_prefetch=1,
            grid=(count // group,),
            in_specs=[pl.BlockSpec((own, rows, cols), lambda i, ids: (0, 0, 0))],
            out_specs=pl.BlockSpec((group, rows, cols), lambda i, ids: (i, 0, 0)),
        ),
        compiler_params=params(),
        name="pick_blocks",
    )(ids, store)


def gather_tables(index, table):
    count, _, width = index.shape
    functions, points = table.shape
    lanes = 128

    def kernel(index_ref, table_ref, out_ref):
        pieces = []
        for start in range(0, width, lanes):
            row = index_ref[0, :, start : start + lanes]
            column = jnp.broadcast_to(row, (lanes, lanes)).T
            hot = [
                jnp.where(
                    column == lax.broadcasted_iota(jnp.int32, (lanes, lanes), 1) + f, 1.0, 0.0
                ).astype(jnp.bfloat16)
                for f in range(0, functions, lanes)
            ]
            pieces.append(jnp.concatenate(hot, axis=1))
        onehot = jnp.concatenate(pieces, axis=0)
        out_ref[0] = jnp.dot(
            onehot, table_ref[...], preferred_element_type=jnp.float32
        ).astype(jnp.bfloat16)

    return pl.pallas_call(
        kernel,
        out_shape=jax.ShapeDtypeStruct((count, width, points), jnp.bfloat16),
        grid=(count,),
        in_specs=[
            pl.BlockSpec((1, 1, width), lambda i: (i, 0, 0)),
            pl.BlockSpec((functions, points), lambda i: (0, 0)),
        ],
        out_specs=pl.BlockSpec((1, width, points), lambda i: (i, 0, 0)),
        compiler_params=params(),
        cost_estimate=pl.CostEstimate(
            flops=2 * count * width * functions * points,
            bytes_accessed=2 * count * width * points,
            transcendentals=0,
        ),
        name="gather_tables",
    )(index, table)


def collocate(slots, blocks, tables):
    count, both, points = tables.shape
    width = both // 2

    def kernel(slots_ref, block_ref, table_ref, out_ref):
        @pl.when(pl.program_id(0) == 0)
        def _():
            out_ref[...] = jnp.zeros_like(out_ref)

        product = jnp.dot(
            block_ref[0], table_ref[0, width:, :], preferred_element_type=jnp.float32
        )
        term = table_ref[0, :width, :].astype(jnp.float32) * product
        out_ref[...] += jnp.sum(term.reshape(width // 8, 8, points), axis=0)

    return pl.pallas_call(
        kernel,
        out_shape=jax.ShapeDtypeStruct((8, points), jnp.float32),
        grid_spec=pltpu.PrefetchScalarGridSpec(
            num_scalar_prefetch=1,
            grid=(count,),
            in_specs=[
                pl.BlockSpec((1, width, width), lambda j, slots: (slots[j], 0, 0)),
                pl.BlockSpec((1, both, points), lambda j, slots: (j, 0, 0)),
            ],
            out_specs=pl.BlockSpec((8, points), lambda j, slots: (0, 0)),
        ),
        compiler_params=params(),
        name="collocate",
    )(slots, blocks, tables)


def integrate(slots, scaled, tables, total):
    count, both, points = tables.shape
    width = both // 2

    def kernel(slots_ref, scaled_ref, table_ref, out_ref):
        weighted = (table_ref[0, width:, :].astype(jnp.float32) * scaled_ref[...]).astype(
            jnp.bfloat16
        )
        out_ref[0] = lax.dot_general(
            table_ref[0, :width, :],
            weighted,
            (((1,), (1,)), ((), ())),
            preferred_element_type=jnp.float32,
        ).astype(jnp.bfloat16)

    return pl.pallas_call(
        kernel,
        out_shape=jax.ShapeDtypeStruct((total, width, width), jnp.bfloat16),
        grid_spec=pltpu.PrefetchScalarGridSpec(
            num_scalar_prefetch=1,
            grid=(count,),
            in_specs=[
                pl.BlockSpec((1, points), lambda j, slots: (0, 0)),
                pl.BlockSpec((1, both, points), lambda j, slots: (j, 0, 0)),
            ],
            out_specs=pl.BlockSpec((1, width, width), lambda j, slots: (slots[j], 0, 0)),
        ),
        compiler_params=params(),
        name="integrate",
    )(slots, scaled, tables)


def add_up(targets, parts, own_count, group=8):
    count, rows, cols = parts.shape

    def kernel(targets_ref, parts_ref, out_ref):
        step = pl.program_id(0)

        @pl.when(step == 0)
        def _():
            out_ref[...] = jnp.zeros_like(out_ref)

        for i in range(group):
            target = targets_ref[step * group + i]

            @pl.when(target >= 0)
            def _():
                out_ref[target] += parts_ref[i].astype(jnp.float32)

    return pl.pallas_call(
        kernel,
        out_shape=jax.ShapeDtypeStruct((own_count, rows, cols), jnp.float32),
        grid_spec=pltpu.PrefetchScalarGridSpec(
            num_scalar_prefetch=1,
            grid=(count // group,),
            in_specs=[pl.BlockSpec((group, rows, cols), lambda i, t: (i, 0, 0))],
            out_specs=pl.BlockSpec((own_count, rows, cols), lambda i, t: (0, 0, 0)),
        ),
        compiler_params=params(),
        name="add_up",
    )(targets, parts)


def extended(block, axis, dim, width):
    count = lax.axis_size(axis)
    forward = [(i, (i + 1) % count) for i in range(count)]
    backward = [(target, source) for source, target in forward]
    size = block.shape[dim]
    low = lax.ppermute(lax.slice_in_dim(block, size - width, size, axis=dim), axis, forward)
    high = lax.ppermute(lax.slice_in_dim(block, 0, width, axis=dim), axis, backward)
    return jnp.concatenate([low, block, high], axis=dim)


def middle(field, dim, width=1):
    return lax.slice_in_dim(field, width, field.shape[dim] - width, axis=dim)


def slope(field, dim):
    size = field.shape[dim]
    return (
        lax.slice_in_dim(field, 2, size, axis=dim) - lax.slice_in_dim(field, 0, size - 2, axis=dim)
    ) * 0.5


def slope_z(field):
    return (jnp.roll(field, -1, 2) - jnp.roll(field, 1, 2)) * 0.5


def potential_of(padded):
    grad_x = middle(slope(padded, 0), 1)
    grad_y = middle(slope(padded, 1), 0)
    centre = middle(middle(padded, 0), 1)
    grad_z = slope_z(centre)
    sigma = grad_x * grad_x + grad_y * grad_y + grad_z * grad_z
    factor = 2.0 * GRAD_WEIGHT / (1.0 + sigma)
    flux_z = middle(middle(factor * grad_z, 0), 1)
    diverge = (
        middle(slope(factor * grad_x, 0), 1) + middle(slope(factor * grad_y, 1), 0) + slope_z(flux_z)
    )
    density = middle(middle(centre, 0), 1)
    return density / jnp.sqrt(1.0 + density * density) - diverge


def local(store, crossing, phi, rows_index, cols_index):
    position = lax.axis_index("brick")
    brick_count = lax.axis_size("brick")
    own_count, width = store.shape[0], store.shape[1]
    size_x, size_y, size_z, functions = phi.shape
    points = size_x * size_y * size_z
    owners = crossing // own_count
    chosen = owners == position
    filled = jnp.any(chosen, axis=-1)
    send_ids = jnp.sum(jnp.where(chosen, crossing % own_count, 0), axis=-1)
    slots = lax.dynamic_index_in_dim(owners, position, 0, keepdims=False)

    sending = pick_blocks(send_ids, store)
    blocks = lax.all_to_all(sending, "brick", split_axis=0, concat_axis=0, tiled=True)
    table = phi.reshape(points, functions).T
    index = jnp.concatenate([rows_index[0], cols_index[0]], axis=1)[:, None, :]
    tables = gather_tables(index, table)
    density = jnp.sum(collocate(slots, blocks, tables), axis=0).reshape(size_x, size_y, size_z)
    padded = extended(extended(density, "grp", 0, 2), "brick", 1, 2)
    scaled = potential_of(padded).reshape(1, points) * (1.0 / math.sqrt(points))
    returning = integrate(slots, scaled, tables, brick_count)
    arrived = lax.all_to_all(returning, "brick", split_axis=0, concat_axis=0, tiled=True)
    targets = jnp.where(filled, send_ids, -1)
    return add_up(targets, arrived, own_count)


def solution(mesh):
    in_specs = (
        P(("grp", "brick"), None, None),
        P("grp", None),
        P("grp", "brick", None, None),
        P(("grp", "brick"), None, None),
        P(("grp", "brick"), None, None),
    )
    out_specs = P(("grp", "brick"), None, None)
    return jax.shard_map(local, mesh=mesh, in_specs=in_specs, out_specs=out_specs, check_vma=False)
```

time: 347 us -> 178 us (0.51)
  the two profiles are of different devices: /device:TPU:12 before, /device:TPU:96 now
where the time goes in v1:
time: 178 us; the launch traced here: 175 us
  waiting for transfers between devices  86.5 us (49%)
  Pallas kernels  56 us (31%)
  starting transfers between devices  22.7 us (13%)
  local copies, waits for them, and re-layouts  8.69 us (5%)
    all_to_all x1, waiting for transfers between devices, local(): lax.all_to_all(returning, 'brick', split_axis=0, concat_axis=0, tiled=True)  52.7 us
    all_to_all x1, waiting for transfers between devices, local(): lax.all_to_all(sending, 'brick', split_axis=0, concat_axis=0, tiled=True)  27.5 us
    pallas_call x1, Pallas kernels, gather_tables(): pl.pallas_call(kernel, out_shape=jax.ShapeDtypeStruct((count, width, poin...  22.1 us
    pallas_call x1, Pallas kernels, collocate(): pl.pallas_call(kernel, out_shape=jax.ShapeDtypeStruct((8, points), jnp.fl...  14.2 us
    pallas_call x1, Pallas kernels, integrate(): pl.pallas_call(kernel, out_shape=jax.ShapeDtypeStruct((total, width, widt...  14.1 us
    all_to_all x1, starting transfers between devices, local(): lax.all_to_all(sending, 'brick', split_axis=0, concat_axis=0, tiled=True)  7.58 us
    all_to_all x1, starting transfers between devices, local(): lax.all_to_all(returning, 'brick', split_axis=0, concat_axis=0, tiled=True)  6.82 us
    ppermute x2, starting transfers between devices, extended(): lax.ppermute(lax.slice_in_dim(block, 0, width, axis=dim), axis, backward)  5.07 us
  transfers between devices with their start and end apart: 6, of which 5 were waited for; matrix products, arithmetic and copies ran while one was open for 2% of the time, Pallas kernels for 13%

profile of v1, /device:TPU:96, one launch (start us, length us, event | category | flops | bytes accessed | tf_op | source)
XLA Modules:
  0.0 175.2 jit_solution(214957726245346593)
XLA Ops:
  0.0 0.7 fusion.14
  0.7 0.0 copy-start.2
  0.7 1.0 copy-done.2
  1.7 0.9 pick_blocks.1
  2.7 0.0 copy-start.1
  2.7 2.0 %copy-done.1 = bf16[32,256,256]{2,1,0:T(8,128)(2,1)} copy-done((bf16[32,256,256]{2,1,0:T(8,128)(2,1)}, bf16[32,256,256]{2,1,0:T(8,128)(2,1)S(1)}, u32[]{:S(2)}) %copy-start.1) | copy-done | bytes 4194328
  4.6 0.0 copy-start.3
  4.6 0.0 copy-start.4
  4.6 7.6 %all-to-all-start = ((bf16[32,256,256]{2,1,0:T(8,128)(2,1)}), bf16[32,256,256]{2,1,0:T(8,128)(2,1)}, u32[]{:S(2)}, u32[]{:S(2)}) async-start(bf16[32,256,256]{2,1,0:T(8,128)(2,1)} %copy-done.1), calls=%async_computation | async-start | bytes 8388608 | tf_op jit(solution)/shard_map/all_to_all | solution.py:230
  12.2 0.0 copy-done.3
  12.2 0.0 copy-done.4
  12.3 2.9 %copy.7 = bf16[1024,1024]{0,1:T(8,128)(2,1)S(1)} copy(bf16[1024,1024]{1,0:T(8,128)(2,1)} %bitcast.5) | data formatting | bytes 4194304 | tf_op jit(solution)/shard_map/reshape | solution.py:231
  15.2 0.2 dynamic-slice_reduce_fusion.slots_ref
  15.4 22.1 %gather_tables.1.table_ref = bf16[16,512,1024]{2,1,0:T(8,128)(2,1)} custom-call(s32[16,1,512]{2,1,0:T(1,128)S(1)} %broadcast_in_dim.10.index_ref, bf16[1024,1024]{1,0:T(8,128)(2,1)S(1)} %bitcast.4), custom_call_target="tpu_custom_call" | custom-call | flops 17179869184 | bytes 16777216 | tf_op jit(solution)/shard_map/gather_tables/pallas_call | solution.py:63
  37.5 27.5 %all-to-all-done.block_ref = bf16[32,256,256]{2,1,0:T(8,128)(2,1)} async-done(((bf16[32,256,256]{2,1,0:T(8,128)(2,1)}), bf16[32,256,256]{2,1,0:T(8,128)(2,1)}, u32[]{:S(2)}, u32[]{:S(2)}) %all-to-all-start) | async-done | bytes 4194336 | tf_op jit(solution)/shard_map/all_to_all | solution.py:230
  65.0 14.2 %collocate.1 = f32[8,1024]{1,0:T(8,128)S(1)} custom-call(s32[16]{0:T(128)S(1)} %dynamic-slice_reduce_fusion.slots_ref, bf16[32,256,256]{2,1,0:T(8,128)(2,1)} %all-to-all-done.block_ref, bf16[16,512,1024]{2,1,0:T(8,128)(2,1)} %gather_tables.1.table_ref), custom_call_target="tpu_custom_call" | custom-call | tf_op jit(solution)/shard_map/collocate/pallas_call | solution.py:97
  79.3 0.1 slice.120
  79.4 3.1 %collective-permute-start = (f32[2,8,16]{2,1,0:T(8,128)S(1)}, f32[2,8,16]{2,1,0:T(8,128)S(1)}, u32[]{:S(2)}, u32[]{:S(2)}) collective-permute-start(f32[2,8,16]{2,1,0:T(8,128)S(1)} %slice.120), channel_id=1, source_target_pairs={{0,32},{32,64},{64,96},{96,128},{128,160},{160,192},{192,224},{224... | collective-permute-start | bytes 3080 | tf_op jit(solution)/shard_map/ppermute | solution.py:182
  82.5 0.1 reshape.40
  82.6 0.1 slice.122
  82.7 0.0 collective-permute-start.1
  82.7 1.2 collective-permute-done
  83.9 3.7 %collective-permute-done.1 = f32[2,8,16]{2,1,0:T(8,128)S(1)} collective-permute-done((f32[2,8,16]{2,1,0:T(8,128)S(1)}, f32[2,8,16]{2,1,0:T(8,128)S(1)}, u32[]{:S(2)}, u32[]{:S(2)}) %collective-permute-start.1) | collective-permute-done | bytes 1056 | tf_op jit(solution)/shard_map/ppermute | solution.py:183
  87.5 0.1 collective-permute-start.2
  87.6 5.1 %collective-permute-start.3 = (f32[12,2,16]{2,1,0:T(2,128)S(1)}, f32[12,2,16]{2,1,0:T(2,128)S(1)}, u32[]{:S(2)}, u32[]{:S(2)}) collective-permute-start(f32[12,2,16]{2,1,0:T(2,128)S(1)} %get-tuple-element.27), channel_id=1, source_target_pairs={{1,0},{2,1},{3,2},{4,3},{5,4},{6,5},{7,6},{8,7},{9,8},{10,9},{11,1... | collective-permute-start | bytes 4616 | tf_op jit(solution)/shard_map/ppermute | solution.py:183
  92.7 1.4 collective-permute-done.2
  94.1 0.0 collective-permute-done.3
  94.1 0.1 fusion.18
  94.2 0.1 fusion.19
  94.3 0.1 fusion.16
  94.5 0.1 fusion.21
  94.5 0.1 fusion.20
  94.7 0.1 fusion.9
  94.8 0.1 mul.86.scaled_ref
  94.9 14.1 %integrate.1 = bf16[32,256,256]{2,1,0:T(8,128)(2,1)S(1)} custom-call(s32[16]{0:T(128)S(1)} %dynamic-slice_reduce_fusion.slots_ref, f32[1,1024]{1,0:T(1,128)S(1)} %mul.86.scaled_ref, bf16[16,512,1024]{2,1,0:T(8,128)(2,1)} %gather_tables.1.table_ref), custom_call_target="tpu_custom_call" | custom-call | tf_op jit(solution)/shard_map/integrate/pallas_call | solution.py:129
  109.0 0.0 copy-start
  109.0 2.0 %copy-done = bf16[32,256,256]{2,1,0:T(8,128)(2,1)} copy-done((bf16[32,256,256]{2,1,0:T(8,128)(2,1)}, bf16[32,256,256]{2,1,0:T(8,128)(2,1)S(1)}, u32[]{:S(2)}) %copy-start) | copy-done | bytes 4194328
  111.0 6.8 %all-to-all-start.1 = ((bf16[32,256,256]{2,1,0:T(8,128)(2,1)}), bf16[32,256,256]{2,1,0:T(8,128)(2,1)}, u32[]{:S(2)}, u32[]{:S(2)}) async-start(bf16[32,256,256]{2,1,0:T(8,128)(2,1)} %copy-done), calls=%async_computation.1 | async-start | bytes 8388608 | tf_op jit(solution)/shard_map/all_to_all | solution.py:238
  117.8 52.7 %all-to-all-done.1.parts_ref = bf16[32,256,256]{2,1,0:T(8,128)(2,1)} async-done(((bf16[32,256,256]{2,1,0:T(8,128)(2,1)}), bf16[32,256,256]{2,1,0:T(8,128)(2,1)}, u32[]{:S(2)}, u32[]{:S(2)}) %all-to-all-start.1) | async-done | bytes 4194336 | tf_op jit(solution)/shard_map/all_to_all | solution.py:238
  170.6 4.6 %add_up.1 = f32[3,256,256]{2,1,0:T(8,128)} custom-call(s32[32]{0:T(128)S(1)} %broadcast_select_fusion.targets_ref, bf16[32,256,256]{2,1,0:T(8,128)(2,1)} %all-to-all-done.1.parts_ref), custom_call_target="tpu_custom_call" | custom-call | tf_op jit(solution)/shard_map/add_up/pallas_call | solution.py:163
  (15 shorter events, 0.2 us)
Async XLA Ops:
  0.7 1.0 copy-start.2
  2.7 2.0 %copy-start.1 = (bf16[32,256,256]{2,1,0:T(8,128)(2,1)}, bf16[32,256,256]{2,1,0:T(8,128)(2,1)S(1)}, u32[]{:S(2)}) copy-start(bf16[32,256,256]{2,1,0:T(8,128)(2,1)S(1)} %pick_blocks.1) | copy-start | bytes 12582916
  4.6 7.6 %copy-start.3 = (s32[1,16,256]{2,1,0:T(8,128)S(1)}, s32[1,16,256]{2,1,0:T(8,128)}, u32[]{:S(2)}) copy-start(s32[1,16,256]{2,1,0:T(8,128)} %param.9) | copy-start | bytes 49156
  4.6 7.6 %copy-start.4 = (s32[1,16,256]{2,1,0:T(8,128)S(1)}, s32[1,16,256]{2,1,0:T(8,128)}, u32[]{:S(2)}) copy-start(s32[1,16,256]{2,1,0:T(8,128)} %param.8) | copy-start | bytes 49156
  4.6 60.4 %all-to-all-start = ((bf16[32,256,256]{2,1,0:T(8,128)(2,1)}), bf16[32,256,256]{2,1,0:T(8,128)(2,1)}, u32[]{:S(2)}, u32[]{:S(2)}) async-start(bf16[32,256,256]{2,1,0:T(8,128)(2,1)} %copy-done.1), calls=%async_computation | async-start | bytes 8388608 | tf_op jit(solution)/shard_map/all_to_all | solution.py:230
  79.4 4.5 %collective-permute-start = (f32[2,8,16]{2,1,0:T(8,128)S(1)}, f32[2,8,16]{2,1,0:T(8,128)S(1)}, u32[]{:S(2)}, u32[]{:S(2)}) collective-permute-start(f32[2,8,16]{2,1,0:T(8,128)S(1)} %slice.120), channel_id=1, source_target_pairs={{0,32},{32,64},{64,96},{96,128},{128,160},{160,192},{192,224},{224... | collective-permute-start | bytes 3080 | tf_op jit(solution)/shard_map/ppermute | solution.py:182
  82.7 4.9 %collective-permute-start.1 = (f32[2,8,16]{2,1,0:T(8,128)S(1)}, f32[2,8,16]{2,1,0:T(8,128)S(1)}, u32[]{:S(2)}, u32[]{:S(2)}) collective-permute-start(f32[2,8,16]{2,1,0:T(8,128)S(1)} %slice.122), channel_id=1, source_target_pairs={{32,0},{64,32},{96,64},{128,96},{160,128},{192,160},{224,192},{0,2... | collective-permute-start | bytes 3080 | tf_op jit(solution)/shard_map/ppermute | solution.py:183
  87.5 6.5 %collective-permute-start.2 = (f32[12,2,16]{2,1,0:T(2,128)S(1)}, f32[12,2,16]{2,1,0:T(2,128)S(1)}, u32[]{:S(2)}, u32[]{:S(2)}) collective-permute-start(f32[12,2,16]{2,1,0:T(2,128)S(1)} %get-tuple-element.26), channel_id=1, source_target_pairs={{0,1},{1,2},{2,3},{3,4},{4,5},{5,6},{6,7},{7,8},{8,9},{9,10},{10,1... | collective-permute-start | bytes 4616 | tf_op jit(solution)/shard_map/ppermute | solution.py:182
  87.6 6.5 %collective-permute-start.3 = (f32[12,2,16]{2,1,0:T(2,128)S(1)}, f32[12,2,16]{2,1,0:T(2,128)S(1)}, u32[]{:S(2)}, u32[]{:S(2)}) collective-permute-start(f32[12,2,16]{2,1,0:T(2,128)S(1)} %get-tuple-element.27), channel_id=1, source_target_pairs={{1,0},{2,1},{3,2},{4,3},{5,4},{6,5},{7,6},{8,7},{9,8},{10,9},{11,1... | collective-permute-start | bytes 4616 | tf_op jit(solution)/shard_map/ppermute | solution.py:183
  109.0 2.0 %copy-start = (bf16[32,256,256]{2,1,0:T(8,128)(2,1)}, bf16[32,256,256]{2,1,0:T(8,128)(2,1)S(1)}, u32[]{:S(2)}) copy-start(bf16[32,256,256]{2,1,0:T(8,128)(2,1)S(1)} %integrate.1) | copy-start | bytes 12582916
  111.0 59.6 %all-to-all-start.1 = ((bf16[32,256,256]{2,1,0:T(8,128)(2,1)}), bf16[32,256,256]{2,1,0:T(8,128)(2,1)}, u32[]{:S(2)}, u32[]{:S(2)}) async-start(bf16[32,256,256]{2,1,0:T(8,128)(2,1)} %copy-done), calls=%async_computation.1 | async-start | bytes 8388608 | tf_op jit(solution)/shard_map/all_to_all | solution.py:238

commit v2 on v1

v2 whole, which is shorter than its diff:
```python
import math

import jax
import jax.numpy as jnp
from jax import lax
from jax.experimental import pallas as pl
from jax.experimental.pallas import tpu as pltpu
from jax.sharding import PartitionSpec as P

GRAD_WEIGHT = 0.5
MIB = 1024 * 1024


RESIDENT = pl.BlockSpec(memory_space=pltpu.VMEM)
IN_HBM = pl.BlockSpec(memory_space=pltpu.HBM)
SCALARS = pl.BlockSpec(memory_space=pltpu.SMEM)


def params(mib):
    return pltpu.CompilerParams(vmem_limit_bytes=mib * MIB)


def pick_blocks(ids, store):
    count = ids.shape[0]

    def kernel(ids_ref, store_ref, out_ref, sems):
        copies = [
            pltpu.make_async_copy(store_ref.at[ids_ref[i]], out_ref.at[i], sems.at[i])
            for i in range(count)
        ]
        for copy in copies:
            copy.start()
        for copy in copies:
            copy.wait()

    return pl.pallas_call(
        kernel,
        out_shape=pltpu.HBM((count,) + store.shape[1:], store.dtype),
        in_specs=[SCALARS, RESIDENT],
        out_specs=IN_HBM,
        scratch_shapes=[pltpu.SemaphoreType.DMA((count,))],
        compiler_params=params(4),
        name="pick_blocks",
    )(ids, store)


def gather_tables(index, table):
    count, _, width = index.shape
    functions, points = table.shape
    lanes = 128

    def kernel(index_ref, table_ref, out_ref):
        pieces = []
        for start in range(0, width, lanes):
            row = index_ref[0, :, start : start + lanes]
            column = jnp.broadcast_to(row, (lanes, lanes)).T
            hot = [
                jnp.where(
                    column == lax.broadcasted_iota(jnp.int32, (lanes, lanes), 1) + f, 1.0, 0.0
                ).astype(jnp.bfloat16)
                for f in range(0, functions, lanes)
            ]
            pieces.append(jnp.concatenate(hot, axis=1))
        onehot = jnp.concatenate(pieces, axis=0)
        out_ref[0] = jnp.dot(
            onehot, table_ref[...], preferred_element_type=jnp.float32
        ).astype(jnp.bfloat16)

    return pl.pallas_call(
        kernel,
        out_shape=pltpu.HBM((count, width, points), jnp.bfloat16),
        grid=(count,),
        in_specs=[
            pl.BlockSpec((1, 1, width), lambda i: (i, 0, 0)),
            pl.BlockSpec((functions, points), lambda i: (0, 0)),
        ],
        out_specs=pl.BlockSpec((1, width, points), lambda i: (i, 0, 0)),
        compiler_params=params(24),
        cost_estimate=pl.CostEstimate(
            flops=2 * count * width * functions * points,
            bytes_accessed=2 * count * width * points,
            transcendentals=0,
        ),
        name="gather_tables",
    )(index, table)


def collocate(slots, blocks, tables):
    count, both, points = tables.shape
    width = both // 2

    def kernel(slots_ref, blocks_ref, tables_ref, out_ref, held, kept, sems):
        def fetch(j):
            return (
                pltpu.make_async_copy(blocks_ref.at[slots_ref[j]], held.at[j], sems.at[0, j]),
                pltpu.make_async_copy(tables_ref.at[j], kept.at[j], sems.at[1, j]),
            )

        for j in range(count):
            for copy in fetch(j):
                copy.start()
        out_ref[...] = jnp.zeros_like(out_ref)

        def body(j, carry):
            for copy in fetch(j):
                copy.wait()
            product = jnp.dot(held[j], kept[j, width:, :], preferred_element_type=jnp.float32)
            term = kept[j, :width, :].astype(jnp.float32) * product
            out_ref[...] += jnp.sum(term.reshape(width // 8, 8, points), axis=0)
            return carry

        lax.fori_loop(0, count, body, 0)

    return pl.pallas_call(
        kernel,
        out_shape=jax.ShapeDtypeStruct((8, points), jnp.float32),
        in_specs=[SCALARS, IN_HBM, IN_HBM],
        out_specs=RESIDENT,
        scratch_shapes=[
            pltpu.VMEM((count, width, width), jnp.bfloat16),
            pltpu.VMEM(tables.shape, tables.dtype),
            pltpu.SemaphoreType.DMA((2, count)),
        ],
        compiler_params=params(52),
        name="collocate",
    )(slots, blocks, tables)


def integrate(slots, scaled, tables, total):
    count, both, points = tables.shape
    width = both // 2

    def kernel(slots_ref, scaled_ref, tables_ref, out_ref, held, kept, sems):
        def fetch(j):
            return pltpu.make_async_copy(tables_ref.at[j], kept.at[j], sems.at[1, j])

        def leave(j):
            return pltpu.make_async_copy(held.at[j], out_ref.at[slots_ref[j]], sems.at[0, j])

        for j in range(count):
            fetch(j).start()

        def body(j, carry):
            fetch(j).wait()
            weighted = (kept[j, width:, :].astype(jnp.float32) * scaled_ref[...]).astype(
                jnp.bfloat16
            )
            held[j] = lax.dot_general(
                kept[j, :width, :],
                weighted,
                (((1,), (1,)), ((), ())),
                preferred_element_type=jnp.float32,
            ).astype(jnp.bfloat16)
            leave(j).start()
            return carry

        lax.fori_loop(0, count, body, 0)
        for j in range(count):
            leave(j).wait()

    return pl.pallas_call(
        kernel,
        out_shape=pltpu.HBM((total, width, width), jnp.bfloat16),
        in_specs=[SCALARS, RESIDENT, IN_HBM],
        out_specs=IN_HBM,
        scratch_shapes=[
            pltpu.VMEM((count, width, width), jnp.bfloat16),
            pltpu.VMEM(tables.shape, tables.dtype),
            pltpu.SemaphoreType.DMA((2, count)),
        ],
        compiler_params=params(52),
        name="integrate",
    )(slots, scaled, tables)


def add_up(targets, parts, own_count):
    count, rows, cols = parts.shape

    def kernel(targets_ref, parts_ref, out_ref, held, sems):
        def fetch(i):
            return pltpu.make_async_copy(parts_ref.at[i], held.at[i], sems.at[i])

        for i in range(count):

            @pl.when(targets_ref[i] >= 0)
            def _():
                fetch(i).start()

        out_ref[...] = jnp.zeros_like(out_ref)
        for i in range(count):
            target = targets_ref[i]

            @pl.when(target >= 0)
            def _():
                fetch(i).wait()
                out_ref[target] += held[i].astype(jnp.float32)

    return pl.pallas_call(
        kernel,
        out_shape=jax.ShapeDtypeStruct((own_count, rows, cols), jnp.float32),
        in_specs=[SCALARS, IN_HBM],
        out_specs=RESIDENT,
        scratch_shapes=[
            pltpu.VMEM((count, rows, cols), parts.dtype),
            pltpu.SemaphoreType.DMA((count,)),
        ],
        compiler_params=params(12),
        name="add_up",
    )(targets, parts)


def ends(block, dim, width):
    size = block.shape[dim]
    return (
        lax.slice_in_dim(block, 0, width, axis=dim),
        lax.slice_in_dim(block, size - width, size, axis=dim),
    )


def extended_ring(block, axis, dim, width):
    count = lax.axis_size(axis)
    low, high = ends(block, dim, width)
    forward = [(i, (i + 1) % count) for i in range(count)]
    backward = [(target, source) for source, target in forward]
    below = lax.ppermute(high, axis, forward)
    above = lax.ppermute(low, axis, backward)
    return jnp.concatenate([below, block, above], axis=dim)


def extended_pairs(block, axis, dim, width):
    count = lax.axis_size(axis)
    odd = lax.axis_index(axis) % 2 == 1
    low, high = ends(block, dim, width)
    within = [(i, i ^ 1) for i in range(count)]
    between = [(i, (i + 1) % count if i % 2 else (i - 1) % count) for i in range(count)]
    far = lax.ppermute(jnp.where(odd, high, low), axis, between)
    near = lax.ppermute(jnp.where(odd, low, high), axis, within)
    below = jnp.where(odd, near, far)
    above = jnp.where(odd, far, near)
    return jnp.concatenate([below, block, above], axis=dim)


def middle(field, dim, width=1):
    return lax.slice_in_dim(field, width, field.shape[dim] - width, axis=dim)


def slope(field, dim):
    size = field.shape[dim]
    return (
        lax.slice_in_dim(field, 2, size, axis=dim) - lax.slice_in_dim(field, 0, size - 2, axis=dim)
    ) * 0.5


def slope_z(field):
    return (jnp.roll(field, -1, 2) - jnp.roll(field, 1, 2)) * 0.5


def potential_of(padded):
    grad_x = middle(slope(padded, 0), 1)
    grad_y = middle(slope(padded, 1), 0)
    centre = middle(middle(padded, 0), 1)
    grad_z = slope_z(centre)
    sigma = grad_x * grad_x + grad_y * grad_y + grad_z * grad_z
    factor = 2.0 * GRAD_WEIGHT / (1.0 + sigma)
    flux_z = middle(middle(factor * grad_z, 0), 1)
    diverge = (
        middle(slope(factor * grad_x, 0), 1) + middle(slope(factor * grad_y, 1), 0) + slope_z(flux_z)
    )
    density = middle(middle(centre, 0), 1)
    return density / jnp.sqrt(1.0 + density * density) - diverge


def local(store, crossing, phi, rows_index, cols_index):
    position = lax.axis_index("brick")
    brick_count = lax.axis_size("brick")
    own_count, width = store.shape[0], store.shape[1]
    size_x, size_y, size_z, functions = phi.shape
    points = size_x * size_y * size_z
    owners = crossing // own_count
    chosen = owners == position
    filled = jnp.any(chosen, axis=-1)
    send_ids = jnp.sum(jnp.where(chosen, crossing % own_count, 0), axis=-1)
    slots = lax.dynamic_index_in_dim(owners, position, 0, keepdims=False)

    sending = pick_blocks(send_ids, store)
    blocks = lax.all_to_all(sending, "brick", split_axis=0, concat_axis=0, tiled=True)
    table = phi.reshape(points, functions).T
    index = jnp.concatenate([rows_index[0], cols_index[0]], axis=1)[:, None, :]
    tables = gather_tables(index, table)
    density = jnp.sum(collocate(slots, blocks, tables), axis=0).reshape(size_x, size_y, size_z)
    padded = extended_pairs(extended_ring(density, "grp", 0, 2), "brick", 1, 2)
    scaled = potential_of(padded).reshape(1, points) * (1.0 / math.sqrt(points))
    returning = integrate(slots, scaled, tables, brick_count)
    arrived = lax.all_to_all(returning, "brick", split_axis=0, concat_axis=0, tiled=True)
    targets = jnp.where(filled, send_ids, -1)
    return add_up(targets, arrived, own_count)


def solution(mesh):
    in_specs = (
        P(("grp", "brick"), None, None),
        P("grp", None),
        P("grp", "brick", None, None),
        P(("grp", "brick"), None, None),
        P(("grp", "brick"), None, None),
    )
    out_specs = P(("grp", "brick"), None, None)
    return jax.shard_map(local, mesh=mesh, in_specs=in_specs, out_specs=out_specs, check_vma=False)
```

time: 178 us -> 160 us (0.90)
  Pallas kernels: 56 us -> 44 us
  starting transfers between devices: 22.7 us -> 17.5 us
  local copies, waits for them, and re-layouts: 8.69 us -> 4.76 us
  waiting for transfers between devices: 86.5 us -> 89.5 us
    pallas_call x1, Pallas kernels: 14.2 us -> 7.54 us  [collocate(): pl.pallas_call(kernel, out_shape=jax.ShapeDtypeStruct((8, points), jnp.fl...]
    pallas_call x3, Pallas kernels: 37.2 us -> 33.2 us  [the longest x1 22.1 us: gather_tables(): pl.pallas_call(kernel, out_shape=pltpu.HBM((count, width, points), jnp.bf...]
    unnamed x12 -> x8, local copies, waits for them, and re-layouts: 4.94 us -> 1.01 us
    ppermute x4, waiting for transfers between devices: 6.25 us -> 9.43 us  [the longest x1 4.58 us: extended_pairs(): far = lax.ppermute(jnp.where(odd, high, low), axis, between)]
    ppermute x4, starting transfers between devices: 8.3 us -> 5.2 us  [the longest x1 3.15 us: extended_ring(): below = lax.ppermute(high, axis, forward)]
    all_to_all x1, starting transfers between devices: 6.82 us -> 4.87 us  [local(): lax.all_to_all(returning, 'brick', split_axis=0, concat_axis=0, tiled=True)]
  transfers between devices with their start and end apart: 6 -> 6, of which waited for: 5 -> 5; matrix products, arithmetic and copies ran while one was open for 2% -> 2% of each run, Pallas kernels for 13% -> 14%
where the time goes in v2:
time: 160 us; the launch traced here: 157 us
  waiting for transfers between devices  89.5 us (56%)
  Pallas kernels  44 us (28%)
  starting transfers between devices  17.5 us (11%)
  local copies, waits for them, and re-layouts  4.76 us (3%)
    all_to_all x1, waiting for transfers between devices, local(): lax.all_to_all(returning, 'brick', split_axis=0, concat_axis=0, tiled=True)  52.6 us
    all_to_all x1, waiting for transfers between devices, local(): lax.all_to_all(sending, 'brick', split_axis=0, concat_axis=0, tiled=True)  27.5 us
    pallas_call x1, Pallas kernels, gather_tables(): pl.pallas_call(kernel, out_shape=pltpu.HBM((count, width, points), jnp.bf...  22.1 us
    pallas_call x1, Pallas kernels, integrate(): pl.pallas_call(kernel, out_shape=pltpu.HBM((total, width, width), jnp.bfl...  8.29 us
    pallas_call x1, Pallas kernels, collocate(): pl.pallas_call(kernel, out_shape=jax.ShapeDtypeStruct((8, points), jnp.fl...  7.54 us
    all_to_all x1, starting transfers between devices, local(): lax.all_to_all(sending, 'brick', split_axis=0, concat_axis=0, tiled=True)  7.46 us
    all_to_all x1, starting transfers between devices, local(): lax.all_to_all(returning, 'brick', split_axis=0, concat_axis=0, tiled=True)  4.87 us
    ppermute x1, waiting for transfers between devices, extended_pairs(): far = lax.ppermute(jnp.where(odd, high, low), axis, between)  4.58 us
  transfers between devices with their start and end apart: 6, of which 5 were waited for; matrix products, arithmetic and copies ran while one was open for 2% of the time, Pallas kernels for 14%

profile of v2, /device:TPU:96, one launch (start us, length us, event | category | flops | bytes accessed | tf_op | source)
XLA Modules:
  0.0 157.1 jit_solution(4192654892029959851)
XLA Ops:
  0.0 0.7 fusion.14
  0.7 0.0 copy-start
  0.7 1.0 copy-done
  1.7 2.8 %pick_blocks.1 = bf16[32,256,256]{2,1,0:T(8,128)(2,1)} custom-call(s32[32]{0:T(128)S(1)} %get-tuple-element.7.ids_ref, bf16[3,256,256]{2,1,0:T(8,128)(2,1)S(1)} %copy-done), custom_call_target="tpu_custom_call" | custom-call | tf_op jit(solution)/shard_map/pick_blocks/pallas_call | solution.py:36
  4.5 0.0 copy-start.1
  4.5 0.0 copy-start.2
  4.5 7.5 %all-to-all-start = ((bf16[32,256,256]{2,1,0:T(8,128)(2,1)}), bf16[32,256,256]{2,1,0:T(8,128)(2,1)}, u32[]{:S(2)}, u32[]{:S(2)}) async-start(bf16[32,256,256]{2,1,0:T(8,128)(2,1)} %pick_blocks.1), calls=%async_computation | async-start | bytes 8388608 | tf_op jit(solution)/shard_map/all_to_all | solution.py:286
  12.0 0.0 copy-done.1
  12.0 0.0 copy-done.2
  12.1 2.9 %copy.7 = bf16[1024,1024]{0,1:T(8,128)(2,1)S(1)} copy(bf16[1024,1024]{1,0:T(8,128)(2,1)} %bitcast.9) | data formatting | bytes 4194304 | tf_op jit(solution)/shard_map/reshape | solution.py:287
  14.9 0.2 dynamic-slice_reduce_fusion.slots_ref
  15.1 22.1 %gather_tables.1.tables_ref = bf16[16,512,1024]{2,1,0:T(8,128)(2,1)} custom-call(s32[16,1,512]{2,1,0:T(1,128)S(1)} %broadcast_in_dim.10.index_ref, bf16[1024,1024]{1,0:T(8,128)(2,1)S(1)} %bitcast.8), custom_call_target="tpu_custom_call" | custom-call | flops 17179869184 | bytes 16777216 | tf_op jit(solution)/shard_map/gather_tables/pallas_call | solution.py:69
  37.3 27.5 %all-to-all-done.blocks_ref = bf16[32,256,256]{2,1,0:T(8,128)(2,1)} async-done(((bf16[32,256,256]{2,1,0:T(8,128)(2,1)}), bf16[32,256,256]{2,1,0:T(8,128)(2,1)}, u32[]{:S(2)}, u32[]{:S(2)}) %all-to-all-start) | async-done | bytes 4194336 | tf_op jit(solution)/shard_map/all_to_all | solution.py:286
  64.8 7.5 %collocate.1 = f32[8,1024]{1,0:T(8,128)S(1)} custom-call(s32[16]{0:T(128)S(1)} %dynamic-slice_reduce_fusion.slots_ref, bf16[32,256,256]{2,1,0:T(8,128)(2,1)} %all-to-all-done.blocks_ref, bf16[16,512,1024]{2,1,0:T(8,128)(2,1)} %gather_tables.1.tables_ref), custom_call_target="tpu_custom_call" | custom-call | tf_op jit(solution)/shard_map/collocate/pallas_call | solution.py:114
  72.4 0.1 slice.120
  72.5 3.1 %collective-permute-start = (f32[2,8,16]{2,1,0:T(8,128)S(1)}, f32[2,8,16]{2,1,0:T(8,128)S(1)}, u32[]{:S(2)}, u32[]{:S(2)}) collective-permute-start(f32[2,8,16]{2,1,0:T(8,128)S(1)} %slice.120), channel_id=1, source_target_pairs={{0,32},{32,64},{64,96},{96,128},{128,160},{160,192},{192,224},{224... | collective-permute-start | bytes 3080 | tf_op jit(solution)/shard_map/ppermute | solution.py:225
  75.6 0.1 reshape.40
  75.7 0.1 slice.122
  75.7 0.0 collective-permute-start.1
  75.8 1.2 collective-permute-done
  77.0 3.7 %collective-permute-done.1 = f32[2,8,16]{2,1,0:T(8,128)S(1)} collective-permute-done((f32[2,8,16]{2,1,0:T(8,128)S(1)}, f32[2,8,16]{2,1,0:T(8,128)S(1)}, u32[]{:S(2)}, u32[]{:S(2)}) %collective-permute-start.1) | collective-permute-done | bytes 1056 | tf_op jit(solution)/shard_map/ppermute | solution.py:226
  80.6 0.1 collective-permute-start.2
  80.7 1.9 %collective-permute-start.3 = (f32[12,2,16]{2,1,0:T(2,128)S(1)}, f32[12,2,16]{2,1,0:T(2,128)S(1)}, u32[]{:S(2)}, u32[]{:S(2)}) collective-permute-start(f32[12,2,16]{2,1,0:T(2,128)S(1)} %get-tuple-element.27), channel_id=1, source_target_pairs={{0,31},{1,2},{2,1},{3,4},{4,3},{5,6},{6,5},{7,8},{8,7},{9,10},{10,... | collective-permute-start | bytes 4616 | tf_op jit(solution)/shard_map/ppermute | solution.py:236
  82.7 0.0 collective-permute-done.2
  82.7 4.6 %collective-permute-done.3 = f32[12,2,16]{2,1,0:T(2,128)S(1)} collective-permute-done((f32[12,2,16]{2,1,0:T(2,128)S(1)}, f32[12,2,16]{2,1,0:T(2,128)S(1)}, u32[]{:S(2)}, u32[]{:S(2)}) %collective-permute-start.3) | collective-permute-done | bytes 1568 | tf_op jit(solution)/shard_map/ppermute | solution.py:236
  87.3 0.1 fusion.18
  87.4 0.1 fusion.19
  87.5 0.1 fusion.16
  87.6 0.1 fusion.21
  87.7 0.1 fusion.20
  87.9 0.1 fusion.9
  88.0 0.1 mul.86.scaled_ref
  88.1 8.3 %integrate.1 = bf16[32,256,256]{2,1,0:T(8,128)(2,1)} custom-call(s32[16]{0:T(128)S(1)} %dynamic-slice_reduce_fusion.slots_ref, f32[1,1024]{1,0:T(1,128)S(1)} %mul.86.scaled_ref, bf16[16,512,1024]{2,1,0:T(8,128)(2,1)} %gather_tables.1.tables_ref), custom_call_target="tpu_custom_call" | custom-call | tf_op jit(solution)/shard_map/integrate/pallas_call | solution.py:161
  96.4 4.9 %all-to-all-start.1 = ((bf16[32,256,256]{2,1,0:T(8,128)(2,1)}), bf16[32,256,256]{2,1,0:T(8,128)(2,1)}, u32[]{:S(2)}, u32[]{:S(2)}) async-start(bf16[32,256,256]{2,1,0:T(8,128)(2,1)} %integrate.1), calls=%async_computation.1 | async-start | bytes 8388608 | tf_op jit(solution)/shard_map/all_to_all | solution.py:294
  101.3 52.6 %all-to-all-done.1.parts_ref = bf16[32,256,256]{2,1,0:T(8,128)(2,1)} async-done(((bf16[32,256,256]{2,1,0:T(8,128)(2,1)}), bf16[32,256,256]{2,1,0:T(8,128)(2,1)}, u32[]{:S(2)}, u32[]{:S(2)}) %all-to-all-start.1) | async-done | bytes 4194336 | tf_op jit(solution)/shard_map/all_to_all | solution.py:294
  153.9 3.3 %add_up.1 = f32[3,256,256]{2,1,0:T(8,128)} custom-call(s32[32]{0:T(128)S(1)} %broadcast_select_fusion.4.targets_ref, bf16[32,256,256]{2,1,0:T(8,128)(2,1)} %all-to-all-done.1.parts_ref), custom_call_target="tpu_custom_call" | custom-call | tf_op jit(solution)/shard_map/add_up/pallas_call | solution.py:198
  (16 shorter events, 0.2 us)
Async XLA Ops:
  0.7 1.0 copy-start
  4.5 7.5 %copy-start.1 = (s32[1,16,256]{2,1,0:T(8,128)S(1)}, s32[1,16,256]{2,1,0:T(8,128)}, u32[]{:S(2)}) copy-start(s32[1,16,256]{2,1,0:T(8,128)} %param.9) | copy-start | bytes 49156
  4.5 7.5 %copy-start.2 = (s32[1,16,256]{2,1,0:T(8,128)S(1)}, s32[1,16,256]{2,1,0:T(8,128)}, u32[]{:S(2)}) copy-start(s32[1,16,256]{2,1,0:T(8,128)} %param.8) | copy-start | bytes 49156
  4.5 60.2 %all-to-all-start = ((bf16[32,256,256]{2,1,0:T(8,128)(2,1)}), bf16[32,256,256]{2,1,0:T(8,128)(2,1)}, u32[]{:S(2)}, u32[]{:S(2)}) async-start(bf16[32,256,256]{2,1,0:T(8,128)(2,1)} %pick_blocks.1), calls=%async_computation | async-start | bytes 8388608 | tf_op jit(solution)/shard_map/all_to_all | solution.py:286
  72.5 4.5 %collective-permute-start = (f32[2,8,16]{2,1,0:T(8,128)S(1)}, f32[2,8,16]{2,1,0:T(8,128)S(1)}, u32[]{:S(2)}, u32[]{:S(2)}) collective-permute-start(f32[2,8,16]{2,1,0:T(8,128)S(1)} %slice.120), channel_id=1, source_target_pairs={{0,32},{32,64},{64,96},{96,128},{128,160},{160,192},{192,224},{224... | collective-permute-start | bytes 3080 | tf_op jit(solution)/shard_map/ppermute | solution.py:225
  75.7 4.9 %collective-permute-start.1 = (f32[2,8,16]{2,1,0:T(8,128)S(1)}, f32[2,8,16]{2,1,0:T(8,128)S(1)}, u32[]{:S(2)}, u32[]{:S(2)}) collective-permute-start(f32[2,8,16]{2,1,0:T(8,128)S(1)} %slice.122), channel_id=1, source_target_pairs={{32,0},{64,32},{96,64},{128,96},{160,128},{192,160},{224,192},{0,2... | collective-permute-start | bytes 3080 | tf_op jit(solution)/shard_map/ppermute | solution.py:226
  80.6 2.0 %collective-permute-start.2 = (f32[12,2,16]{2,1,0:T(2,128)S(1)}, f32[12,2,16]{2,1,0:T(2,128)S(1)}, u32[]{:S(2)}, u32[]{:S(2)}) collective-permute-start(f32[12,2,16]{2,1,0:T(2,128)S(1)} %get-tuple-element.26), channel_id=1, source_target_pairs={{0,1},{1,0},{2,3},{3,2},{4,5},{5,4},{6,7},{7,6},{8,9},{9,8},{10,11... | collective-permute-start | bytes 4616 | tf_op jit(solution)/shard_map/ppermute | solution.py:237
  80.7 6.5 %collective-permute-start.3 = (f32[12,2,16]{2,1,0:T(2,128)S(1)}, f32[12,2,16]{2,1,0:T(2,128)S(1)}, u32[]{:S(2)}, u32[]{:S(2)}) collective-permute-start(f32[12,2,16]{2,1,0:T(2,128)S(1)} %get-tuple-element.27), channel_id=1, source_target_pairs={{0,31},{1,2},{2,1},{3,4},{4,3},{5,6},{6,5},{7,8},{8,7},{9,10},{10,... | collective-permute-start | bytes 4616 | tf_op jit(solution)/shard_map/ppermute | solution.py:236
  96.4 57.5 %all-to-all-start.1 = ((bf16[32,256,256]{2,1,0:T(8,128)(2,1)}), bf16[32,256,256]{2,1,0:T(8,128)(2,1)}, u32[]{:S(2)}, u32[]{:S(2)}) async-start(bf16[32,256,256]{2,1,0:T(8,128)(2,1)} %integrate.1), calls=%async_computation.1 | async-start | bytes 8388608 | tf_op jit(solution)/shard_map/all_to_all | solution.py:294

commit v3 on v2

--- a/solution.py
+++ b/solution.py
@@ -5,9 +5,11 @@
 from jax import lax
 from jax.experimental import pallas as pl
 from jax.experimental.pallas import tpu as pltpu
+from jax.sharding import Mesh
 from jax.sharding import PartitionSpec as P
 
 GRAD_WEIGHT = 0.5
+BRICK = ("x", "y", "core")
 MIB = 1024 * 1024
 
 
@@ -126,16 +128,28 @@
     )(slots, blocks, tables)
 
 
-def integrate(slots, scaled, tables, total):
+def integrate(places, scaled, tables, total, half):
     count, both, points = tables.shape
     width = both // 2
-
-    def kernel(slots_ref, scaled_ref, tables_ref, out_ref, held, kept, sems):
+    parts, inner = total
+
+    def kernel(places_ref, scaled_ref, tables_ref, first_ref, *rest):
+        others, (held, kept, sems) = rest[:parts], rest[parts:]
+
         def fetch(j):
-            return pltpu.make_async_copy(tables_ref.at[j], kept.at[j], sems.at[1, j])
-
-        def leave(j):
-            return pltpu.make_async_copy(held.at[j], out_ref.at[slots_ref[j]], sems.at[0, j])
+            return pltpu.make_async_copy(tables_ref.at[j], kept.at[j], sems.at[0, j])
+
+        def leave_first(j):
+            return pltpu.make_async_copy(
+                held.at[j, pl.ds(0, half)], first_ref.at[places_ref[0, j]], sems.at[1, j]
+            )
+
+        def leave_other(j, part):
+            return pltpu.make_async_copy(
+                held.at[j, pl.ds(half, width - half)],
+                others[part].at[places_ref[2, j]],
+                sems.at[2, j],
+            )
 
         for j in range(count):
             fetch(j).start()
@@ -151,34 +165,49 @@
                 (((1,), (1,)), ((), ())),
                 preferred_element_type=jnp.float32,
             ).astype(jnp.bfloat16)
-            leave(j).start()
+            leave_first(j).start()
+            for part in range(parts):
+
+                @pl.when(places_ref[1, j] == part)
+                def _():
+                    leave_other(j, part).start()
+
             return carry
 
         lax.fori_loop(0, count, body, 0)
         for j in range(count):
-            leave(j).wait()
-
-    return pl.pallas_call(
-        kernel,
-        out_shape=pltpu.HBM((total, width, width), jnp.bfloat16),
+            leave_first(j).wait()
+            leave_other(j, 0).wait()
+
+    return pl.pallas_call(
+        kernel,
+        out_shape=[pltpu.HBM((parts * inner, half, width), jnp.bfloat16)]
+        + [pltpu.HBM((inner, width - half, width), jnp.bfloat16)] * parts,
         in_specs=[SCALARS, RESIDENT, IN_HBM],
-        out_specs=IN_HBM,
+        out_specs=[IN_HBM] * (1 + parts),
         scratch_shapes=[
             pltpu.VMEM((count, width, width), jnp.bfloat16),
             pltpu.VMEM(tables.shape, tables.dtype),
-            pltpu.SemaphoreType.DMA((2, count)),
+            pltpu.SemaphoreType.DMA((3, count)),
         ],
         compiler_params=params(52),
         name="integrate",
-    )(slots, scaled, tables)
-
-
-def add_up(targets, parts, own_count):
-    count, rows, cols = parts.shape
-
-    def kernel(targets_ref, parts_ref, out_ref, held, sems):
+    )(places, scaled, tables)
+
+
+def add_up(targets, parts, own_count, inner):
+    rows, cols = parts[0].shape[1:]
+    count = sum(part.shape[0] for part in parts)
+
+    def kernel(targets_ref, *refs):
+        parts_refs = refs[: len(parts)]
+        own_ref, *outs = refs[len(parts) : len(parts) + inner]
+        held, total, sems = refs[len(parts) + inner :]
+        where = [(ref, i) for ref in parts_refs for i in range(ref.shape[0])]
+
         def fetch(i):
-            return pltpu.make_async_copy(parts_ref.at[i], held.at[i], sems.at[i])
+            ref, place = where[i]
+            return pltpu.make_async_copy(ref.at[place], held.at[i], sems.at[i])
 
         for i in range(count):
 
@@ -186,27 +215,60 @@
             def _():
                 fetch(i).start()
 
-        out_ref[...] = jnp.zeros_like(out_ref)
+        total[...] = jnp.zeros_like(total)
         for i in range(count):
             target = targets_ref[i]
 
             @pl.when(target >= 0)
             def _():
                 fetch(i).wait()
-                out_ref[target] += held[i].astype(jnp.float32)
-
-    return pl.pallas_call(
-        kernel,
-        out_shape=jax.ShapeDtypeStruct((own_count, rows, cols), jnp.float32),
-        in_specs=[SCALARS, IN_HBM],
-        out_specs=RESIDENT,
+                total[(i % inner) * own_count + target] += held[i].astype(jnp.float32)
+
+        own_ref[...] = total[:own_count]
+        for d, out in enumerate(outs):
+            out[...] = total[(d + 1) * own_count : (d + 2) * own_count].astype(jnp.bfloat16)
+
+    return pl.pallas_call(
+        kernel,
+        out_shape=[jax.ShapeDtypeStruct((own_count, rows, cols), jnp.float32)]
+        + [jax.ShapeDtypeStruct((own_count, rows, cols), jnp.bfloat16)] * (inner - 1),
+        in_specs=[SCALARS] + [IN_HBM] * len(parts),
+        out_specs=[RESIDENT] * inner,
         scratch_shapes=[
-            pltpu.VMEM((count, rows, cols), parts.dtype),
+            pltpu.VMEM((count, rows, cols), jnp.bfloat16),
+            pltpu.VMEM((inner * own_count, rows, cols), jnp.float32),
             pltpu.SemaphoreType.DMA((count,)),
         ],
         compiler_params=params(12),
         name="add_up",
-    )(targets, parts)
+    )(targets, *parts)
+
+
+def join(first, other):
+    own_count, half, cols = first[0].shape
+    rest = other[0].shape[1]
+
+    def kernel(*refs):
+        out_ref = refs[-1]
+
+        def total(some):
+            value = some[0][...]
+            for ref in some[1:]:
+                value = value + ref[...].astype(jnp.float32)
+            return value
+
+        out_ref[:, :half, :] = total(refs[: len(first)])
+        out_ref[:, half:, :] = total(refs[len(first) : -1])
+
+    return pl.pallas_call(
+        kernel,
+        out_shape=jax.ShapeDtypeStruct((own_count, half + rest, cols), jnp.float32),
+        grid=(own_count,),
+        in_specs=[pl.BlockSpec((1,) + a.shape[1:], lambda i: (i, 0, 0)) for a in first + other],
+        out_specs=pl.BlockSpec((1, half + rest, cols), lambda i: (i, 0, 0)),
+        compiler_params=params(8),
+        name="join",
+    )(*first, *other)
 
 
 def ends(block, dim, width):
@@ -228,7 +290,7 @@
 
 
 def extended_pairs(block, axis, dim, width):
-    count = lax.axis_size(axis)
+    count = size_of(axis)
     odd = lax.axis_index(axis) % 2 == 1
     low, high = ends(block, dim, width)
     within = [(i, i ^ 1) for i in range(count)]
@@ -270,39 +332,91 @@
     return density / jnp.sqrt(1.0 + density * density) - diverge
 
 
+def size_of(axes):
+    return math.prod(lax.axis_size(axis) for axis in axes)
+
+
+def moved(value, dx=0, dy=0, dc=0):
+    sizes = tuple(lax.axis_size(axis) for axis in BRICK)
+    pairs = []
+    for source in range(math.prod(sizes)):
+        x, rest = divmod(source, sizes[1] * sizes[2])
+        y, c = divmod(rest, sizes[2])
+        x, y, c = (x + dx) % sizes[0], (y + dy) % sizes[1], (c + dc) % sizes[2]
+        pairs.append((source, (x * sizes[1] + y) * sizes[2] + c))
+    return lax.ppermute(value, BRICK, pairs)
+
+
+def find(owners, ids, bricks, wanted):
+    hit = owners[bricks][:, None, :] == wanted[None, :, None]
+    number = jnp.sum(jnp.where(hit, ids[bricks][:, None, :], 0), axis=-1)
+    return jnp.where(jnp.any(hit, axis=-1), number, -1).reshape(-1).astype(jnp.int32)
+
+
 def local(store, crossing, phi, rows_index, cols_index):
-    position = lax.axis_index("brick")
-    brick_count = lax.axis_size("brick")
+    nx, ny, nc = (lax.axis_size(axis) for axis in BRICK)
+    x, y, c = (lax.axis_index(axis) for axis in BRICK)
+    position = (x * ny + y) * nc + c
     own_count, width = store.shape[0], store.shape[1]
+    half = width // 2
     size_x, size_y, size_z, functions = phi.shape
     points = size_x * size_y * size_z
     owners = crossing // own_count
+    ids = crossing % own_count
     chosen = owners == position
-    filled = jnp.any(chosen, axis=-1)
-    send_ids = jnp.sum(jnp.where(chosen, crossing % own_count, 0), axis=-1)
+    send_ids = jnp.sum(jnp.where(chosen, ids, 0), axis=-1)
     slots = lax.dynamic_index_in_dim(owners, position, 0, keepdims=False)
 
     sending = pick_blocks(send_ids, store)
-    blocks = lax.all_to_all(sending, "brick", split_axis=0, concat_axis=0, tiled=True)
+    blocks = lax.all_to_all(sending, BRICK, split_axis=0, concat_axis=0, tiled=True)
     table = phi.reshape(points, functions).T
     index = jnp.concatenate([rows_index[0], cols_index[0]], axis=1)[:, None, :]
     tables = gather_tables(index, table)
     density = jnp.sum(collocate(slots, blocks, tables), axis=0).reshape(size_x, size_y, size_z)
-    padded = extended_pairs(extended_ring(density, "grp", 0, 2), "brick", 1, 2)
+    padded = extended_pairs(extended_ring(density, "grp", 0, 2), BRICK, 1, 2)
     scaled = potential_of(padded).reshape(1, points) * (1.0 / math.sqrt(points))
-    returning = integrate(slots, scaled, tables, brick_count)
-    arrived = lax.all_to_all(returning, "brick", split_axis=0, concat_axis=0, tiled=True)
-    targets = jnp.where(filled, send_ids, -1)
-    return add_up(targets, arrived, own_count)
+
+    to_x, rest = slots // (ny * nc), slots % (ny * nc)
+    to_y, to_c = rest // nc, rest % nc
+    ahead_x, ahead_y, ahead_c = (to_x - x) % nx, (to_y - y) % ny, (to_c - c) % nc
+    places = jnp.stack(
+        [(to_y * nc + to_c) * nx + ahead_x, ahead_x * nc + ahead_c, ahead_y]
+    ).astype(jnp.int32)
+    first, *others = integrate(places, scaled, tables, (nx * nc, ny), half)
+    first = lax.all_to_all(first, ("y", "core"), split_axis=0, concat_axis=0, tiled=True)
+    others = [
+        moved(piece, dx=i // nc, dc=i % nc) if i else piece for i, piece in enumerate(others)
+    ]
+    step_x, step_y, step_c = jnp.arange(nx), jnp.arange(ny), jnp.arange(nc)
+    from_first = ((x * ny + step_y[:, None]) * nc + step_c[None, :]).reshape(-1)
+    for_first = (((x + step_x) % nx) * ny + y) * nc + c
+    from_other = (
+        (((x - step_x) % nx) * ny + y)[:, None] * nc + ((c - step_c) % nc)[None, :]
+    ).reshape(-1)
+    for_other = (x * ny + (y + step_y) % ny) * nc + c
+    other_own, *other_send = add_up(
+        find(owners, ids, from_other, for_other), others, own_count, ny
+    )
+    other_all = [other_own] + [moved(piece, dy=1 + d) for d, piece in enumerate(other_send)]
+    first_own, *first_send = add_up(
+        find(owners, ids, from_first, for_first), [first], own_count, nx
+    )
+    first_all = [first_own] + [moved(piece, dx=1 + d) for d, piece in enumerate(first_send)]
+    return join(first_all, other_all)
 
 
 def solution(mesh):
+    groups, bricks = mesh.shape["grp"], mesh.shape["brick"]
+    side = math.isqrt(bricks // 2)
+    split = Mesh(mesh.devices.reshape(groups, side, bricks // (2 * side), 2), ("grp",) + BRICK)
+    whole = ("grp",) + BRICK
     in_specs = (
-        P(("grp", "brick"), None, None),
+        P(whole, None, None),
         P("grp", None),
-        P("grp", "brick", None, None),
-        P(("grp", "brick"), None, None),
-        P(("grp", "brick"), None, None),
-    )
-    out_specs = P(("grp", "brick"), None, None)
-    return jax.shard_map(local, mesh=mesh, in_specs=in_specs, out_specs=out_specs, check_vma=False)
+        P("grp", BRICK, None, None),
+        P(whole, None, None),
+        P(whole, None, None),
+    )
+    return jax.shard_map(
+        local, mesh=split, in_specs=in_specs, out_specs=P(whole, None, None), check_vma=False
+    )

time: 160 us -> 160 us (level); the launches traced: 157 us -> 160 us
  waiting for transfers between devices: 89.5 us -> 63.2 us
  starting transfers between devices: 17.5 us -> 34.4 us
  local copies, waits for them, and re-layouts: 4.76 us -> 11.1 us
  Pallas kernels: 44 us -> 49 us
    all_to_all x2, waiting for transfers between devices: 80.1 us -> 27.7 us  [the longest x1 27.7 us: local(): lax.all_to_all(sending, BRICK, split_axis=0, concat_axis=0, tiled=True)]
    ppermute x0 -> x13, waiting for transfers between devices: none -> 26.1 us  [moved(): return lax.ppermute(value, BRICK, pairs)]
    ppermute x0 -> x13, starting transfers between devices: none -> 18 us  [moved(): return lax.ppermute(value, BRICK, pairs)]
    pallas_call x2 -> x4, Pallas kernels: 11.5 us -> 16.6 us  [the longest x1 8.51 us: integrate(): pl.pallas_call(kernel, out_shape=[pltpu.HBM((parts * inner, half, width),...]
    unnamed x8 -> x19, local copies, waits for them, and re-layouts: 1.01 us -> 4.79 us
    gather x0 -> x4, local copies, waits for them, and re-layouts: none -> 2.22 us  [the longest x2 1.11 us: find(): number = jnp.sum(jnp.where(hit, ids[bricks][:, None, :], 0), axis=-1)]
  transfers between devices with their start and end apart: 6 -> 19, of which waited for: 5 -> 9; matrix products, arithmetic and copies ran while one was open for 2% -> 4% of each run, Pallas kernels for 14% -> 18%
where the time goes in v3:
time: 160 us
  waiting for transfers between devices  63.2 us (40%)
  Pallas kernels  49 us (31%)
  starting transfers between devices  34.4 us (22%)
  local copies, waits for them, and re-layouts  11.1 us (7%)
  other arithmetic  1.6 us (1%)
    all_to_all x1, waiting for transfers between devices, local(): lax.all_to_all(sending, BRICK, split_axis=0, concat_axis=0, tiled=True)  27.7 us
    ppermute x13, waiting for transfers between devices, moved(): return lax.ppermute(value, BRICK, pairs)  26.1 us
    pallas_call x1, Pallas kernels, gather_tables(): pl.pallas_call(kernel, out_shape=pltpu.HBM((count, width, points), jnp.bf...  22 us
    ppermute x13, starting transfers between devices, moved(): return lax.ppermute(value, BRICK, pairs)  18 us
    pallas_call x1, Pallas kernels, integrate(): pl.pallas_call(kernel, out_shape=[pltpu.HBM((parts * inner, half, width),...  8.51 us
    pallas_call x1, Pallas kernels, collocate(): pl.pallas_call(kernel, out_shape=jax.ShapeDtypeStruct((8, points), jnp.fl...  7.54 us
    all_to_all x1, starting transfers between devices, local(): lax.all_to_all(sending, BRICK, split_axis=0, concat_axis=0, tiled=True)  7.46 us
    pallas_call x2, Pallas kernels, add_up(): pl.pallas_call(kernel, out_shape=[jax.ShapeDtypeStruct((own_count, rows,...  6.6 us
  transfers between devices with their start and end apart: 19, of which 9 were waited for; matrix products, arithmetic and copies ran while one was open for 4% of the time, Pallas kernels for 18%

profile of v3, /device:TPU:96, one launch (start us, length us, event | category | flops | bytes accessed | tf_op | source)
XLA Modules:
  0.0 159.7 jit_solution(14394289796068724971)
XLA Ops:
  0.0 0.8 copy.14
  0.8 0.1 select_reduce_fusion
  0.9 1.0 copy-done
  1.9 2.8 %pick_blocks.1 = bf16[32,256,256]{2,1,0:T(8,128)(2,1)} custom-call(s32[32]{0:T(128)S(1)} %get-tuple-element.65.ids_ref, bf16[3,256,256]{2,1,0:T(8,128)(2,1)S(1)} %copy-done), custom_call_target="tpu_custom_call" | custom-call | tf_op jit(solution)/shard_map/pick_blocks/pallas_call | solution.py:38
  4.8 7.5 %all-to-all-start = ((bf16[32,256,256]{2,1,0:T(8,128)(2,1)}), bf16[32,256,256]{2,1,0:T(8,128)(2,1)}, u32[]{:S(2)}, u32[]{:S(2)}) async-start(bf16[32,256,256]{2,1,0:T(8,128)(2,1)} %pick_blocks.1), calls=%async_computation | async-start | bytes 8388608 | tf_op jit(solution)/shard_map/all_to_all | solution.py:371
  12.3 2.9 %copy.18 = bf16[1024,1024]{0,1:T(8,128)(2,1)S(1)} copy(bf16[1024,1024]{1,0:T(8,128)(2,1)} %bitcast.15) | data formatting | bytes 4194304 | tf_op jit(solution)/shard_map/reshape | solution.py:372
  15.3 0.1 broadcast_add_fusion
  15.4 22.0 %gather_tables.1.tables_ref = bf16[16,512,1024]{2,1,0:T(8,128)(2,1)} custom-call(s32[16,1,512]{2,1,0:T(1,128)S(1)} %broadcast_in_dim.45.index_ref, bf16[1024,1024]{1,0:T(8,128)(2,1)S(1)} %bitcast.14), custom_call_target="tpu_custom_call" | custom-call | flops 17179869184 | bytes 16777216 | tf_op jit(solution)/shard_map/gather_tables/pallas_call | solution.py:71
  37.4 27.7 %all-to-all-done.blocks_ref = bf16[32,256,256]{2,1,0:T(8,128)(2,1)} async-done(((bf16[32,256,256]{2,1,0:T(8,128)(2,1)}), bf16[32,256,256]{2,1,0:T(8,128)(2,1)}, u32[]{:S(2)}, u32[]{:S(2)}) %all-to-all-start) | async-done | bytes 4194336 | tf_op jit(solution)/shard_map/all_to_all | solution.py:371
  65.0 7.5 %collocate.1 = f32[8,1024]{1,0:T(8,128)S(1)} custom-call(s32[16]{0:T(128)S(1)} %get-tuple-element.68.slots_ref, bf16[32,256,256]{2,1,0:T(8,128)(2,1)} %all-to-all-done.blocks_ref, bf16[16,512,1024]{2,1,0:T(8,128)(2,1)} %gather_tables.1.tables_ref), custom_call_target="tpu_custom_call" | custom-call | tf_op jit(solution)/shard_map/collocate/pallas_call | solution.py:116
  72.6 0.1 slice.120
  72.7 3.1 %collective-permute-start = (f32[2,8,16]{2,1,0:T(8,128)S(1)}, f32[2,8,16]{2,1,0:T(8,128)S(1)}, u32[]{:S(2)}, u32[]{:S(2)}) collective-permute-start(f32[2,8,16]{2,1,0:T(8,128)S(1)} %slice.120), channel_id=1, source_target_pairs={{0,32},{32,64},{64,96},{96,128},{128,160},{160,192},{192,224},{224... | collective-permute-start | bytes 3080 | tf_op jit(solution)/shard_map/ppermute | solution.py:287
  75.9 0.1 slice.122
  76.0 1.2 collective-permute-done
  77.2 3.7 %collective-permute-done.1 = f32[2,8,16]{2,1,0:T(8,128)S(1)} collective-permute-done((f32[2,8,16]{2,1,0:T(8,128)S(1)}, f32[2,8,16]{2,1,0:T(8,128)S(1)}, u32[]{:S(2)}, u32[]{:S(2)}) %collective-permute-start.1) | collective-permute-done | bytes 1056 | tf_op jit(solution)/shard_map/ppermute | solution.py:288
  80.9 0.1 collective-permute-start.2
  81.0 1.9 %collective-permute-start.3 = (f32[12,2,16]{2,1,0:T(2,128)S(1)}, f32[12,2,16]{2,1,0:T(2,128)S(1)}, u32[]{:S(2)}, u32[]{:S(2)}) collective-permute-start(f32[12,2,16]{2,1,0:T(2,128)S(1)} %get-tuple-element.62), channel_id=1, source_target_pairs={{0,31},{1,2},{2,1},{3,4},{4,3},{5,6},{6,5},{7,8},{8,7},{9,10},{10,... | collective-permute-start | bytes 4616 | tf_op jit(solution)/shard_map/ppermute | solution.py:298
  82.9 4.6 %collective-permute-done.3 = f32[12,2,16]{2,1,0:T(2,128)S(1)} collective-permute-done((f32[12,2,16]{2,1,0:T(2,128)S(1)}, f32[12,2,16]{2,1,0:T(2,128)S(1)}, u32[]{:S(2)}, u32[]{:S(2)}) %collective-permute-start.3) | collective-permute-done | bytes 1568 | tf_op jit(solution)/shard_map/ppermute | solution.py:298
  87.5 0.1 fusion.39
  87.6 0.1 fusion.40
  87.7 0.1 fusion.37
  87.9 0.1 fusion.42
  88.0 0.1 fusion.41
  88.1 0.1 fusion.9
  88.2 0.1 mul.166.scaled_ref
  88.3 8.5 %integrate.1 = (bf16[32,128,256]{2,1,0:T(8,128)(2,1)}, bf16[4,128,256]{2,1,0:T(8,128)(2,1)}, bf16[4,128,256]{2,1,0:T(8,128)(2,1)}, bf16[4,128,256]{2,1,0:T(8,128...) custom-call(s32[3,16]{1,0:T(4,128)S(1)} %pad_add_fusion.1.places_ref, ...), custom_call_target="tpu_custom_call" | custom-call | tf_op jit(solution)/shard_map/integrate/pallas_call | solution.py:182
  96.8 3.7 %all-to-all-start.1 = ((bf16[32,128,256]{2,1,0:T(8,128)(2,1)}), bf16[32,128,256]{2,1,0:T(8,128)(2,1)S(1)}, u32[]{:S(2)}, u32[]{:S(2)}) async-start(bf16[32,128,256]{2,1,0:T(8,128)(2,1)} %get-tuple-element.22), calls=%async_computation.1 | async-start | bytes 4194304 | tf_op jit(solution)/shard_map/all_to_all | solution.py:386
  100.6 0.1 add.318
  100.8 0.1 add.281
  100.9 0.6 gather_fusion.2
  101.4 0.6 gather_fusion.3
  102.0 0.2 fusion.14
  102.2 0.5 collective-permute-start.7
  102.7 0.2 compare_reduce_fusion
  102.9 0.1 collective-permute-start.9
  103.0 4.1 %collective-permute-start.10 = (bf16[4,128,256]{2,1,0:T(8,128)(2,1)}, bf16[4,128,256]{2,1,0:T(8,128)(2,1)S(1)}, u32[]{:S(2)}, u32[]{:S(2)}) collective-permute-start(bf16[4,128,256]{2,1,0:T(8,128)(2,1)} %get-tuple-element.31), channel_id=1, source_target_pairs={{0,16},{1,17},{2,18},{3,19},{4,20},{5,21},{6,22},{7,23},{8,24},{9,... | collective-permute-start | bytes 786440 | tf_op jit(solution)/shard_map/ppermute | solution.py:347
  107.1 0.3 collective-permute-start.11
  107.4 1.8 %collective-permute-start.12 = (bf16[4,128,256]{2,1,0:T(8,128)(2,1)}, bf16[4,128,256]{2,1,0:T(8,128)(2,1)}, u32[]{:S(2)}, u32[]{:S(2)}) collective-permute-start(bf16[4,128,256]{2,1,0:T(8,128)(2,1)} %get-tuple-element.33), channel_id=1, source_target_pairs={{0,24},{1,25},{2,26},{3,27},{4,28},{5,29},{6,30},{7,31},{8,0},{9,1... | collective-permute-start | bytes 786440 | tf_op jit(solution)/shard_map/ppermute | solution.py:347
  109.2 4.1 %collective-permute-done.8.refs_2_ = bf16[4,128,256]{2,1,0:T(8,128)(2,1)S(1)} collective-permute-done((bf16[4,128,256]{2,1,0:T(8,128)(2,1)}, bf16[4,128,256]{2,1,0:T(8,128)(2,1)S(1)}, u32[]{:S(2)}, u32[]{:S(2)}) %collective-permute-start.8) | collective-permute-done | bytes 262176 | tf_op jit(solution)/shard_map/ppermute | solution.py:347
  113.3 0.6 gather_fusion
  113.8 0.6 gather_fusion.1
  114.4 0.1 copy.19
  114.5 0.1 select_n.197.targets_ref
  114.6 0.2 compare_reduce_fusion.1
  114.8 0.2 fusion.13
  115.0 13.4 %collective-permute-done.9.refs_3_ = bf16[4,128,256]{2,1,0:T(8,128)(2,1)S(1)} collective-permute-done((bf16[4,128,256]{2,1,0:T(8,128)(2,1)}, bf16[4,128,256]{2,1,0:T(8,128)(2,1)S(1)}, u32[]{:S(2)}, u32[]{:S(2)}) %collective-permute-start.9) | collective-permute-done | bytes 262176 | tf_op jit(solution)/shard_map/ppermute | solution.py:347
  128.5 0.7 copy-done.2
  129.2 0.5 collective-permute-done.13.refs_7_
  129.7 0.9 copy-done.3
  130.6 3.9 %add_up.3 = (f32[3,128,256]{2,1,0:T(8,128)S(1)}, bf16[3,128,256]{2,1,0:T(8,128)(2,1)}, bf16[3,128,256]{2,1,0:T(8,128)(2,1)S(1)}, bf16[3,128,256]{2,1,0:T(8,128)(2,1)S(1)}) custom-call(s32[32]{0:T(128)S(1)} %select_n.197.targets_ref, bf16[4,128,256]{2,1,0:T(8,128)(2,1)S(1)} %copy-done.1, bf16[4,128,256]{2,1,0:T(8,128)(2,1)S(1)} %collective-permute-done.7.refs_1_, ...), custom_call_target="tpu_custom_call" | custom-call | tf_op jit(solution)/shard_map/add_up/pallas_call | solution.py:231
  134.5 0.7 copy-done.4
  135.2 0.7 copy-done.5
  135.8 1.7 %collective-permute-start.14 = (bf16[3,128,256]{2,1,0:T(8,128)(2,1)}, bf16[3,128,256]{2,1,0:T(8,128)(2,1)S(1)}, u32[]{:S(2)}, u32[]{:S(2)}) collective-permute-start(bf16[3,128,256]{2,1,0:T(8,128)(2,1)} %get-tuple-element.36), channel_id=1, source_target_pairs={{0,2},{1,3},{2,4},{3,5},{4,6},{5,7},{6,0},{7,1},{8,10},{9,11},{10,... | collective-permute-start | bytes 589832 | tf_op jit(solution)/shard_map/ppermute | solution.py:347
  137.6 0.1 copy.17
  137.6 0.1 select_n.175.targets_ref
  137.7 2.7 %collective-permute-start.15 = (bf16[3,128,256]{2,1,0:T(8,128)(2,1)}, bf16[3,128,256]{2,1,0:T(8,128)(2,1)S(1)}, u32[]{:S(2)}, u32[]{:S(2)}) collective-permute-start(bf16[3,128,256]{2,1,0:T(8,128)(2,1)} %copy-done.5), channel_id=1, source_target_pairs={{0,4},{1,5},{2,6},{3,7},{4,0},{5,1},{6,2},{7,3},{8,12},{9,13},{10,... | collective-permute-start | bytes 589832 | tf_op jit(solution)/shard_map/ppermute | solution.py:347
  140.5 1.5 collective-permute-start.16
  142.0 2.7 %add_up.2 = (f32[3,128,256]{2,1,0:T(8,128)S(1)}, bf16[3,128,256]{2,1,0:T(8,128)(2,1)S(1)}, bf16[3,128,256]{2,1,0:T(8,128)(2,1)S(1)}, bf16[3,128,256]{2,1,0:T(8,128)(2,1)S(1)}) custom-call(s32[32]{0:T(128)S(1)} %select_n.175.targets_ref, bf16[32,128,256]{2,1,0:T(8,128)(2,1)S(1)} %all-to-all-done.1.refs_0_), custom_call_target="tpu_custom_call" | custom-call | tf_op jit(solution)/shard_map/add_up/pallas_call | solution.py:231
  144.7 2.5 %collective-permute-start.4 = (bf16[3,128,256]{2,1,0:T(8,128)(2,1)S(1)}, bf16[3,128,256]{2,1,0:T(8,128)(2,1)S(1)}, u32[]{:S(2)}, u32[]{:S(2)}) collective-permute-start(bf16[3,128,256]{2,1,0:T(8,128)(2,1)S(1)} %get-tuple-element.24), channel_id=1, source_target_pairs={{0,8},{1,9},{2,10},{3,11},{4,12},{5,13},{6,14},{7,15},{8,16},{9,17... | collective-permute-start | bytes 589832 | tf_op jit(solution)/shard_map/ppermute | solution.py:347
  147.2 1.9 %collective-permute-start.5 = (bf16[3,128,256]{2,1,0:T(8,128)(2,1)S(1)}, bf16[3,128,256]{2,1,0:T(8,128)(2,1)S(1)}, u32[]{:S(2)}, u32[]{:S(2)}) collective-permute-start(bf16[3,128,256]{2,1,0:T(8,128)(2,1)S(1)} %get-tuple-element.25), channel_id=1, source_target_pairs={{0,16},{1,17},{2,18},{3,19},{4,20},{5,21},{6,22},{7,23},{8,24},{9,... | collective-permute-start | bytes 589832 | tf_op jit(solution)/shard_map/ppermute | solution.py:347
  149.2 0.8 collective-permute-start.6
  150.0 2.9 %collective-permute-done.4.refs_1_ = bf16[3,128,256]{2,1,0:T(8,128)(2,1)S(1)} collective-permute-done((bf16[3,128,256]{2,1,0:T(8,128)(2,1)S(1)}, bf16[3,128,256]{2,1,0:T(8,128)(2,1)S(1)}, u32[]{:S(2)}, u32[]{:S(2)}) %collective-permute-start.4) | collective-permute-done | bytes 196640 | tf_op jit(solution)/shard_map/ppermute | solution.py:347
  152.9 5.2 %collective-permute-done.5.refs_2_ = bf16[3,128,256]{2,1,0:T(8,128)(2,1)S(1)} collective-permute-done((bf16[3,128,256]{2,1,0:T(8,128)(2,1)S(1)}, bf16[3,128,256]{2,1,0:T(8,128)(2,1)S(1)}, u32[]{:S(2)}, u32[]{:S(2)}) %collective-permute-start.5) | collective-permute-done | bytes 196640 | tf_op jit(solution)/shard_map/ppermute | solution.py:347
  158.1 1.5 join.1
  (52 shorter events, 0.5 us)
Async XLA Ops:
  0.9 1.0 copy-start
  4.8 7.5 %copy-start.6 = (s32[1,16,256]{2,1,0:T(8,128)S(1)}, s32[1,16,256]{2,1,0:T(8,128)}, u32[]{:S(2)}) copy-start(s32[1,16,256]{2,1,0:T(8,128)} %param.9) | copy-start | bytes 49156
  4.8 7.5 %copy-start.7 = (s32[1,16,256]{2,1,0:T(8,128)S(1)}, s32[1,16,256]{2,1,0:T(8,128)}, u32[]{:S(2)}) copy-start(s32[1,16,256]{2,1,0:T(8,128)} %param.8) | copy-start | bytes 49156
  4.8 60.2 %all-to-all-start = ((bf16[32,256,256]{2,1,0:T(8,128)(2,1)}), bf16[32,256,256]{2,1,0:T(8,128)(2,1)}, u32[]{:S(2)}, u32[]{:S(2)}) async-start(bf16[32,256,256]{2,1,0:T(8,128)(2,1)} %pick_blocks.1), calls=%async_computation | async-start | bytes 8388608 | tf_op jit(solution)/shard_map/all_to_all | solution.py:371
  72.7 4.5 %collective-permute-start = (f32[2,8,16]{2,1,0:T(8,128)S(1)}, f32[2,8,16]{2,1,0:T(8,128)S(1)}, u32[]{:S(2)}, u32[]{:S(2)}) collective-permute-start(f32[2,8,16]{2,1,0:T(8,128)S(1)} %slice.120), channel_id=1, source_target_pairs={{0,32},{32,64},{64,96},{96,128},{128,160},{160,192},{192,224},{224... | collective-permute-start | bytes 3080 | tf_op jit(solution)/shard_map/ppermute | solution.py:287
  76.0 4.9 %collective-permute-start.1 = (f32[2,8,16]{2,1,0:T(8,128)S(1)}, f32[2,8,16]{2,1,0:T(8,128)S(1)}, u32[]{:S(2)}, u32[]{:S(2)}) collective-permute-start(f32[2,8,16]{2,1,0:T(8,128)S(1)} %slice.122), channel_id=1, source_target_pairs={{32,0},{64,32},{96,64},{128,96},{160,128},{192,160},{224,192},{0,2... | collective-permute-start | bytes 3080 | tf_op jit(solution)/shard_map/ppermute | solution.py:288
  80.9 2.1 %collective-permute-start.2 = (f32[12,2,16]{2,1,0:T(2,128)S(1)}, f32[12,2,16]{2,1,0:T(2,128)S(1)}, u32[]{:S(2)}, u32[]{:S(2)}) collective-permute-start(f32[12,2,16]{2,1,0:T(2,128)S(1)} %get-tuple-element.61), channel_id=1, source_target_pairs={{0,1},{1,0},{2,3},{3,2},{4,5},{5,4},{6,7},{7,6},{8,9},{9,8},{10,11... | collective-permute-start | bytes 4616 | tf_op jit(solution)/shard_map/ppermute | solution.py:299
  81.0 6.5 %collective-permute-start.3 = (f32[12,2,16]{2,1,0:T(2,128)S(1)}, f32[12,2,16]{2,1,0:T(2,128)S(1)}, u32[]{:S(2)}, u32[]{:S(2)}) collective-permute-start(f32[12,2,16]{2,1,0:T(2,128)S(1)} %get-tuple-element.62), channel_id=1, source_target_pairs={{0,31},{1,2},{2,1},{3,4},{4,3},{5,6},{6,5},{7,8},{8,7},{9,10},{10,... | collective-permute-start | bytes 4616 | tf_op jit(solution)/shard_map/ppermute | solution.py:298
  96.8 32.8 %copy-start.1 = (bf16[4,128,256]{2,1,0:T(8,128)(2,1)S(1)}, bf16[4,128,256]{2,1,0:T(8,128)(2,1)}, u32[]{:S(2)}) copy-start(bf16[4,128,256]{2,1,0:T(8,128)(2,1)} %get-tuple-element.27.refs_0_) | copy-start | bytes 786436
  96.8 45.2 %all-to-all-start.1 = ((bf16[32,128,256]{2,1,0:T(8,128)(2,1)}), bf16[32,128,256]{2,1,0:T(8,128)(2,1)S(1)}, u32[]{:S(2)}, u32[]{:S(2)}) async-start(bf16[32,128,256]{2,1,0:T(8,128)(2,1)} %get-tuple-element.22), calls=%async_computation.1 | async-start | bytes 4194304 | tf_op jit(solution)/shard_map/all_to_all | solution.py:386
  102.2 5.2 %collective-permute-start.7 = (bf16[4,128,256]{2,1,0:T(8,128)(2,1)}, bf16[4,128,256]{2,1,0:T(8,128)(2,1)S(1)}, u32[]{:S(2)}, u32[]{:S(2)}) collective-permute-start(bf16[4,128,256]{2,1,0:T(8,128)(2,1)} %get-tuple-element.28), channel_id=1, source_target_pairs={{0,1},{1,0},{2,3},{3,2},{4,5},{5,4},{6,7},{7,6},{8,9},{9,8},{10,11... | collective-permute-start | bytes 786440 | tf_op jit(solution)/shard_map/ppermute | solution.py:347
  102.7 10.6 %collective-permute-start.8 = (bf16[4,128,256]{2,1,0:T(8,128)(2,1)}, bf16[4,128,256]{2,1,0:T(8,128)(2,1)S(1)}, u32[]{:S(2)}, u32[]{:S(2)}) collective-permute-start(bf16[4,128,256]{2,1,0:T(8,128)(2,1)} %get-tuple-element.29), channel_id=1, source_target_pairs={{0,8},{1,9},{2,10},{3,11},{4,12},{5,13},{6,14},{7,15},{8,16},{9,17... | collective-permute-start | bytes 786440 | tf_op jit(solution)/shard_map/ppermute | solution.py:347
  102.9 25.5 %collective-permute-start.9 = (bf16[4,128,256]{2,1,0:T(8,128)(2,1)}, bf16[4,128,256]{2,1,0:T(8,128)(2,1)S(1)}, u32[]{:S(2)}, u32[]{:S(2)}) collective-permute-start(bf16[4,128,256]{2,1,0:T(8,128)(2,1)} %get-tuple-element.30), channel_id=1, source_target_pairs={{0,9},{1,8},{2,11},{3,10},{4,13},{5,12},{6,15},{7,14},{8,17},{9,16... | collective-permute-start | bytes 786440 | tf_op jit(solution)/shard_map/ppermute | solution.py:347
  103.0 25.4 %collective-permute-start.10 = (bf16[4,128,256]{2,1,0:T(8,128)(2,1)}, bf16[4,128,256]{2,1,0:T(8,128)(2,1)S(1)}, u32[]{:S(2)}, u32[]{:S(2)}) collective-permute-start(bf16[4,128,256]{2,1,0:T(8,128)(2,1)} %get-tuple-element.31), channel_id=1, source_target_pairs={{0,16},{1,17},{2,18},{3,19},{4,20},{5,21},{6,22},{7,23},{8,24},{9,... | collective-permute-start | bytes 786440 | tf_op jit(solution)/shard_map/ppermute | solution.py:347
  107.1 22.0 %collective-permute-start.11 = (bf16[4,128,256]{2,1,0:T(8,128)(2,1)}, bf16[4,128,256]{2,1,0:T(8,128)(2,1)}, u32[]{:S(2)}, u32[]{:S(2)}) collective-permute-start(bf16[4,128,256]{2,1,0:T(8,128)(2,1)} %get-tuple-element.32), channel_id=1, source_target_pairs={{0,17},{1,16},{2,19},{3,18},{4,21},{5,20},{6,23},{7,22},{8,25},{9,... | collective-permute-start | bytes 786440 | tf_op jit(solution)/shard_map/ppermute | solution.py:347
  107.4 21.7 %collective-permute-start.12 = (bf16[4,128,256]{2,1,0:T(8,128)(2,1)}, bf16[4,128,256]{2,1,0:T(8,128)(2,1)}, u32[]{:S(2)}, u32[]{:S(2)}) collective-permute-start(bf16[4,128,256]{2,1,0:T(8,128)(2,1)} %get-tuple-element.33), channel_id=1, source_target_pairs={{0,24},{1,25},{2,26},{3,27},{4,28},{5,29},{6,30},{7,31},{8,0},{9,1... | collective-permute-start | bytes 786440 | tf_op jit(solution)/shard_map/ppermute | solution.py:347
  113.3 16.4 %collective-permute-start.13 = (bf16[4,128,256]{2,1,0:T(8,128)(2,1)}, bf16[4,128,256]{2,1,0:T(8,128)(2,1)}, u32[]{:S(2)}, u32[]{:S(2)}) collective-permute-start(bf16[4,128,256]{2,1,0:T(8,128)(2,1)} %get-tuple-element.34), channel_id=1, source_target_pairs={{0,25},{1,24},{2,27},{3,26},{4,29},{5,28},{6,31},{7,30},{8,1},{9,0... | collective-permute-start | bytes 786440 | tf_op jit(solution)/shard_map/ppermute | solution.py:347
  128.5 0.7 copy-start.2
  129.7 1.0 copy-start.3
  134.5 0.7 copy-start.4
  135.2 0.7 copy-start.5
  135.8 13.3 %collective-permute-start.14 = (bf16[3,128,256]{2,1,0:T(8,128)(2,1)}, bf16[3,128,256]{2,1,0:T(8,128)(2,1)S(1)}, u32[]{:S(2)}, u32[]{:S(2)}) collective-permute-start(bf16[3,128,256]{2,1,0:T(8,128)(2,1)} %get-tuple-element.36), channel_id=1, source_target_pairs={{0,2},{1,3},{2,4},{3,5},{4,6},{5,7},{6,0},{7,1},{8,10},{9,11},{10,... | collective-permute-start | bytes 589832 | tf_op jit(solution)/shard_map/ppermute | solution.py:347
  137.7 12.3 %collective-permute-start.15 = (bf16[3,128,256]{2,1,0:T(8,128)(2,1)}, bf16[3,128,256]{2,1,0:T(8,128)(2,1)S(1)}, u32[]{:S(2)}, u32[]{:S(2)}) collective-permute-start(bf16[3,128,256]{2,1,0:T(8,128)(2,1)} %copy-done.5), channel_id=1, source_target_pairs={{0,4},{1,5},{2,6},{3,7},{4,0},{5,1},{6,2},{7,3},{8,12},{9,13},{10,... | collective-permute-start | bytes 589832 | tf_op jit(solution)/shard_map/ppermute | solution.py:347
  140.5 9.6 %collective-permute-start.16 = (bf16[3,128,256]{2,1,0:T(8,128)(2,1)}, bf16[3,128,256]{2,1,0:T(8,128)(2,1)S(1)}, u32[]{:S(2)}, u32[]{:S(2)}) collective-permute-start(bf16[3,128,256]{2,1,0:T(8,128)(2,1)} %copy-done.4), channel_id=1, source_target_pairs={{0,6},{1,7},{2,0},{3,1},{4,2},{5,3},{6,4},{7,5},{8,14},{9,15},{10,... | collective-permute-start | bytes 589832 | tf_op jit(solution)/shard_map/ppermute | solution.py:347
  144.7 8.2 %collective-permute-start.4 = (bf16[3,128,256]{2,1,0:T(8,128)(2,1)S(1)}, bf16[3,128,256]{2,1,0:T(8,128)(2,1)S(1)}, u32[]{:S(2)}, u32[]{:S(2)}) collective-permute-start(bf16[3,128,256]{2,1,0:T(8,128)(2,1)S(1)} %get-tuple-element.24), channel_id=1, source_target_pairs={{0,8},{1,9},{2,10},{3,11},{4,12},{5,13},{6,14},{7,15},{8,16},{9,17... | collective-permute-start | bytes 589832 | tf_op jit(solution)/shard_map/ppermute | solution.py:347
  147.2 10.9 %collective-permute-start.5 = (bf16[3,128,256]{2,1,0:T(8,128)(2,1)S(1)}, bf16[3,128,256]{2,1,0:T(8,128)(2,1)S(1)}, u32[]{:S(2)}, u32[]{:S(2)}) collective-permute-start(bf16[3,128,256]{2,1,0:T(8,128)(2,1)S(1)} %get-tuple-element.25), channel_id=1, source_target_pairs={{0,16},{1,17},{2,18},{3,19},{4,20},{5,21},{6,22},{7,23},{8,24},{9,... | collective-permute-start | bytes 589832 | tf_op jit(solution)/shard_map/ppermute | solution.py:347
  149.2 9.0 %collective-permute-start.6 = (bf16[3,128,256]{2,1,0:T(8,128)(2,1)S(1)}, bf16[3,128,256]{2,1,0:T(8,128)(2,1)S(1)}, u32[]{:S(2)}, u32[]{:S(2)}) collective-permute-start(bf16[3,128,256]{2,1,0:T(8,128)(2,1)S(1)} %get-tuple-element.26), channel_id=1, source_target_pairs={{0,24},{1,25},{2,26},{3,27},{4,28},{5,29},{6,30},{7,31},{8,0},{9,1... | collective-permute-start | bytes 589832 | tf_op jit(solution)/shard_map/ppermute | solution.py:347

commit v4 on v2

--- a/solution.py
+++ b/solution.py
@@ -5,9 +5,11 @@
 from jax import lax
 from jax.experimental import pallas as pl
 from jax.experimental.pallas import tpu as pltpu
+from jax.sharding import Mesh
 from jax.sharding import PartitionSpec as P
 
 GRAD_WEIGHT = 0.5
+BRICK = ("x", "y", "core")
 MIB = 1024 * 1024
 
 
@@ -126,16 +128,18 @@
     )(slots, blocks, tables)
 
 
-def integrate(slots, scaled, tables, total):
+def integrate(places, scaled, tables, parts, inner):
     count, both, points = tables.shape
     width = both // 2
 
-    def kernel(slots_ref, scaled_ref, tables_ref, out_ref, held, kept, sems):
+    def kernel(places_ref, scaled_ref, tables_ref, *rest):
+        outs, (held, kept, sems) = rest[:parts], rest[parts:]
+
         def fetch(j):
-            return pltpu.make_async_copy(tables_ref.at[j], kept.at[j], sems.at[1, j])
-
-        def leave(j):
-            return pltpu.make_async_copy(held.at[j], out_ref.at[slots_ref[j]], sems.at[0, j])
+            return pltpu.make_async_copy(tables_ref.at[j], kept.at[j], sems.at[0, j])
+
+        def leave(j, part):
+            return pltpu.make_async_copy(held.at[j], outs[part].at[places_ref[1, j]], sems.at[1, j])
 
         for j in range(count):
             fetch(j).start()
@@ -151,18 +155,23 @@
                 (((1,), (1,)), ((), ())),
                 preferred_element_type=jnp.float32,
             ).astype(jnp.bfloat16)
-            leave(j).start()
+            for part in range(parts):
+
+                @pl.when(places_ref[0, j] == part)
+                def _():
+                    leave(j, part).start()
+
             return carry
 
         lax.fori_loop(0, count, body, 0)
         for j in range(count):
-            leave(j).wait()
-
-    return pl.pallas_call(
-        kernel,
-        out_shape=pltpu.HBM((total, width, width), jnp.bfloat16),
+            leave(j, 0).wait()
+
+    return pl.pallas_call(
+        kernel,
+        out_shape=[pltpu.HBM((inner, width, width), jnp.bfloat16)] * parts,
         in_specs=[SCALARS, RESIDENT, IN_HBM],
-        out_specs=IN_HBM,
+        out_specs=[IN_HBM] * parts,
         scratch_shapes=[
             pltpu.VMEM((count, width, width), jnp.bfloat16),
             pltpu.VMEM(tables.shape, tables.dtype),
@@ -170,43 +179,49 @@
         ],
         compiler_params=params(52),
         name="integrate",
-    )(slots, scaled, tables)
-
-
-def add_up(targets, parts, own_count):
-    count, rows, cols = parts.shape
-
-    def kernel(targets_ref, parts_ref, out_ref, held, sems):
-        def fetch(i):
-            return pltpu.make_async_copy(parts_ref.at[i], held.at[i], sems.at[i])
-
-        for i in range(count):
-
-            @pl.when(targets_ref[i] >= 0)
+    )(places, scaled, tables)
+
+
+def add_up(targets, parts, place, own_count, dtype):
+    _, rows, cols = parts[0].shape
+    count = len(parts)
+
+    def kernel(targets_ref, *refs):
+        parts_refs, (out_ref, held, total, sems) = refs[:count], refs[count:]
+
+        def fetch(s):
+            return pltpu.make_async_copy(parts_refs[s].at[place], held.at[s], sems.at[s])
+
+        for s in range(count):
+
+            @pl.when(targets_ref[s] >= 0)
             def _():
-                fetch(i).start()
-
-        out_ref[...] = jnp.zeros_like(out_ref)
-        for i in range(count):
-            target = targets_ref[i]
+                fetch(s).start()
+
+        total[...] = jnp.zeros_like(total)
+        for s in range(count):
+            target = targets_ref[s]
 
             @pl.when(target >= 0)
             def _():
-                fetch(i).wait()
-                out_ref[target] += held[i].astype(jnp.float32)
-
-    return pl.pallas_call(
-        kernel,
-        out_shape=jax.ShapeDtypeStruct((own_count, rows, cols), jnp.float32),
-        in_specs=[SCALARS, IN_HBM],
+                fetch(s).wait()
+                total[target] += held[s].astype(jnp.float32)
+
+        out_ref[...] = total[...].astype(dtype)
+
+    return pl.pallas_call(
+        kernel,
+        out_shape=jax.ShapeDtypeStruct((own_count, rows, cols), dtype),
+        in_specs=[SCALARS] + [IN_HBM] * count,
         out_specs=RESIDENT,
         scratch_shapes=[
-            pltpu.VMEM((count, rows, cols), parts.dtype),
+            pltpu.VMEM((count, rows, cols), jnp.bfloat16),
+            pltpu.VMEM((own_count, rows, cols), jnp.float32),
             pltpu.SemaphoreType.DMA((count,)),
         ],
-        compiler_params=params(12),
+        compiler_params=params(8),
         name="add_up",
-    )(targets, parts)
+    )(targets, *parts)
 
 
 def ends(block, dim, width):
@@ -228,7 +243,7 @@
 
 
 def extended_pairs(block, axis, dim, width):
-    count = lax.axis_size(axis)
+    count = size_of(axis)
     odd = lax.axis_index(axis) % 2 == 1
     low, high = ends(block, dim, width)
     within = [(i, i ^ 1) for i in range(count)]
@@ -270,39 +285,91 @@
     return density / jnp.sqrt(1.0 + density * density) - diverge
 
 
+def size_of(axes):
+    return math.prod(lax.axis_size(axis) for axis in axes)
+
+
+def moved(value, stage, step, other=False):
+    nx, ny, nc = (lax.axis_size(axis) for axis in BRICK)
+    pairs = []
+    for x in range(nx):
+        for y in range(ny):
+            for c in range(nc):
+                core = (c + 1) % nc if other else c
+                along_y = (core == 0) == (stage == 1)
+                to_x, to_y = (x, (y + step) % ny) if along_y else ((x + step) % nx, y)
+                pairs.append(((x * ny + y) * nc + c, (to_x * ny + to_y) * nc + core))
+    return lax.ppermute(value, BRICK, pairs)
+
+
+def find(owners, ids, bricks, wanted):
+    hit = owners[bricks][:, None, :] == wanted[None, :, None]
+    number = jnp.sum(jnp.where(hit, ids[bricks][:, None, :], 0), axis=-1)
+    return jnp.where(jnp.any(hit, axis=-1), number, -1).astype(jnp.int32)
+
+
 def local(store, crossing, phi, rows_index, cols_index):
-    position = lax.axis_index("brick")
-    brick_count = lax.axis_size("brick")
+    nx, ny, nc = (lax.axis_size(axis) for axis in BRICK)
+    x, y, c = (lax.axis_index(axis) for axis in BRICK)
+    position = (x * ny + y) * nc + c
     own_count, width = store.shape[0], store.shape[1]
     size_x, size_y, size_z, functions = phi.shape
     points = size_x * size_y * size_z
     owners = crossing // own_count
+    ids = crossing % own_count
     chosen = owners == position
-    filled = jnp.any(chosen, axis=-1)
-    send_ids = jnp.sum(jnp.where(chosen, crossing % own_count, 0), axis=-1)
+    send_ids = jnp.sum(jnp.where(chosen, ids, 0), axis=-1)
     slots = lax.dynamic_index_in_dim(owners, position, 0, keepdims=False)
 
     sending = pick_blocks(send_ids, store)
-    blocks = lax.all_to_all(sending, "brick", split_axis=0, concat_axis=0, tiled=True)
+    blocks = lax.all_to_all(sending, BRICK, split_axis=0, concat_axis=0, tiled=True)
     table = phi.reshape(points, functions).T
     index = jnp.concatenate([rows_index[0], cols_index[0]], axis=1)[:, None, :]
     tables = gather_tables(index, table)
     density = jnp.sum(collocate(slots, blocks, tables), axis=0).reshape(size_x, size_y, size_z)
-    padded = extended_pairs(extended_ring(density, "grp", 0, 2), "brick", 1, 2)
+    padded = extended_pairs(extended_ring(density, "grp", 0, 2), BRICK, 1, 2)
     scaled = potential_of(padded).reshape(1, points) * (1.0 / math.sqrt(points))
-    returning = integrate(slots, scaled, tables, brick_count)
-    arrived = lax.all_to_all(returning, "brick", split_axis=0, concat_axis=0, tiled=True)
-    targets = jnp.where(filled, send_ids, -1)
-    return add_up(targets, arrived, own_count)
+
+    to_x, rest = slots // (ny * nc), slots % (ny * nc)
+    to_y, to_c = rest // nc, rest % nc
+    ahead_x, ahead_y = (to_x - x) % nx, (to_y - y) % ny
+    side = nx
+    first = jnp.where(to_c == 0, ahead_y, ahead_x)
+    second = jnp.where(to_c == 0, ahead_x, ahead_y)
+    places = jnp.stack([first + jnp.where(to_c == c, 0, side), second]).astype(jnp.int32)
+    parts = list(integrate(places, scaled, tables, 2 * side, side))
+    for step in [side // 2] + [k for k in range(side) if k not in (side // 2, 0)] + [0]:
+        for other in (0, 1):
+            if step or other:
+                i = other * side + step
+                parts[i] = moved(parts[i], 1, step, bool(other))
+    steps = jnp.arange(side)
+    behind = jnp.where(c == 0, x * ny + (y - steps) % ny, ((x - steps) % nx) * ny + y) * nc
+    sources = jnp.concatenate([behind + c, behind + (1 - c)])
+    wanted = jnp.where(c == 0, ((x + steps) % nx) * ny + y, x * ny + (y + steps) % ny) * nc + c
+    targets = find(owners, ids, sources, wanted)
+    total = []
+    for step in [side // 2] + [k for k in range(side) if k not in (side // 2, 0)]:
+        summed = add_up(targets[:, step], parts, step, own_count, jnp.bfloat16)
+        total.append(moved(summed, 2, step))
+    own = add_up(targets[:, 0], parts, 0, own_count, jnp.float32)
+    for piece in total:
+        own = own + piece.astype(jnp.float32)
+    return own
 
 
 def solution(mesh):
+    groups, bricks = mesh.shape["grp"], mesh.shape["brick"]
+    side = math.isqrt(bricks // 2)
+    split = Mesh(mesh.devices.reshape(groups, side, bricks // (2 * side), 2), ("grp",) + BRICK)
+    whole = ("grp",) + BRICK
     in_specs = (
-        P(("grp", "brick"), None, None),
+        P(whole, None, None),
         P("grp", None),
-        P("grp", "brick", None, None),
-        P(("grp", "brick"), None, None),
-        P(("grp", "brick"), None, None),
+        P("grp", BRICK, None, None),
+        P(whole, None, None),
+        P(whole, None, None),
     )
-    out_specs = P(("grp", "brick"), None, None)
-    return jax.shard_map(local, mesh=mesh, in_specs=in_specs, out_specs=out_specs, check_vma=False)
+    return jax.shard_map(
+        local, mesh=split, in_specs=in_specs, out_specs=P(whole, None, None), check_vma=False
+    )

time: 160 us -> 147 us (0.919)
  waiting for transfers between devices: 89.5 us -> 67.2 us
  starting transfers between devices: 17.5 us -> 21.4 us
  Pallas kernels: 44 us -> 46.9 us
  local copies, waits for them, and re-layouts: 4.76 us -> 7.5 us
    all_to_all x2 -> x1, waiting for transfers between devices: 80.1 us -> 27.7 us  [local(): lax.all_to_all(sending, BRICK, split_axis=0, concat_axis=0, tiled=True)]
    ppermute x0 -> x10, waiting for transfers between devices: none -> 30.1 us  [moved(): return lax.ppermute(value, BRICK, pairs)]
    ppermute x0 -> x10, starting transfers between devices: none -> 8.78 us  [moved(): return lax.ppermute(value, BRICK, pairs)]
    all_to_all x2 -> x1, starting transfers between devices: 12.3 us -> 7.46 us  [local(): lax.all_to_all(sending, BRICK, split_axis=0, concat_axis=0, tiled=True)]
    pallas_call x1 -> x4, Pallas kernels: 3.25 us -> 6.12 us  [add_up(): pl.pallas_call(kernel, out_shape=jax.ShapeDtypeStruct((own_count, rows, c...]
    unnamed x8 -> x11, local copies, waits for them, and re-layouts: 1.01 us -> 2.82 us
  transfers between devices with their start and end apart: 6 -> 15, of which waited for: 5 -> 11; matrix products, arithmetic and copies ran while one was open for 2% -> 3% of each run, Pallas kernels for 14% -> 19%
where the time goes in v4:
time: 147 us; the launch traced here: 145 us
  waiting for transfers between devices  67.2 us (46%)
  Pallas kernels  46.9 us (32%)
  starting transfers between devices  21.4 us (15%)
  local copies, waits for them, and re-layouts  7.5 us (5%)
  other arithmetic  2.09 us (1%)
    ppermute x10, waiting for transfers between devices, moved(): return lax.ppermute(value, BRICK, pairs)  30.1 us
    all_to_all x1, waiting for transfers between devices, local(): lax.all_to_all(sending, BRICK, split_axis=0, concat_axis=0, tiled=True)  27.7 us
    pallas_call x1, Pallas kernels, gather_tables(): pl.pallas_call(kernel, out_shape=pltpu.HBM((count, width, points), jnp.bf...  22.1 us
    ppermute x10, starting transfers between devices, moved(): return lax.ppermute(value, BRICK, pairs)  8.78 us
    pallas_call x1, Pallas kernels, integrate(): pl.pallas_call(kernel, out_shape=[pltpu.HBM((inner, width, width), jnp.bf...  8.36 us
    pallas_call x1, Pallas kernels, collocate(): pl.pallas_call(kernel, out_shape=jax.ShapeDtypeStruct((8, points), jnp.fl...  7.54 us
    all_to_all x1, starting transfers between devices, local(): lax.all_to_all(sending, BRICK, split_axis=0, concat_axis=0, tiled=True)  7.46 us
    pallas_call x4, Pallas kernels, add_up(): pl.pallas_call(kernel, out_shape=jax.ShapeDtypeStruct((own_count, rows, c...  6.12 us
  transfers between devices with their start and end apart: 15, of which 11 were waited for; matrix products, arithmetic and copies ran while one was open for 3% of the time, Pallas kernels for 19%

profile of v4, /device:TPU:96, one launch (start us, length us, event | category | flops | bytes accessed | tf_op | source)
XLA Modules:
  0.0 145.5 jit_solution(17247789120387189082)
XLA Ops:
  0.0 0.8 copy.14
  0.8 0.1 select_reduce_fusion
  0.9 0.0 copy-start.1
  0.9 1.0 copy-done.1
  1.9 2.8 %pick_blocks.1 = bf16[32,256,256]{2,1,0:T(8,128)(2,1)} custom-call(s32[32]{0:T(128)S(1)} %get-tuple-element.49.ids_ref, bf16[3,256,256]{2,1,0:T(8,128)(2,1)S(1)} %copy-done.1), custom_call_target="tpu_custom_call" | custom-call | tf_op jit(solution)/shard_map/pick_blocks/pallas_call | solution.py:38
  4.7 0.0 copy-start.2
  4.8 0.0 copy-start.3
  4.8 7.5 %all-to-all-start = ((bf16[32,256,256]{2,1,0:T(8,128)(2,1)}), bf16[32,256,256]{2,1,0:T(8,128)(2,1)}, u32[]{:S(2)}, u32[]{:S(2)}) async-start(bf16[32,256,256]{2,1,0:T(8,128)(2,1)} %pick_blocks.1), calls=%async_computation | async-start | bytes 8388608 | tf_op jit(solution)/shard_map/all_to_all | solution.py:325
  12.2 0.0 copy-done.2
  12.2 0.0 copy-done.3
  12.3 2.9 %copy.17 = bf16[1024,1024]{0,1:T(8,128)(2,1)S(1)} copy(bf16[1024,1024]{1,0:T(8,128)(2,1)} %bitcast.25) | data formatting | bytes 4194304 | tf_op jit(solution)/shard_map/reshape | solution.py:326
  15.2 22.1 %gather_tables.1.tables_ref = bf16[16,512,1024]{2,1,0:T(8,128)(2,1)} custom-call(s32[16,1,512]{2,1,0:T(1,128)S(1)} %broadcast_in_dim.33.index_ref, bf16[1024,1024]{1,0:T(8,128)(2,1)S(1)} %bitcast.24), custom_call_target="tpu_custom_call" | custom-call | flops 17179869184 | bytes 16777216 | tf_op jit(solution)/shard_map/gather_tables/pallas_call | solution.py:71
  37.3 27.7 %all-to-all-done.blocks_ref = bf16[32,256,256]{2,1,0:T(8,128)(2,1)} async-done(((bf16[32,256,256]{2,1,0:T(8,128)(2,1)}), bf16[32,256,256]{2,1,0:T(8,128)(2,1)}, u32[]{:S(2)}, u32[]{:S(2)}) %all-to-all-start) | async-done | bytes 4194336 | tf_op jit(solution)/shard_map/all_to_all | solution.py:325
  65.0 7.5 %collocate.1 = f32[8,1024]{1,0:T(8,128)S(1)} custom-call(s32[16]{0:T(128)S(1)} %get-tuple-element.52.slots_ref, bf16[32,256,256]{2,1,0:T(8,128)(2,1)} %all-to-all-done.blocks_ref, bf16[16,512,1024]{2,1,0:T(8,128)(2,1)} %gather_tables.1.tables_ref), custom_call_target="tpu_custom_call" | custom-call | tf_op jit(solution)/shard_map/collocate/pallas_call | solution.py:116
  72.6 0.1 slice.133
  72.7 3.1 %collective-permute-start = (f32[2,8,16]{2,1,0:T(8,128)S(1)}, f32[2,8,16]{2,1,0:T(8,128)S(1)}, u32[]{:S(2)}, u32[]{:S(2)}) collective-permute-start(f32[2,8,16]{2,1,0:T(8,128)S(1)} %slice.133), channel_id=1, source_target_pairs={{0,32},{32,64},{64,96},{96,128},{128,160},{160,192},{192,224},{224... | collective-permute-start | bytes 3080 | tf_op jit(solution)/shard_map/ppermute | solution.py:240
  75.8 0.1 reshape.129
  75.9 0.1 slice.135
  76.0 0.0 collective-permute-start.1
  76.0 1.2 collective-permute-done
  77.2 3.7 %collective-permute-done.1 = f32[2,8,16]{2,1,0:T(8,128)S(1)} collective-permute-done((f32[2,8,16]{2,1,0:T(8,128)S(1)}, f32[2,8,16]{2,1,0:T(8,128)S(1)}, u32[]{:S(2)}, u32[]{:S(2)}) %collective-permute-start.1) | collective-permute-done | bytes 1056 | tf_op jit(solution)/shard_map/ppermute | solution.py:241
  80.9 0.1 collective-permute-start.2
  81.0 1.9 %collective-permute-start.3 = (f32[12,2,16]{2,1,0:T(2,128)S(1)}, f32[12,2,16]{2,1,0:T(2,128)S(1)}, u32[]{:S(2)}, u32[]{:S(2)}) collective-permute-start(f32[12,2,16]{2,1,0:T(2,128)S(1)} %get-tuple-element.46), channel_id=1, source_target_pairs={{0,31},{1,2},{2,1},{3,4},{4,3},{5,6},{6,5},{7,8},{8,7},{9,10},{10,... | collective-permute-start | bytes 4616 | tf_op jit(solution)/shard_map/ppermute | solution.py:251
  82.9 0.0 collective-permute-done.2
  82.9 4.6 %collective-permute-done.3 = f32[12,2,16]{2,1,0:T(2,128)S(1)} collective-permute-done((f32[12,2,16]{2,1,0:T(2,128)S(1)}, f32[12,2,16]{2,1,0:T(2,128)S(1)}, u32[]{:S(2)}, u32[]{:S(2)}) %collective-permute-start.3) | collective-permute-done | bytes 1568 | tf_op jit(solution)/shard_map/ppermute | solution.py:251
  87.5 0.1 fusion.36
  87.6 0.1 fusion.37
  87.7 0.1 fusion.33
  87.9 0.1 fusion.39
  87.9 0.1 fusion.38
  88.1 0.1 fusion.9
  88.2 0.1 mul.176.scaled_ref
  88.3 8.4 %integrate.1 = (bf16[4,256,256]{2,1,0:T(8,128)(2,1)}, bf16[4,256,256]{2,1,0:T(8,128)(2,1)}, bf16[4,256,256]{2,1,0:T(8,128)(2,1)}, bf16[4,256,256]{2,1,0:T(8,128)...) custom-call(s32[2,16]{1,0:T(2,128)S(1)} %pad_add_fusion.1.places_ref, ...), custom_call_target="tpu_custom_call" | custom-call | tf_op jit(solution)/shard_map/integrate/pallas_call | solution.py:170
  96.7 0.2 collective-permute-start.4
  96.9 0.4 collective-permute-start.5
  97.4 0.1 fusion.31
  97.5 0.6 gather_fusion
  98.0 0.6 gather_fusion.1
  98.6 0.2 fusion.13
  98.8 2.7 %collective-permute-start.6 = (bf16[4,256,256]{2,1,0:T(8,128)(2,1)}, bf16[4,256,256]{2,1,0:T(8,128)(2,1)S(1)}, u32[]{:S(2)}, u32[]{:S(2)}) collective-permute-start(bf16[4,256,256]{2,1,0:T(8,128)(2,1)} %get-tuple-element.16), channel_id=1, source_target_pairs={{0,6},{1,25},{2,0},{3,27},{4,2},{5,29},{6,4},{7,31},{8,14},{9,1},{... | collective-permute-start | bytes 1572872 | tf_op jit(solution)/shard_map/ppermute | solution.py:302
  101.5 0.0 collective-permute-start.7
  101.5 0.2 collective-permute-start.8
  101.7 13.8 %collective-permute-done.4.refs_1_ = bf16[4,256,256]{2,1,0:T(8,128)(2,1)S(1)} collective-permute-done((bf16[4,256,256]{2,1,0:T(8,128)(2,1)}, bf16[4,256,256]{2,1,0:T(8,128)(2,1)S(1)}, u32[]{:S(2)}, u32[]{:S(2)}) %collective-permute-start.4) | collective-permute-done | bytes 524320 | tf_op jit(solution)/shard_map/ppermute | solution.py:302
  115.5 0.0 collective-permute-start.9
  115.5 0.2 collective-permute-done.5.refs_2_
  115.7 0.0 collective-permute-start.10
  115.7 0.2 compare_reduce_fusion
  115.9 0.0 collective-permute-done.6.refs_3_
  115.9 0.0 collective-permute-done.7.refs_4_
  115.9 2.6 %collective-permute-done.8.refs_5_ = bf16[4,256,256]{2,1,0:T(8,128)(2,1)S(1)} collective-permute-done((bf16[4,256,256]{2,1,0:T(8,128)(2,1)}, bf16[4,256,256]{2,1,0:T(8,128)(2,1)S(1)}, u32[]{:S(2)}, u32[]{:S(2)}) %collective-permute-start.8) | collective-permute-done | bytes 524320 | tf_op jit(solution)/shard_map/ppermute | solution.py:302
  118.6 7.2 %collective-permute-done.9.refs_6_ = bf16[4,256,256]{2,1,0:T(8,128)(2,1)S(1)} collective-permute-done((bf16[4,256,256]{2,1,0:T(8,128)(2,1)}, bf16[4,256,256]{2,1,0:T(8,128)(2,1)S(1)}, u32[]{:S(2)}, u32[]{:S(2)}) %collective-permute-start.9) | collective-permute-done | bytes 524320 | tf_op jit(solution)/shard_map/ppermute | solution.py:302
  125.8 2.5 %collective-permute-done.10.refs_7_ = bf16[4,256,256]{2,1,0:T(8,128)(2,1)S(1)} collective-permute-done((bf16[4,256,256]{2,1,0:T(8,128)(2,1)}, bf16[4,256,256]{2,1,0:T(8,128)(2,1)S(1)}, u32[]{:S(2)}, u32[]{:S(2)}) %collective-permute-start.10) | collective-permute-done | bytes 524320 | tf_op jit(solution)/shard_map/ppermute | solution.py:302
  128.3 1.0 copy-done
  129.4 1.2 add_up.5
  130.6 1.8 %collective-permute-start.11 = (bf16[3,256,256]{2,1,0:T(8,128)(2,1)S(1)}, bf16[3,256,256]{2,1,0:T(8,128)(2,1)S(1)}, u32[]{:S(2)}, u32[]{:S(2)}) collective-permute-start(bf16[3,256,256]{2,1,0:T(8,128)(2,1)S(1)} %add_up.5), channel_id=1, source_target_pairs={{0,16},{1,5},{2,18},{3,7},{4,20},{5,1},{6,22},{7,3},{8,24},{9,13},... | collective-permute-start | bytes 1179656 | tf_op jit(solution)/shard_map/ppermute | solution.py:302
  132.4 1.6 %add_up.6 = bf16[3,256,256]{2,1,0:T(8,128)(2,1)S(1)} custom-call(s32[8]{0:T(128)S(1)} %get-tuple-element.57.targets_ref, bf16[4,256,256]{2,1,0:T(8,128)(2,1)S(1)} %copy-done, bf16[4,256,256]{2,1,0:T(8,128)(2,1)S(1)} %collective-permute-done.4.refs_1_, bf16[4,256,256]{2,1,0:T(8,128)(2,1)S(1)} %collective-permute-done.5.refs_2_, ...), custom_call_target="tpu_custom_call" | custom-call | tf_op jit(solution)/shard_map/add_up/pallas_call | solution.py:212
  134.0 0.1 collective-permute-start.12
  134.1 1.8 %add_up.7 = bf16[3,256,256]{2,1,0:T(8,128)(2,1)S(1)} custom-call(s32[8]{0:T(128)S(1)} %get-tuple-element.56.targets_ref, bf16[4,256,256]{2,1,0:T(8,128)(2,1)S(1)} %copy-done, bf16[4,256,256]{2,1,0:T(8,128)(2,1)S(1)} %collective-permute-done.4.refs_1_, bf16[4,256,256]{2,1,0:T(8,128)(2,1)S(1)} %collective-permute-done.5.refs_2_, ...), custom_call_target="tpu_custom_call" | custom-call | tf_op jit(solution)/shard_map/add_up/pallas_call | solution.py:212
  135.8 3.3 %collective-permute-start.13 = (bf16[3,256,256]{2,1,0:T(8,128)(2,1)S(1)}, bf16[3,256,256]{2,1,0:T(8,128)(2,1)S(1)}, u32[]{:S(2)}, u32[]{:S(2)}) collective-permute-start(bf16[3,256,256]{2,1,0:T(8,128)(2,1)S(1)} %add_up.7), channel_id=1, source_target_pairs={{0,24},{1,7},{2,26},{3,1},{4,28},{5,3},{6,30},{7,5},{8,0},{9,15},{... | collective-permute-start | bytes 1179656 | tf_op jit(solution)/shard_map/ppermute | solution.py:302
  139.1 1.6 %add_up.4 = f32[3,256,256]{2,1,0:T(8,128)S(1)} custom-call(s32[8]{0:T(128)S(1)} %get-tuple-element.58.targets_ref, bf16[4,256,256]{2,1,0:T(8,128)(2,1)S(1)} %copy-done, bf16[4,256,256]{2,1,0:T(8,128)(2,1)S(1)} %collective-permute-done.4.refs_1_, bf16[4,256,256]{2,1,0:T(8,128)(2,1)S(1)} %collective-permute-done.5.refs_2_, ...), custom_call_target="tpu_custom_call" | custom-call | tf_op jit(solution)/shard_map/add_up/pallas_call | solution.py:212
  140.7 0.0 collective-permute-done.11
  140.7 3.6 %collective-permute-done.12 = bf16[3,256,256]{2,1,0:T(8,128)(2,1)S(1)} collective-permute-done((bf16[3,256,256]{2,1,0:T(8,128)(2,1)S(1)}, bf16[3,256,256]{2,1,0:T(8,128)(2,1)S(1)}, u32[]{:S(2)}, u32[]{:S(2)}) %collective-permute-start.12) | collective-permute-done | bytes 393248 | tf_op jit(solution)/shard_map/ppermute | solution.py:302
  144.3 0.1 collective-permute-done.13
  144.4 1.0 convert_add_fusion
  (23 shorter events, 0.3 us)
Async XLA Ops:
  0.9 1.0 copy-start.1
  4.7 7.5 %copy-start.2 = (s32[1,16,256]{2,1,0:T(8,128)S(1)}, s32[1,16,256]{2,1,0:T(8,128)}, u32[]{:S(2)}) copy-start(s32[1,16,256]{2,1,0:T(8,128)} %param.9) | copy-start | bytes 49156
  4.8 7.5 %copy-start.3 = (s32[1,16,256]{2,1,0:T(8,128)S(1)}, s32[1,16,256]{2,1,0:T(8,128)}, u32[]{:S(2)}) copy-start(s32[1,16,256]{2,1,0:T(8,128)} %param.8) | copy-start | bytes 49156
  4.8 60.2 %all-to-all-start = ((bf16[32,256,256]{2,1,0:T(8,128)(2,1)}), bf16[32,256,256]{2,1,0:T(8,128)(2,1)}, u32[]{:S(2)}, u32[]{:S(2)}) async-start(bf16[32,256,256]{2,1,0:T(8,128)(2,1)} %pick_blocks.1), calls=%async_computation | async-start | bytes 8388608 | tf_op jit(solution)/shard_map/all_to_all | solution.py:325
  72.7 4.5 %collective-permute-start = (f32[2,8,16]{2,1,0:T(8,128)S(1)}, f32[2,8,16]{2,1,0:T(8,128)S(1)}, u32[]{:S(2)}, u32[]{:S(2)}) collective-permute-start(f32[2,8,16]{2,1,0:T(8,128)S(1)} %slice.133), channel_id=1, source_target_pairs={{0,32},{32,64},{64,96},{96,128},{128,160},{160,192},{192,224},{224... | collective-permute-start | bytes 3080 | tf_op jit(solution)/shard_map/ppermute | solution.py:240
  76.0 4.9 %collective-permute-start.1 = (f32[2,8,16]{2,1,0:T(8,128)S(1)}, f32[2,8,16]{2,1,0:T(8,128)S(1)}, u32[]{:S(2)}, u32[]{:S(2)}) collective-permute-start(f32[2,8,16]{2,1,0:T(8,128)S(1)} %slice.135), channel_id=1, source_target_pairs={{32,0},{64,32},{96,64},{128,96},{160,128},{192,160},{224,192},{0,2... | collective-permute-start | bytes 3080 | tf_op jit(solution)/shard_map/ppermute | solution.py:241
  80.9 2.1 %collective-permute-start.2 = (f32[12,2,16]{2,1,0:T(2,128)S(1)}, f32[12,2,16]{2,1,0:T(2,128)S(1)}, u32[]{:S(2)}, u32[]{:S(2)}) collective-permute-start(f32[12,2,16]{2,1,0:T(2,128)S(1)} %get-tuple-element.45), channel_id=1, source_target_pairs={{0,1},{1,0},{2,3},{3,2},{4,5},{5,4},{6,7},{7,6},{8,9},{9,8},{10,11... | collective-permute-start | bytes 4616 | tf_op jit(solution)/shard_map/ppermute | solution.py:252
  81.0 6.5 %collective-permute-start.3 = (f32[12,2,16]{2,1,0:T(2,128)S(1)}, f32[12,2,16]{2,1,0:T(2,128)S(1)}, u32[]{:S(2)}, u32[]{:S(2)}) collective-permute-start(f32[12,2,16]{2,1,0:T(2,128)S(1)} %get-tuple-element.46), channel_id=1, source_target_pairs={{0,31},{1,2},{2,1},{3,4},{4,3},{5,6},{6,5},{7,8},{8,7},{9,10},{10,... | collective-permute-start | bytes 4616 | tf_op jit(solution)/shard_map/ppermute | solution.py:251
  96.7 18.8 %collective-permute-start.4 = (bf16[4,256,256]{2,1,0:T(8,128)(2,1)}, bf16[4,256,256]{2,1,0:T(8,128)(2,1)S(1)}, u32[]{:S(2)}, u32[]{:S(2)}) collective-permute-start(bf16[4,256,256]{2,1,0:T(8,128)(2,1)} %get-tuple-element.14), channel_id=1, source_target_pairs={{0,2},{1,9},{2,4},{3,11},{4,6},{5,13},{6,0},{7,15},{8,10},{9,17},{... | collective-permute-start | bytes 1572872 | tf_op jit(solution)/shard_map/ppermute | solution.py:302
  96.9 18.8 %collective-permute-start.5 = (bf16[4,256,256]{2,1,0:T(8,128)(2,1)}, bf16[4,256,256]{2,1,0:T(8,128)(2,1)S(1)}, u32[]{:S(2)}, u32[]{:S(2)}) collective-permute-start(bf16[4,256,256]{2,1,0:T(8,128)(2,1)} %get-tuple-element.15), channel_id=1, source_target_pairs={{0,4},{1,17},{2,6},{3,19},{4,0},{5,21},{6,2},{7,23},{8,12},{9,25},... | collective-permute-start | bytes 1572872 | tf_op jit(solution)/shard_map/ppermute | solution.py:302
  98.8 17.1 %collective-permute-start.6 = (bf16[4,256,256]{2,1,0:T(8,128)(2,1)}, bf16[4,256,256]{2,1,0:T(8,128)(2,1)S(1)}, u32[]{:S(2)}, u32[]{:S(2)}) collective-permute-start(bf16[4,256,256]{2,1,0:T(8,128)(2,1)} %get-tuple-element.16), channel_id=1, source_target_pairs={{0,6},{1,25},{2,0},{3,27},{4,2},{5,29},{6,4},{7,31},{8,14},{9,1},{... | collective-permute-start | bytes 1572872 | tf_op jit(solution)/shard_map/ppermute | solution.py:302
  101.5 14.4 %collective-permute-start.7 = (bf16[4,256,256]{2,1,0:T(8,128)(2,1)}, bf16[4,256,256]{2,1,0:T(8,128)(2,1)S(1)}, u32[]{:S(2)}, u32[]{:S(2)}) collective-permute-start(bf16[4,256,256]{2,1,0:T(8,128)(2,1)} %get-tuple-element.17), channel_id=1, source_target_pairs={{0,1},{1,0},{2,3},{3,2},{4,5},{5,4},{6,7},{7,6},{8,9},{9,8},{10,11... | collective-permute-start | bytes 1572872 | tf_op jit(solution)/shard_map/ppermute | solution.py:302
  101.5 17.1 %collective-permute-start.8 = (bf16[4,256,256]{2,1,0:T(8,128)(2,1)}, bf16[4,256,256]{2,1,0:T(8,128)(2,1)S(1)}, u32[]{:S(2)}, u32[]{:S(2)}) collective-permute-start(bf16[4,256,256]{2,1,0:T(8,128)(2,1)} %get-tuple-element.18), channel_id=1, source_target_pairs={{0,9},{1,2},{2,11},{3,4},{4,13},{5,6},{6,15},{7,0},{8,17},{9,10},{... | collective-permute-start | bytes 1572872 | tf_op jit(solution)/shard_map/ppermute | solution.py:302
  115.5 10.3 %collective-permute-start.9 = (bf16[4,256,256]{2,1,0:T(8,128)(2,1)}, bf16[4,256,256]{2,1,0:T(8,128)(2,1)S(1)}, u32[]{:S(2)}, u32[]{:S(2)}) collective-permute-start(bf16[4,256,256]{2,1,0:T(8,128)(2,1)} %get-tuple-element.19), channel_id=1, source_target_pairs={{0,17},{1,4},{2,19},{3,6},{4,21},{5,0},{6,23},{7,2},{8,25},{9,12},... | collective-permute-start | bytes 1572872 | tf_op jit(solution)/shard_map/ppermute | solution.py:302
  115.7 12.7 %collective-permute-start.10 = (bf16[4,256,256]{2,1,0:T(8,128)(2,1)}, bf16[4,256,256]{2,1,0:T(8,128)(2,1)S(1)}, u32[]{:S(2)}, u32[]{:S(2)}) collective-permute-start(bf16[4,256,256]{2,1,0:T(8,128)(2,1)} %get-tuple-element.20), channel_id=1, source_target_pairs={{0,25},{1,6},{2,27},{3,0},{4,29},{5,2},{6,31},{7,4},{8,1},{9,14},{... | collective-permute-start | bytes 1572872 | tf_op jit(solution)/shard_map/ppermute | solution.py:302
  128.3 1.0 copy-start
  130.6 10.1 %collective-permute-start.11 = (bf16[3,256,256]{2,1,0:T(8,128)(2,1)S(1)}, bf16[3,256,256]{2,1,0:T(8,128)(2,1)S(1)}, u32[]{:S(2)}, u32[]{:S(2)}) collective-permute-start(bf16[3,256,256]{2,1,0:T(8,128)(2,1)S(1)} %add_up.5), channel_id=1, source_target_pairs={{0,16},{1,5},{2,18},{3,7},{4,20},{5,1},{6,22},{7,3},{8,24},{9,13},... | collective-permute-start | bytes 1179656 | tf_op jit(solution)/shard_map/ppermute | solution.py:302
  134.0 10.4 %collective-permute-start.12 = (bf16[3,256,256]{2,1,0:T(8,128)(2,1)S(1)}, bf16[3,256,256]{2,1,0:T(8,128)(2,1)S(1)}, u32[]{:S(2)}, u32[]{:S(2)}) collective-permute-start(bf16[3,256,256]{2,1,0:T(8,128)(2,1)S(1)} %add_up.6), channel_id=1, source_target_pairs={{0,8},{1,3},{2,10},{3,5},{4,12},{5,7},{6,14},{7,1},{8,16},{9,11},{... | collective-permute-start | bytes 1179656 | tf_op jit(solution)/shard_map/ppermute | solution.py:302
  135.8 8.6 %collective-permute-start.13 = (bf16[3,256,256]{2,1,0:T(8,128)(2,1)S(1)}, bf16[3,256,256]{2,1,0:T(8,128)(2,1)S(1)}, u32[]{:S(2)}, u32[]{:S(2)}) collective-permute-start(bf16[3,256,256]{2,1,0:T(8,128)(2,1)S(1)} %add_up.7), channel_id=1, source_target_pairs={{0,24},{1,7},{2,26},{3,1},{4,28},{5,3},{6,30},{7,5},{8,0},{9,15},{... | collective-permute-start | bytes 1179656 | tf_op jit(solution)/shard_map/ppermute | solution.py:302

commit v5 on v4

--- a/solution.py
+++ b/solution.py
@@ -9,6 +9,7 @@
 from jax.sharding import PartitionSpec as P
 
 GRAD_WEIGHT = 0.5
+GATHERS = 4
 BRICK = ("x", "y", "core")
 MIB = 1024 * 1024
 
@@ -22,28 +23,39 @@
     return pltpu.CompilerParams(vmem_limit_bytes=mib * MIB)
 
 
-def pick_blocks(ids, store):
-    count = ids.shape[0]
-
-    def kernel(ids_ref, store_ref, out_ref, sems):
-        copies = [
-            pltpu.make_async_copy(store_ref.at[ids_ref[i]], out_ref.at[i], sems.at[i])
-            for i in range(count)
-        ]
-        for copy in copies:
-            copy.start()
-        for copy in copies:
-            copy.wait()
+def select_blocks(numbers, stores, parts):
+    inner = len(stores)
+    block = stores[0].shape[1:]
+
+    def kernel(numbers_ref, *refs):
+        ins, outs, sems = refs[:inner], refs[inner:-1], refs[-1]
+        places = [(p, d) for p in range(parts) for d in range(inner)]
+
+        def copy(p, d):
+            number = jnp.maximum(numbers_ref[p, d], 0)
+            return pltpu.make_async_copy(ins[d].at[number], outs[p].at[d], sems.at[p, d])
+
+        for p, d in places:
+
+            @pl.when(numbers_ref[p, d] >= 0)
+            def _():
+                copy(p, d).start()
+
+        for p, d in places:
+
+            @pl.when(numbers_ref[p, d] >= 0)
+            def _():
+                copy(p, d).wait()
 
     return pl.pallas_call(
         kernel,
-        out_shape=pltpu.HBM((count,) + store.shape[1:], store.dtype),
-        in_specs=[SCALARS, RESIDENT],
-        out_specs=IN_HBM,
-        scratch_shapes=[pltpu.SemaphoreType.DMA((count,))],
+        out_shape=[pltpu.HBM((inner,) + block, stores[0].dtype)] * parts,
+        in_specs=[SCALARS] + [IN_HBM] * inner,
+        out_specs=[IN_HBM] * parts,
+        scratch_shapes=[pltpu.SemaphoreType.DMA((parts, inner))],
         compiler_params=params(4),
-        name="pick_blocks",
-    )(ids, store)
+        name="select_blocks",
+    )(numbers, *stores)
 
 
 def gather_tables(index, table):
@@ -87,25 +99,37 @@
     )(index, table)
 
 
-def collocate(slots, blocks, tables):
-    count, both, points = tables.shape
+def collocate(places, blocks, tables):
+    each, both, points = tables[0].shape
+    count = each * len(tables)
     width = both // 2
-
-    def kernel(slots_ref, blocks_ref, tables_ref, out_ref, held, kept, sems):
-        def fetch(j):
-            return (
-                pltpu.make_async_copy(blocks_ref.at[slots_ref[j]], held.at[j], sems.at[0, j]),
-                pltpu.make_async_copy(tables_ref.at[j], kept.at[j], sems.at[1, j]),
+    parts = len(blocks)
+
+    def kernel(places_ref, *refs):
+        blocks_refs, tables_refs = refs[:parts], refs[parts:-4]
+        out_ref, held, kept, sems = refs[-4:]
+
+        def fetch_block(j, part):
+            return pltpu.make_async_copy(
+                blocks_refs[part].at[places_ref[1, j]], held.at[j], sems.at[0, j]
             )
 
+        def fetch_table(j, ref, place):
+            return pltpu.make_async_copy(ref.at[place], kept.at[j], sems.at[1, j])
+
         for j in range(count):
-            for copy in fetch(j):
-                copy.start()
+            for part in range(parts):
+
+                @pl.when(places_ref[0, j] == part)
+                def _():
+                    fetch_block(j, part).start()
+
+            fetch_table(j, tables_refs[j // each], j % each).start()
         out_ref[...] = jnp.zeros_like(out_ref)
 
         def body(j, carry):
-            for copy in fetch(j):
-                copy.wait()
+            fetch_block(j, 0).wait()
+            fetch_table(j, tables_refs[0], 0).wait()
             product = jnp.dot(held[j], kept[j, width:, :], preferred_element_type=jnp.float32)
             term = kept[j, :width, :].astype(jnp.float32) * product
             out_ref[...] += jnp.sum(term.reshape(width // 8, 8, points), axis=0)
@@ -116,36 +140,38 @@
     return pl.pallas_call(
         kernel,
         out_shape=jax.ShapeDtypeStruct((8, points), jnp.float32),
-        in_specs=[SCALARS, IN_HBM, IN_HBM],
+        in_specs=[SCALARS] + [IN_HBM] * (parts + len(tables)),
         out_specs=RESIDENT,
         scratch_shapes=[
             pltpu.VMEM((count, width, width), jnp.bfloat16),
-            pltpu.VMEM(tables.shape, tables.dtype),
+            pltpu.VMEM((count, both, points), jnp.bfloat16),
             pltpu.SemaphoreType.DMA((2, count)),
         ],
         compiler_params=params(52),
         name="collocate",
-    )(slots, blocks, tables)
+    )(places, *blocks, *tables)
 
 
 def integrate(places, scaled, tables, parts, inner):
-    count, both, points = tables.shape
+    each, both, points = tables[0].shape
+    count = each * len(tables)
     width = both // 2
 
-    def kernel(places_ref, scaled_ref, tables_ref, *rest):
-        outs, (held, kept, sems) = rest[:parts], rest[parts:]
-
-        def fetch(j):
-            return pltpu.make_async_copy(tables_ref.at[j], kept.at[j], sems.at[0, j])
+    def kernel(places_ref, scaled_ref, *refs):
+        tables_refs, outs = refs[: len(tables)], refs[len(tables) : -3]
+        held, kept, sems = refs[-3:]
+
+        def fetch(j, ref, place):
+            return pltpu.make_async_copy(ref.at[place], kept.at[j], sems.at[0, j])
 
         def leave(j, part):
             return pltpu.make_async_copy(held.at[j], outs[part].at[places_ref[1, j]], sems.at[1, j])
 
         for j in range(count):
-            fetch(j).start()
+            fetch(j, tables_refs[j // each], j % each).start()
 
         def body(j, carry):
-            fetch(j).wait()
+            fetch(j, tables_refs[0], 0).wait()
             weighted = (kept[j, width:, :].astype(jnp.float32) * scaled_ref[...]).astype(
                 jnp.bfloat16
             )
@@ -170,16 +196,16 @@
     return pl.pallas_call(
         kernel,
         out_shape=[pltpu.HBM((inner, width, width), jnp.bfloat16)] * parts,
-        in_specs=[SCALARS, RESIDENT, IN_HBM],
+        in_specs=[SCALARS, RESIDENT] + [IN_HBM] * len(tables),
         out_specs=[IN_HBM] * parts,
         scratch_shapes=[
             pltpu.VMEM((count, width, width), jnp.bfloat16),
-            pltpu.VMEM(tables.shape, tables.dtype),
+            pltpu.VMEM((count, both, points), jnp.bfloat16),
             pltpu.SemaphoreType.DMA((2, count)),
         ],
         compiler_params=params(52),
         name="integrate",
-    )(places, scaled, tables)
+    )(places, scaled, *tables)
 
 
 def add_up(targets, parts, place, own_count, dtype):
@@ -289,17 +315,20 @@
     return math.prod(lax.axis_size(axis) for axis in axes)
 
 
-def moved(value, stage, step, other=False):
+def moved(value, step, other, along):
     nx, ny, nc = (lax.axis_size(axis) for axis in BRICK)
     pairs = []
     for x in range(nx):
         for y in range(ny):
             for c in range(nc):
                 core = (c + 1) % nc if other else c
-                along_y = (core == 0) == (stage == 1)
-                to_x, to_y = (x, (y + step) % ny) if along_y else ((x + step) % nx, y)
+                to_x, to_y = (x, (y + step) % ny) if along(c, core) else ((x + step) % nx, y)
                 pairs.append(((x * ny + y) * nc + c, (to_x * ny + to_y) * nc + core))
     return lax.ppermute(value, BRICK, pairs)
+
+
+def order(side):
+    return [side // 2] + [k for k in range(side) if k not in (side // 2, 0)]
 
 
 def find(owners, ids, bricks, wanted):
@@ -317,41 +346,54 @@
     points = size_x * size_y * size_z
     owners = crossing // own_count
     ids = crossing % own_count
-    chosen = owners == position
-    send_ids = jnp.sum(jnp.where(chosen, ids, 0), axis=-1)
     slots = lax.dynamic_index_in_dim(owners, position, 0, keepdims=False)
-
-    sending = pick_blocks(send_ids, store)
-    blocks = lax.all_to_all(sending, BRICK, split_axis=0, concat_axis=0, tiled=True)
+    side = nx
+    steps = jnp.arange(side)
+
+    stores = [store] + [None] * (side - 1)
+    for step in order(side):
+        stores[step] = moved(store, step, False, lambda c, to: c == 1)
     table = phi.reshape(points, functions).T
     index = jnp.concatenate([rows_index[0], cols_index[0]], axis=1)[:, None, :]
-    tables = gather_tables(index, table)
-    density = jnp.sum(collocate(slots, blocks, tables), axis=0).reshape(size_x, size_y, size_z)
+    each = index.shape[0] // GATHERS
+    tables = [gather_tables(index[i : i + each], table) for i in range(0, index.shape[0], each)]
+    ahead = jnp.where(c == 0, x * ny + (y + steps) % ny, ((x + steps) % nx) * ny + y) * nc
+    served = jnp.concatenate([ahead + c, ahead + (1 - c)])
+    source = jnp.where(c == 0, ((x - steps) % nx) * ny + y, x * ny + (y - steps) % ny) * nc + c
+    blocks = list(select_blocks(find(owners, ids, served, source), stores, 2 * side))
+    for step in order(side) + [0]:
+        for other in (0, 1):
+            if step or other:
+                i = other * side + step
+                blocks[i] = moved(blocks[i], step, bool(other), lambda c, to: c == 0)
+    to_x, rest = slots // (ny * nc), slots % (ny * nc)
+    to_y, to_c = rest // nc, rest % nc
+    behind_x, behind_y = (x - to_x) % nx, (y - to_y) % ny
+    last = jnp.where(to_c == 0, behind_y, behind_x) + jnp.where(to_c == c, 0, side)
+    places = jnp.stack([last, jnp.where(to_c == 0, behind_x, behind_y)]).astype(jnp.int32)
+    layers = collocate(places, blocks, tables)
+    density = jnp.sum(layers, axis=0).reshape(size_x, size_y, size_z)
     padded = extended_pairs(extended_ring(density, "grp", 0, 2), BRICK, 1, 2)
     scaled = potential_of(padded).reshape(1, points) * (1.0 / math.sqrt(points))
 
-    to_x, rest = slots // (ny * nc), slots % (ny * nc)
-    to_y, to_c = rest // nc, rest % nc
     ahead_x, ahead_y = (to_x - x) % nx, (to_y - y) % ny
-    side = nx
     first = jnp.where(to_c == 0, ahead_y, ahead_x)
     second = jnp.where(to_c == 0, ahead_x, ahead_y)
     places = jnp.stack([first + jnp.where(to_c == c, 0, side), second]).astype(jnp.int32)
     parts = list(integrate(places, scaled, tables, 2 * side, side))
-    for step in [side // 2] + [k for k in range(side) if k not in (side // 2, 0)] + [0]:
+    for step in order(side) + [0]:
         for other in (0, 1):
             if step or other:
                 i = other * side + step
-                parts[i] = moved(parts[i], 1, step, bool(other))
-    steps = jnp.arange(side)
+                parts[i] = moved(parts[i], step, bool(other), lambda c, to: to == 0)
     behind = jnp.where(c == 0, x * ny + (y - steps) % ny, ((x - steps) % nx) * ny + y) * nc
     sources = jnp.concatenate([behind + c, behind + (1 - c)])
     wanted = jnp.where(c == 0, ((x + steps) % nx) * ny + y, x * ny + (y + steps) % ny) * nc + c
     targets = find(owners, ids, sources, wanted)
     total = []
-    for step in [side // 2] + [k for k in range(side) if k not in (side // 2, 0)]:
+    for step in order(side):
         summed = add_up(targets[:, step], parts, step, own_count, jnp.bfloat16)
-        total.append(moved(summed, 2, step))
+        total.append(moved(summed, step, False, lambda c, to: c == 1))
     own = add_up(targets[:, 0], parts, 0, own_count, jnp.float32)
     for piece in total:
         own = own + piece.astype(jnp.float32)

time: 147 us -> 140 us (0.952); the launches traced: 145 us -> 140 us
  waiting for transfers between devices: 67.2 us -> 52.4 us
  Pallas kernels: 46.9 us -> 52.2 us
  starting transfers between devices: 21.4 us -> 23.7 us
    all_to_all x1 -> x0, waiting for transfers between devices: 27.7 us -> none  [local(): lax.all_to_all(sending, BRICK, split_axis=0, concat_axis=0, tiled=True)]
    ppermute x10 -> x20, waiting for transfers between devices: 30.1 us -> 42 us  [moved(): return lax.ppermute(value, BRICK, pairs)]
    ppermute x10 -> x20, starting transfers between devices: 8.78 us -> 19.2 us  [moved(): return lax.ppermute(value, BRICK, pairs)]
    all_to_all x1 -> x0, starting transfers between devices: 7.46 us -> none  [local(): lax.all_to_all(sending, BRICK, split_axis=0, concat_axis=0, tiled=True)]
    pallas_call x1 -> x4, Pallas kernels: 22.1 us -> 25.1 us  [gather_tables(): pl.pallas_call(kernel, out_shape=pltpu.HBM((count, width, points), jnp.bf...]
    pallas_call x4, Pallas kernels: 6.12 us -> 8.81 us  [add_up(): pl.pallas_call(kernel, out_shape=jax.ShapeDtypeStruct((own_count, rows, c...]
  transfers between devices with their start and end apart: 15 -> 24, of which waited for: 11 -> 12; matrix products, arithmetic and copies ran while one was open for 3% -> 6% of each run, Pallas kernels for 19% -> 22%
where the time goes in v5:
time: 140 us
  waiting for transfers between devices  52.4 us (37%)
  Pallas kernels  52.2 us (37%)
  starting transfers between devices  23.7 us (17%)
  local copies, waits for them, and re-layouts  8.21 us (6%)
  other arithmetic  3.4 us (2%)
    ppermute x20, waiting for transfers between devices, moved(): return lax.ppermute(value, BRICK, pairs)  42 us
    pallas_call x4, Pallas kernels, gather_tables(): pl.pallas_call(kernel, out_shape=pltpu.HBM((count, width, points), jnp.bf...  25.1 us
    ppermute x20, starting transfers between devices, moved(): return lax.ppermute(value, BRICK, pairs)  19.2 us
    pallas_call x4, Pallas kernels, add_up(): pl.pallas_call(kernel, out_shape=jax.ShapeDtypeStruct((own_count, rows, c...  8.81 us
    pallas_call x1, Pallas kernels, integrate(): pl.pallas_call(kernel, out_shape=[pltpu.HBM((inner, width, width), jnp.bf...  8.35 us
    pallas_call x1, Pallas kernels, collocate(): pl.pallas_call(kernel, out_shape=jax.ShapeDtypeStruct((8, points), jnp.fl...  7.62 us
    ppermute x1, waiting for transfers between devices, extended_pairs(): far = lax.ppermute(jnp.where(odd, high, low), axis, between)  5.36 us
    ppermute x1, waiting for transfers between devices, extended_ring(): above = lax.ppermute(low, axis, backward)  3.65 us
  transfers between devices with their start and end apart: 24, of which 12 were waited for; matrix products, arithmetic and copies ran while one was open for 6% of the time, Pallas kernels for 22%

profile of v5, /device:TPU:96, one launch (start us, length us, event | category | flops | bytes accessed | tf_op | source)
XLA Modules:
  0.0 140.2 jit_solution(18161356079163982473)
XLA Ops:
  0.0 3.0 %collective-permute-start.1 = (bf16[3,256,256]{2,1,0:T(8,128)(2,1)}, bf16[3,256,256]{2,1,0:T(8,128)(2,1)S(1)}, u32[]{:S(2)}, u32[]{:S(2)}) collective-permute-start(bf16[3,256,256]{2,1,0:T(8,128)(2,1)} %refs_0_.1), channel_id=1, source_target_pairs={{0,16},{1,5},{2,18},{3,7},{4,20},{5,1},{6,22},{7,3},{8,24},{9,13},... | collective-permute-start | bytes 1179656 | tf_op jit(solution)/shard_map/ppermute | solution.py:327
  3.0 0.6 collective-permute-start
  3.6 2.6 %collective-permute-start.2 = (bf16[3,256,256]{2,1,0:T(8,128)(2,1)}, bf16[3,256,256]{2,1,0:T(8,128)(2,1)S(1)}, u32[]{:S(2)}, u32[]{:S(2)}) collective-permute-start(bf16[3,256,256]{2,1,0:T(8,128)(2,1)} %refs_0_.1), channel_id=1, source_target_pairs={{0,24},{1,7},{2,26},{3,1},{4,28},{5,3},{6,30},{7,5},{8,0},{9,15},{... | collective-permute-start | bytes 1179656 | tf_op jit(solution)/shard_map/ppermute | solution.py:327
  6.4 0.8 copy.20
  7.2 0.6 gather_fusion.2
  7.8 0.6 gather_fusion.3
  8.4 0.2 compare_reduce_fusion
  8.6 0.2 fusion.14
  8.8 0.1 copy.25
  8.9 0.1 copy.26
  9.0 0.8 pad_add_fusion
  9.9 2.9 %copy.27 = bf16[1024,1024]{0,1:T(8,128)(2,1)S(1)} copy(bf16[1024,1024]{1,0:T(8,128)(2,1)} %bitcast.30) | data formatting | bytes 4194304 | tf_op jit(solution)/shard_map/reshape | solution.py:356
  12.7 6.3 %gather_tables.7.refs_11_.refs_3_ = bf16[4,512,1024]{2,1,0:T(8,128)(2,1)} custom-call(s32[4,1,512]{2,1,0:T(1,128)S(1)} %slice.163.index_ref, bf16[1024,1024]{1,0:T(8,128)(2,1)S(1)} %bitcast.26), custom_call_target="tpu_custom_call" | custom-call | flops 4294967296 | bytes 4194304 | tf_op jit(solution)/shard_map/gather_tables/pallas_call | solution.py:83
  19.1 6.2 %gather_tables.6.refs_10_.refs_2_ = bf16[4,512,1024]{2,1,0:T(8,128)(2,1)} custom-call(s32[4,1,512]{2,1,0:T(1,128)S(1)} %copy.30.index_ref, bf16[1024,1024]{1,0:T(8,128)(2,1)S(1)} %bitcast.27), custom_call_target="tpu_custom_call" | custom-call | flops 4294967296 | bytes 4194304 | tf_op jit(solution)/shard_map/gather_tables/pallas_call | solution.py:83
  25.3 2.4 %select_blocks.1 = (bf16[4,256,256]{2,1,0:T(8,128)(2,1)}, bf16[4,256,256]{2,1,0:T(8,128)(2,1)}, bf16[4,256,256]{2,1,0:T(8,128)(2,1)}, bf16[4,256,256]{2,1,0:T(8,...) custom-call(s32[8,4]{1,0:T(8,128)S(1)} %broadcast_select_fusion.4.nu, ...), custom_call_target="tpu_custom_call" | custom-call | tf_op jit(solution)/shard_map/select_blocks/pallas_call | solution.py:50
  27.7 1.5 %collective-permute-start.3 = (bf16[4,256,256]{2,1,0:T(8,128)(2,1)}, bf16[4,256,256]{2,1,0:T(8,128)(2,1)S(1)}, u32[]{:S(2)}, u32[]{:S(2)}) collective-permute-start(bf16[4,256,256]{2,1,0:T(8,128)(2,1)} %get-tuple-element.22), channel_id=1, source_target_pairs={{0,2},{1,9},{2,4},{3,11},{4,6},{5,13},{6,0},{7,15},{8,10},{9,17},{... | collective-permute-start | bytes 1572872 | tf_op jit(solution)/shard_map/ppermute | solution.py:327
  29.2 2.8 %collective-permute-start.4 = (bf16[4,256,256]{2,1,0:T(8,128)(2,1)}, bf16[4,256,256]{2,1,0:T(8,128)(2,1)S(1)}, u32[]{:S(2)}, u32[]{:S(2)}) collective-permute-start(bf16[4,256,256]{2,1,0:T(8,128)(2,1)} %get-tuple-element.23), channel_id=1, source_target_pairs={{0,4},{1,17},{2,6},{3,19},{4,0},{5,21},{6,2},{7,23},{8,12},{9,25},... | collective-permute-start | bytes 1572872 | tf_op jit(solution)/shard_map/ppermute | solution.py:327
  32.0 6.3 %gather_tables.5.refs_9_.refs_1_ = bf16[4,512,1024]{2,1,0:T(8,128)(2,1)} custom-call(s32[4,1,512]{2,1,0:T(1,128)S(1)} %copy.29.index_ref, bf16[1024,1024]{1,0:T(8,128)(2,1)S(1)} %bitcast.28), custom_call_target="tpu_custom_call" | custom-call | flops 4294967296 | bytes 4194304 | tf_op jit(solution)/shard_map/gather_tables/pallas_call | solution.py:83
  38.3 1.3 collective-permute-start.5
  39.6 0.9 collective-permute-start.7
  40.4 4.6 %collective-permute-done.4.refs_2_ = bf16[4,256,256]{2,1,0:T(8,128)(2,1)S(1)} collective-permute-done((bf16[4,256,256]{2,1,0:T(8,128)(2,1)}, bf16[4,256,256]{2,1,0:T(8,128)(2,1)S(1)}, u32[]{:S(2)}, u32[]{:S(2)}) %collective-permute-start.4) | collective-permute-done | bytes 524320 | tf_op jit(solution)/shard_map/ppermute | solution.py:327
  45.1 6.2 %gather_tables.4.refs_8_.refs_0_ = bf16[4,512,1024]{2,1,0:T(8,128)(2,1)} custom-call(s32[4,1,512]{2,1,0:T(1,128)S(1)} %copy.28.index_ref, bf16[1024,1024]{1,0:T(8,128)(2,1)S(1)} %bitcast.29), custom_call_target="tpu_custom_call" | custom-call | flops 4294967296 | bytes 4194304 | tf_op jit(solution)/shard_map/gather_tables/pallas_call | solution.py:83
  51.3 4.0 %collective-permute-done.7.refs_5_ = bf16[4,256,256]{2,1,0:T(8,128)(2,1)} collective-permute-done((bf16[4,256,256]{2,1,0:T(8,128)(2,1)}, bf16[4,256,256]{2,1,0:T(8,128)(2,1)}, u32[]{:S(2)}, u32[]{:S(2)}) %collective-permute-start.7) | collective-permute-done | bytes 524320 | tf_op jit(solution)/shard_map/ppermute | solution.py:327
  55.3 2.5 %collective-permute-done.9.refs_7_ = bf16[4,256,256]{2,1,0:T(8,128)(2,1)} collective-permute-done((bf16[4,256,256]{2,1,0:T(8,128)(2,1)}, bf16[4,256,256]{2,1,0:T(8,128)(2,1)}, u32[]{:S(2)}, u32[]{:S(2)}) %collective-permute-start.9) | collective-permute-done | bytes 524320 | tf_op jit(solution)/shard_map/ppermute | solution.py:327
  57.8 7.6 %collocate.1 = f32[8,1024]{1,0:T(8,128)S(1)} custom-call(s32[2,16]{1,0:T(2,128)S(1)} %pad_add_fusion.2.places_ref, bf16[4,256,256]{2,1,0:T(8,128)(2,1)S(1)} %copy-done.1, bf16[4,256,256]{2,1,0:T(8,128)(2,1)S(1)} %collective-permute-done.3.refs_1_, bf16[4,256,256]{2,1,0:T(8,128)(2,1)S(1)} %collective-permute-done.4.refs_2_, ...), custom_call_target="tpu_custom_call" | custom-call | tf_op jit(solution)/shard_map/collocate/pallas_call | solution.py:140
  65.5 0.1 slice.165
  65.6 3.4 %collective-permute-start.10 = (f32[2,8,16]{2,1,0:T(8,128)S(1)}, f32[2,8,16]{2,1,0:T(8,128)S(1)}, u32[]{:S(2)}, u32[]{:S(2)}) collective-permute-start(f32[2,8,16]{2,1,0:T(8,128)S(1)} %slice.165), channel_id=1, source_target_pairs={{0,32},{32,64},{64,96},{96,128},{128,160},{160,192},{192,224},{224... | collective-permute-start | bytes 3080 | tf_op jit(solution)/shard_map/ppermute | solution.py:266
  69.2 1.2 collective-permute-done.10
  70.4 3.7 %collective-permute-done.11 = f32[2,8,16]{2,1,0:T(8,128)S(1)} collective-permute-done((f32[2,8,16]{2,1,0:T(8,128)S(1)}, f32[2,8,16]{2,1,0:T(8,128)S(1)}, u32[]{:S(2)}, u32[]{:S(2)}) %collective-permute-start.11) | collective-permute-done | bytes 1056 | tf_op jit(solution)/shard_map/ppermute | solution.py:267
  74.0 0.1 collective-permute-start.12
  74.1 1.0 collective-permute-start.13
  75.1 0.2 collective-permute-done.12
  75.3 5.4 %collective-permute-done.13 = f32[12,2,16]{2,1,0:T(2,128)S(1)} collective-permute-done((f32[12,2,16]{2,1,0:T(2,128)S(1)}, f32[12,2,16]{2,1,0:T(2,128)S(1)}, u32[]{:S(2)}, u32[]{:S(2)}) %collective-permute-start.13) | collective-permute-done | bytes 1568 | tf_op jit(solution)/shard_map/ppermute | solution.py:277
  80.7 0.1 fusion.50
  80.8 0.1 fusion.51
  80.9 0.1 fusion.46
  81.3 0.1 fusion.9
  81.4 0.1 mul.244.scaled_ref
  81.5 8.3 %integrate.1 = (bf16[4,256,256]{2,1,0:T(8,128)(2,1)}, bf16[4,256,256]{2,1,0:T(8,128)(2,1)}, bf16[4,256,256]{2,1,0:T(8,128)(2,1)}, bf16[4,256,256]{2,1,0:T(8,128)...) custom-call(s32[2,16]{1,0:T(2,128)S(1)} %pad_add_fusion.1.places_ref, ...), custom_call_target="tpu_custom_call" | custom-call | tf_op jit(solution)/shard_map/integrate/pallas_call | solution.py:196
  89.8 0.1 collective-permute-start.14
  89.9 0.1 collective-permute-start.15
  90.1 0.1 fusion.42
  90.2 0.6 gather_fusion
  90.7 0.6 gather_fusion.1
  91.3 3.2 %collective-permute-start.16 = (bf16[4,256,256]{2,1,0:T(8,128)(2,1)}, bf16[4,256,256]{2,1,0:T(8,128)(2,1)S(1)}, u32[]{:S(2)}, u32[]{:S(2)}) collective-permute-start(bf16[4,256,256]{2,1,0:T(8,128)(2,1)} %get-tuple-element.32), channel_id=1, source_target_pairs={{0,6},{1,25},{2,0},{3,27},{4,2},{5,29},{6,4},{7,31},{8,14},{9,1},{... | collective-permute-start | bytes 1572872 | tf_op jit(solution)/shard_map/ppermute | solution.py:327
  94.4 14.6 %collective-permute-done.14.refs_1_ = bf16[4,256,256]{2,1,0:T(8,128)(2,1)S(1)} collective-permute-done((bf16[4,256,256]{2,1,0:T(8,128)(2,1)}, bf16[4,256,256]{2,1,0:T(8,128)(2,1)S(1)}, u32[]{:S(2)}, u32[]{:S(2)}) %collective-permute-start.14) | collective-permute-done | bytes 524320 | tf_op jit(solution)/shard_map/ppermute | solution.py:327
  109.0 0.2 compare_reduce_fusion.1
  109.3 0.1 copy.23
  109.4 0.2 fusion.13
  109.6 0.1 copy.24
  109.7 0.2 slice_reduce_fusion.2
  109.9 1.8 %collective-permute-done.18.refs_5_ = bf16[4,256,256]{2,1,0:T(8,128)(2,1)S(1)} collective-permute-done((bf16[4,256,256]{2,1,0:T(8,128)(2,1)}, bf16[4,256,256]{2,1,0:T(8,128)(2,1)S(1)}, u32[]{:S(2)}, u32[]{:S(2)}) %collective-permute-start.18) | collective-permute-done | bytes 524320 | tf_op jit(solution)/shard_map/ppermute | solution.py:327
  111.7 7.6 %collective-permute-done.19.refs_6_ = bf16[4,256,256]{2,1,0:T(8,128)(2,1)S(1)} collective-permute-done((bf16[4,256,256]{2,1,0:T(8,128)(2,1)}, bf16[4,256,256]{2,1,0:T(8,128)(2,1)S(1)}, u32[]{:S(2)}, u32[]{:S(2)}) %collective-permute-start.19) | collective-permute-done | bytes 524320 | tf_op jit(solution)/shard_map/ppermute | solution.py:327
  119.3 2.7 %collective-permute-done.20.refs_7_ = bf16[4,256,256]{2,1,0:T(8,128)(2,1)} collective-permute-done((bf16[4,256,256]{2,1,0:T(8,128)(2,1)}, bf16[4,256,256]{2,1,0:T(8,128)(2,1)}, u32[]{:S(2)}, u32[]{:S(2)}) %collective-permute-start.20) | collective-permute-done | bytes 524320 | tf_op jit(solution)/shard_map/ppermute | solution.py:327
  122.1 1.0 copy-done
  123.1 2.5 %add_up.5 = bf16[3,256,256]{2,1,0:T(8,128)(2,1)S(1)} custom-call(s32[8]{0:T(128)S(1)} %get-tuple-element.37.targets_ref, bf16[4,256,256]{2,1,0:T(8,128)(2,1)S(1)} %copy-done, bf16[4,256,256]{2,1,0:T(8,128)(2,1)S(1)} %collective-permute-done.14.refs_1_, bf16[4,256,256]{2,1,0:T(8,128)(2,1)S(1)} %collective-permute-done.15.refs_2_, ...), custom_call_target="tpu_custom_call" | custom-call | tf_op jit(solution)/shard_map/add_up/pallas_call | solution.py:238
  125.6 0.1 collective-permute-start.21
  125.7 2.8 %add_up.6 = bf16[3,256,256]{2,1,0:T(8,128)(2,1)S(1)} custom-call(s32[8]{0:T(128)S(1)} %get-tuple-element.39.targets_ref, bf16[4,256,256]{2,1,0:T(8,128)(2,1)S(1)} %copy-done, bf16[4,256,256]{2,1,0:T(8,128)(2,1)S(1)} %collective-permute-done.14.refs_1_, bf16[4,256,256]{2,1,0:T(8,128)(2,1)S(1)} %collective-permute-done.15.refs_2_, ...), custom_call_target="tpu_custom_call" | custom-call | tf_op jit(solution)/shard_map/add_up/pallas_call | solution.py:238
  128.5 0.1 collective-permute-start.22
  128.6 1.4 add_up.7
  130.0 2.9 %collective-permute-start.23 = (bf16[3,256,256]{2,1,0:T(8,128)(2,1)S(1)}, bf16[3,256,256]{2,1,0:T(8,128)(2,1)S(1)}, u32[]{:S(2)}, u32[]{:S(2)}) collective-permute-start(bf16[3,256,256]{2,1,0:T(8,128)(2,1)S(1)} %add_up.7), channel_id=1, source_target_pairs={{0,24},{1,7},{2,26},{3,1},{4,28},{5,3},{6,30},{7,5},{8,0},{9,15},{... | collective-permute-start | bytes 1179656 | tf_op jit(solution)/shard_map/ppermute | solution.py:327
  132.9 2.1 %add_up.4 = f32[3,256,256]{2,1,0:T(8,128)S(1)} custom-call(s32[8]{0:T(128)S(1)} %get-tuple-element.40.targets_ref, bf16[4,256,256]{2,1,0:T(8,128)(2,1)S(1)} %copy-done, bf16[4,256,256]{2,1,0:T(8,128)(2,1)S(1)} %collective-permute-done.14.refs_1_, bf16[4,256,256]{2,1,0:T(8,128)(2,1)S(1)} %collective-permute-done.15.refs_2_, ...), custom_call_target="tpu_custom_call" | custom-call | tf_op jit(solution)/shard_map/add_up/pallas_call | solution.py:238
  135.1 4.1 %collective-permute-done.22 = bf16[3,256,256]{2,1,0:T(8,128)(2,1)S(1)} collective-permute-done((bf16[3,256,256]{2,1,0:T(8,128)(2,1)S(1)}, bf16[3,256,256]{2,1,0:T(8,128)(2,1)S(1)}, u32[]{:S(2)}, u32[]{:S(2)}) %collective-permute-start.22) | collective-permute-done | bytes 393248 | tf_op jit(solution)/shard_map/ppermute | solution.py:327
  139.2 1.0 convert_add_fusion
  (60 shorter events, 0.8 us)
Async XLA Ops:
  0.0 25.3 %collective-permute-start.1 = (bf16[3,256,256]{2,1,0:T(8,128)(2,1)}, bf16[3,256,256]{2,1,0:T(8,128)(2,1)S(1)}, u32[]{:S(2)}, u32[]{:S(2)}) collective-permute-start(bf16[3,256,256]{2,1,0:T(8,128)(2,1)} %refs_0_.1), channel_id=1, source_target_pairs={{0,16},{1,5},{2,18},{3,7},{4,20},{5,1},{6,22},{7,3},{8,24},{9,13},... | collective-permute-start | bytes 1179656 | tf_op jit(solution)/shard_map/ppermute | solution.py:327
  3.0 22.3 %collective-permute-start = (bf16[3,256,256]{2,1,0:T(8,128)(2,1)}, bf16[3,256,256]{2,1,0:T(8,128)(2,1)S(1)}, u32[]{:S(2)}, u32[]{:S(2)}) collective-permute-start(bf16[3,256,256]{2,1,0:T(8,128)(2,1)} %refs_0_.1), channel_id=1, source_target_pairs={{0,8},{1,3},{2,10},{3,5},{4,12},{5,7},{6,14},{7,1},{8,16},{9,11},{... | collective-permute-start | bytes 1179656 | tf_op jit(solution)/shard_map/ppermute | solution.py:327
  3.6 21.7 %collective-permute-start.2 = (bf16[3,256,256]{2,1,0:T(8,128)(2,1)}, bf16[3,256,256]{2,1,0:T(8,128)(2,1)S(1)}, u32[]{:S(2)}, u32[]{:S(2)}) collective-permute-start(bf16[3,256,256]{2,1,0:T(8,128)(2,1)} %refs_0_.1), channel_id=1, source_target_pairs={{0,24},{1,7},{2,26},{3,1},{4,28},{5,3},{6,30},{7,5},{8,0},{9,15},{... | collective-permute-start | bytes 1179656 | tf_op jit(solution)/shard_map/ppermute | solution.py:327
  19.1 6.2 %copy-start.2 = (bf16[3,256,256]{2,1,0:T(8,128)(2,1)S(1)}, bf16[3,256,256]{2,1,0:T(8,128)(2,1)}, u32[]{:S(2)}) copy-start(bf16[3,256,256]{2,1,0:T(8,128)(2,1)} %refs_0_.1) | copy-start | bytes 1179652
  27.7 12.7 %collective-permute-start.3 = (bf16[4,256,256]{2,1,0:T(8,128)(2,1)}, bf16[4,256,256]{2,1,0:T(8,128)(2,1)S(1)}, u32[]{:S(2)}, u32[]{:S(2)}) collective-permute-start(bf16[4,256,256]{2,1,0:T(8,128)(2,1)} %get-tuple-element.22), channel_id=1, source_target_pairs={{0,2},{1,9},{2,4},{3,11},{4,6},{5,13},{6,0},{7,15},{8,10},{9,17},{... | collective-permute-start | bytes 1572872 | tf_op jit(solution)/shard_map/ppermute | solution.py:327
  29.2 15.8 %collective-permute-start.4 = (bf16[4,256,256]{2,1,0:T(8,128)(2,1)}, bf16[4,256,256]{2,1,0:T(8,128)(2,1)S(1)}, u32[]{:S(2)}, u32[]{:S(2)}) collective-permute-start(bf16[4,256,256]{2,1,0:T(8,128)(2,1)} %get-tuple-element.23), channel_id=1, source_target_pairs={{0,4},{1,17},{2,6},{3,19},{4,0},{5,21},{6,2},{7,23},{8,12},{9,25},... | collective-permute-start | bytes 1572872 | tf_op jit(solution)/shard_map/ppermute | solution.py:327
  38.3 13.0 %collective-permute-start.5 = (bf16[4,256,256]{2,1,0:T(8,128)(2,1)}, bf16[4,256,256]{2,1,0:T(8,128)(2,1)}, u32[]{:S(2)}, u32[]{:S(2)}) collective-permute-start(bf16[4,256,256]{2,1,0:T(8,128)(2,1)} %get-tuple-element.24), channel_id=1, source_target_pairs={{0,6},{1,25},{2,0},{3,27},{4,2},{5,29},{6,4},{7,31},{8,14},{9,1},{... | collective-permute-start | bytes 1572872 | tf_op jit(solution)/shard_map/ppermute | solution.py:327
  39.6 11.7 %collective-permute-start.6 = (bf16[4,256,256]{2,1,0:T(8,128)(2,1)}, bf16[4,256,256]{2,1,0:T(8,128)(2,1)}, u32[]{:S(2)}, u32[]{:S(2)}) collective-permute-start(bf16[4,256,256]{2,1,0:T(8,128)(2,1)} %get-tuple-element.25), channel_id=1, source_target_pairs={{0,1},{1,0},{2,3},{3,2},{4,5},{5,4},{6,7},{7,6},{8,9},{9,8},{10,11... | collective-permute-start | bytes 1572872 | tf_op jit(solution)/shard_map/ppermute | solution.py:327
  39.6 15.8 %collective-permute-start.7 = (bf16[4,256,256]{2,1,0:T(8,128)(2,1)}, bf16[4,256,256]{2,1,0:T(8,128)(2,1)}, u32[]{:S(2)}, u32[]{:S(2)}) collective-permute-start(bf16[4,256,256]{2,1,0:T(8,128)(2,1)} %get-tuple-element.26), channel_id=1, source_target_pairs={{0,3},{1,8},{2,5},{3,10},{4,7},{5,12},{6,1},{7,14},{8,11},{9,16},{... | collective-permute-start | bytes 1572872 | tf_op jit(solution)/shard_map/ppermute | solution.py:327
  40.4 14.9 %collective-permute-start.8 = (bf16[4,256,256]{2,1,0:T(8,128)(2,1)}, bf16[4,256,256]{2,1,0:T(8,128)(2,1)}, u32[]{:S(2)}, u32[]{:S(2)}) collective-permute-start(bf16[4,256,256]{2,1,0:T(8,128)(2,1)} %get-tuple-element.27), channel_id=1, source_target_pairs={{0,5},{1,16},{2,7},{3,18},{4,1},{5,20},{6,3},{7,22},{8,13},{9,24},... | collective-permute-start | bytes 1572872 | tf_op jit(solution)/shard_map/ppermute | solution.py:327
  45.0 12.8 %collective-permute-start.9 = (bf16[4,256,256]{2,1,0:T(8,128)(2,1)}, bf16[4,256,256]{2,1,0:T(8,128)(2,1)}, u32[]{:S(2)}, u32[]{:S(2)}) collective-permute-start(bf16[4,256,256]{2,1,0:T(8,128)(2,1)} %get-tuple-element.28), channel_id=1, source_target_pairs={{0,7},{1,24},{2,1},{3,26},{4,3},{5,28},{6,5},{7,30},{8,15},{9,0},{... | collective-permute-start | bytes 1572872 | tf_op jit(solution)/shard_map/ppermute | solution.py:327
  45.1 12.8 %copy-start.1 = (bf16[4,256,256]{2,1,0:T(8,128)(2,1)S(1)}, bf16[4,256,256]{2,1,0:T(8,128)(2,1)}, u32[]{:S(2)}) copy-start(bf16[4,256,256]{2,1,0:T(8,128)(2,1)} %get-tuple-element.21.refs_0_) | copy-start | bytes 1572868
  65.6 4.8 %collective-permute-start.10 = (f32[2,8,16]{2,1,0:T(8,128)S(1)}, f32[2,8,16]{2,1,0:T(8,128)S(1)}, u32[]{:S(2)}, u32[]{:S(2)}) collective-permute-start(f32[2,8,16]{2,1,0:T(8,128)S(1)} %slice.165), channel_id=1, source_target_pairs={{0,32},{32,64},{64,96},{96,128},{128,160},{160,192},{192,224},{224... | collective-permute-start | bytes 3080 | tf_op jit(solution)/shard_map/ppermute | solution.py:266
  69.1 4.9 %collective-permute-start.11 = (f32[2,8,16]{2,1,0:T(8,128)S(1)}, f32[2,8,16]{2,1,0:T(8,128)S(1)}, u32[]{:S(2)}, u32[]{:S(2)}) collective-permute-start(f32[2,8,16]{2,1,0:T(8,128)S(1)} %slice.167), channel_id=1, source_target_pairs={{32,0},{64,32},{96,64},{128,96},{160,128},{192,160},{224,192},{0,2... | collective-permute-start | bytes 3080 | tf_op jit(solution)/shard_map/ppermute | solution.py:267
  74.0 1.3 collective-permute-start.12
  74.1 6.5 %collective-permute-start.13 = (f32[12,2,16]{2,1,0:T(2,128)S(1)}, f32[12,2,16]{2,1,0:T(2,128)S(1)}, u32[]{:S(2)}, u32[]{:S(2)}) collective-permute-start(f32[12,2,16]{2,1,0:T(2,128)S(1)} %get-tuple-element.73), channel_id=1, source_target_pairs={{0,31},{1,2},{2,1},{3,4},{4,3},{5,6},{6,5},{7,8},{8,7},{9,10},{10,... | collective-permute-start | bytes 4616 | tf_op jit(solution)/shard_map/ppermute | solution.py:277
  89.8 19.2 %collective-permute-start.14 = (bf16[4,256,256]{2,1,0:T(8,128)(2,1)}, bf16[4,256,256]{2,1,0:T(8,128)(2,1)S(1)}, u32[]{:S(2)}, u32[]{:S(2)}) collective-permute-start(bf16[4,256,256]{2,1,0:T(8,128)(2,1)} %get-tuple-element.30), channel_id=1, source_target_pairs={{0,2},{1,9},{2,4},{3,11},{4,6},{5,13},{6,0},{7,15},{8,10},{9,17},{... | collective-permute-start | bytes 1572872 | tf_op jit(solution)/shard_map/ppermute | solution.py:327
  89.9 19.1 %collective-permute-start.15 = (bf16[4,256,256]{2,1,0:T(8,128)(2,1)}, bf16[4,256,256]{2,1,0:T(8,128)(2,1)S(1)}, u32[]{:S(2)}, u32[]{:S(2)}) collective-permute-start(bf16[4,256,256]{2,1,0:T(8,128)(2,1)} %get-tuple-element.31), channel_id=1, source_target_pairs={{0,4},{1,17},{2,6},{3,19},{4,0},{5,21},{6,2},{7,23},{8,12},{9,25},... | collective-permute-start | bytes 1572872 | tf_op jit(solution)/shard_map/ppermute | solution.py:327
  91.3 18.6 %collective-permute-start.16 = (bf16[4,256,256]{2,1,0:T(8,128)(2,1)}, bf16[4,256,256]{2,1,0:T(8,128)(2,1)S(1)}, u32[]{:S(2)}, u32[]{:S(2)}) collective-permute-start(bf16[4,256,256]{2,1,0:T(8,128)(2,1)} %get-tuple-element.32), channel_id=1, source_target_pairs={{0,6},{1,25},{2,0},{3,27},{4,2},{5,29},{6,4},{7,31},{8,14},{9,1},{... | collective-permute-start | bytes 1572872 | tf_op jit(solution)/shard_map/ppermute | solution.py:327
  94.4 15.5 %collective-permute-start.17 = (bf16[4,256,256]{2,1,0:T(8,128)(2,1)}, bf16[4,256,256]{2,1,0:T(8,128)(2,1)S(1)}, u32[]{:S(2)}, u32[]{:S(2)}) collective-permute-start(bf16[4,256,256]{2,1,0:T(8,128)(2,1)} %get-tuple-element.33), channel_id=1, source_target_pairs={{0,1},{1,0},{2,3},{3,2},{4,5},{5,4},{6,7},{7,6},{8,9},{9,8},{10,11... | collective-permute-start | bytes 1572872 | tf_op jit(solution)/shard_map/ppermute | solution.py:327
  94.4 17.3 %collective-permute-start.18 = (bf16[4,256,256]{2,1,0:T(8,128)(2,1)}, bf16[4,256,256]{2,1,0:T(8,128)(2,1)S(1)}, u32[]{:S(2)}, u32[]{:S(2)}) collective-permute-start(bf16[4,256,256]{2,1,0:T(8,128)(2,1)} %get-tuple-element.34), channel_id=1, source_target_pairs={{0,9},{1,2},{2,11},{3,4},{4,13},{5,6},{6,15},{7,0},{8,17},{9,10},{... | collective-permute-start | bytes 1572872 | tf_op jit(solution)/shard_map/ppermute | solution.py:327
  109.0 10.3 %collective-permute-start.19 = (bf16[4,256,256]{2,1,0:T(8,128)(2,1)}, bf16[4,256,256]{2,1,0:T(8,128)(2,1)S(1)}, u32[]{:S(2)}, u32[]{:S(2)}) collective-permute-start(bf16[4,256,256]{2,1,0:T(8,128)(2,1)} %get-tuple-element.35), channel_id=1, source_target_pairs={{0,17},{1,4},{2,19},{3,6},{4,21},{5,0},{6,23},{7,2},{8,25},{9,12},... | collective-permute-start | bytes 1572872 | tf_op jit(solution)/shard_map/ppermute | solution.py:327
  109.0 13.1 %collective-permute-start.20 = (bf16[4,256,256]{2,1,0:T(8,128)(2,1)}, bf16[4,256,256]{2,1,0:T(8,128)(2,1)}, u32[]{:S(2)}, u32[]{:S(2)}) collective-permute-start(bf16[4,256,256]{2,1,0:T(8,128)(2,1)} %get-tuple-element.36), channel_id=1, source_target_pairs={{0,25},{1,6},{2,27},{3,0},{4,29},{5,2},{6,31},{7,4},{8,1},{9,14},{... | collective-permute-start | bytes 1572872 | tf_op jit(solution)/shard_map/ppermute | solution.py:327
  122.1 1.0 copy-start
  125.6 9.5 %collective-permute-start.21 = (bf16[3,256,256]{2,1,0:T(8,128)(2,1)S(1)}, bf16[3,256,256]{2,1,0:T(8,128)(2,1)S(1)}, u32[]{:S(2)}, u32[]{:S(2)}) collective-permute-start(bf16[3,256,256]{2,1,0:T(8,128)(2,1)S(1)} %add_up.5), channel_id=1, source_target_pairs={{0,16},{1,5},{2,18},{3,7},{4,20},{5,1},{6,22},{7,3},{8,24},{9,13},... | collective-permute-start | bytes 1179656 | tf_op jit(solution)/shard_map/ppermute | solution.py:327
  128.5 10.7 %collective-permute-start.22 = (bf16[3,256,256]{2,1,0:T(8,128)(2,1)S(1)}, bf16[3,256,256]{2,1,0:T(8,128)(2,1)S(1)}, u32[]{:S(2)}, u32[]{:S(2)}) collective-permute-start(bf16[3,256,256]{2,1,0:T(8,128)(2,1)S(1)} %add_up.6), channel_id=1, source_target_pairs={{0,8},{1,3},{2,10},{3,5},{4,12},{5,7},{6,14},{7,1},{8,16},{9,11},{... | collective-permute-start | bytes 1179656 | tf_op jit(solution)/shard_map/ppermute | solution.py:327
  130.0 9.2 %collective-permute-start.23 = (bf16[3,256,256]{2,1,0:T(8,128)(2,1)S(1)}, bf16[3,256,256]{2,1,0:T(8,128)(2,1)S(1)}, u32[]{:S(2)}, u32[]{:S(2)}) collective-permute-start(bf16[3,256,256]{2,1,0:T(8,128)(2,1)S(1)} %add_up.7), channel_id=1, source_target_pairs={{0,24},{1,7},{2,26},{3,1},{4,28},{5,3},{6,30},{7,5},{8,0},{9,15},{... | collective-permute-start | bytes 1179656 | tf_op jit(solution)/shard_map/ppermute | solution.py:327

commit v6 on v5

--- a/solution.py
+++ b/solution.py
@@ -23,39 +23,39 @@
     return pltpu.CompilerParams(vmem_limit_bytes=mib * MIB)
 
 
-def select_blocks(numbers, stores, parts):
-    inner = len(stores)
+def select_blocks(bricks, numbers, stores):
+    inner, parts = len(stores), bricks.shape[0]
     block = stores[0].shape[1:]
 
-    def kernel(numbers_ref, *refs):
+    def kernel(bricks_ref, numbers_ref, *refs):
         ins, outs, sems = refs[:inner], refs[inner:-1], refs[-1]
         places = [(p, d) for p in range(parts) for d in range(inner)]
 
         def copy(p, d):
-            number = jnp.maximum(numbers_ref[p, d], 0)
+            number = jnp.maximum(numbers_ref[bricks_ref[p], d], 0)
             return pltpu.make_async_copy(ins[d].at[number], outs[p].at[d], sems.at[p, d])
 
         for p, d in places:
 
-            @pl.when(numbers_ref[p, d] >= 0)
+            @pl.when(numbers_ref[bricks_ref[p], d] >= 0)
             def _():
                 copy(p, d).start()
 
         for p, d in places:
 
-            @pl.when(numbers_ref[p, d] >= 0)
+            @pl.when(numbers_ref[bricks_ref[p], d] >= 0)
             def _():
                 copy(p, d).wait()
 
     return pl.pallas_call(
         kernel,
         out_shape=[pltpu.HBM((inner,) + block, stores[0].dtype)] * parts,
-        in_specs=[SCALARS] + [IN_HBM] * inner,
+        in_specs=[SCALARS, SCALARS] + [IN_HBM] * inner,
         out_specs=[IN_HBM] * parts,
         scratch_shapes=[pltpu.SemaphoreType.DMA((parts, inner))],
         compiler_params=params(4),
         name="select_blocks",
-    )(numbers, *stores)
+    )(bricks, numbers, *stores)
 
 
 def gather_tables(index, table):
@@ -147,7 +147,7 @@
             pltpu.VMEM((count, both, points), jnp.bfloat16),
             pltpu.SemaphoreType.DMA((2, count)),
         ],
-        compiler_params=params(52),
+        compiler_params=params(48),
         name="collocate",
     )(places, *blocks, *tables)
 
@@ -208,11 +208,11 @@
     )(places, scaled, *tables)
 
 
-def add_up(targets, parts, place, own_count, dtype):
+def add_up(bricks, numbers, parts, place, own_count, dtype):
     _, rows, cols = parts[0].shape
     count = len(parts)
 
-    def kernel(targets_ref, *refs):
+    def kernel(bricks_ref, numbers_ref, *refs):
         parts_refs, (out_ref, held, total, sems) = refs[:count], refs[count:]
 
         def fetch(s):
@@ -220,13 +220,13 @@
 
         for s in range(count):
 
-            @pl.when(targets_ref[s] >= 0)
+            @pl.when(numbers_ref[bricks_ref[s], place] >= 0)
             def _():
                 fetch(s).start()
 
         total[...] = jnp.zeros_like(total)
         for s in range(count):
-            target = targets_ref[s]
+            target = numbers_ref[bricks_ref[s], place]
 
             @pl.when(target >= 0)
             def _():
@@ -238,7 +238,7 @@
     return pl.pallas_call(
         kernel,
         out_shape=jax.ShapeDtypeStruct((own_count, rows, cols), dtype),
-        in_specs=[SCALARS] + [IN_HBM] * count,
+        in_specs=[SCALARS, SCALARS] + [IN_HBM] * count,
         out_specs=RESIDENT,
         scratch_shapes=[
             pltpu.VMEM((count, rows, cols), jnp.bfloat16),
@@ -247,7 +247,7 @@
         ],
         compiler_params=params(8),
         name="add_up",
-    )(targets, *parts)
+    )(bricks, numbers, *parts)
 
 
 def ends(block, dim, width):
@@ -327,14 +327,19 @@
     return lax.ppermute(value, BRICK, pairs)
 
 
+def turns(side):
+    near = [1, side - 1]
+    far = [k for k in range(side) if k not in (0, 1, side - 1)]
+    return [(o, k) for o in (0, 1) for k in near] + [(o, k) for k in far for o in (0, 1)] + [(1, 0)]
+
+
 def order(side):
     return [side // 2] + [k for k in range(side) if k not in (side // 2, 0)]
 
 
-def find(owners, ids, bricks, wanted):
-    hit = owners[bricks][:, None, :] == wanted[None, :, None]
-    number = jnp.sum(jnp.where(hit, ids[bricks][:, None, :], 0), axis=-1)
-    return jnp.where(jnp.any(hit, axis=-1), number, -1).astype(jnp.int32)
+def find(owners, ids, wanted):
+    hit = owners[:, None, :] == wanted[None, :, None]
+    return jnp.max(jnp.where(hit, ids[:, None, :], -1), axis=-1).astype(jnp.int32)
 
 
 def local(store, crossing, phi, rows_index, cols_index):
@@ -356,16 +361,16 @@
     table = phi.reshape(points, functions).T
     index = jnp.concatenate([rows_index[0], cols_index[0]], axis=1)[:, None, :]
     each = index.shape[0] // GATHERS
-    tables = [gather_tables(index[i : i + each], table) for i in range(0, index.shape[0], each)]
+    pieces = [index[i : i + each] for i in range(0, index.shape[0], each)]
     ahead = jnp.where(c == 0, x * ny + (y + steps) % ny, ((x + steps) % nx) * ny + y) * nc
-    served = jnp.concatenate([ahead + c, ahead + (1 - c)])
+    served = jnp.concatenate([ahead + c, ahead + (1 - c)]).astype(jnp.int32)
     source = jnp.where(c == 0, ((x - steps) % nx) * ny + y, x * ny + (y - steps) % ny) * nc + c
-    blocks = list(select_blocks(find(owners, ids, served, source), stores, 2 * side))
-    for step in order(side) + [0]:
-        for other in (0, 1):
-            if step or other:
-                i = other * side + step
-                blocks[i] = moved(blocks[i], step, bool(other), lambda c, to: c == 0)
+    blocks = list(select_blocks(served, find(owners, ids, source), stores))
+    *pieces[1:], blocks[side] = lax.optimization_barrier((*pieces[1:], blocks[side]))
+    tables = [gather_tables(piece, table) for piece in pieces]
+    for other, step in turns(side):
+        i = other * side + step
+        blocks[i] = moved(blocks[i], step, bool(other), lambda c, to: c == 0)
     to_x, rest = slots // (ny * nc), slots % (ny * nc)
     to_y, to_c = rest // nc, rest % nc
     behind_x, behind_y = (x - to_x) % nx, (y - to_y) % ny
@@ -381,20 +386,18 @@
     second = jnp.where(to_c == 0, ahead_x, ahead_y)
     places = jnp.stack([first + jnp.where(to_c == c, 0, side), second]).astype(jnp.int32)
     parts = list(integrate(places, scaled, tables, 2 * side, side))
-    for step in order(side) + [0]:
-        for other in (0, 1):
-            if step or other:
-                i = other * side + step
-                parts[i] = moved(parts[i], step, bool(other), lambda c, to: to == 0)
+    for other, step in turns(side):
+        i = other * side + step
+        parts[i] = moved(parts[i], step, bool(other), lambda c, to: to == 0)
     behind = jnp.where(c == 0, x * ny + (y - steps) % ny, ((x - steps) % nx) * ny + y) * nc
-    sources = jnp.concatenate([behind + c, behind + (1 - c)])
+    sources = jnp.concatenate([behind + c, behind + (1 - c)]).astype(jnp.int32)
     wanted = jnp.where(c == 0, ((x + steps) % nx) * ny + y, x * ny + (y + steps) % ny) * nc + c
-    targets = find(owners, ids, sources, wanted)
+    numbers = find(owners, ids, wanted)
     total = []
     for step in order(side):
-        summed = add_up(targets[:, step], parts, step, own_count, jnp.bfloat16)
+        summed = add_up(sources, numbers, parts, step, own_count, jnp.bfloat16)
         total.append(moved(summed, step, False, lambda c, to: c == 1))
-    own = add_up(targets[:, 0], parts, 0, own_count, jnp.float32)
+    own = add_up(sources, numbers, parts, 0, own_count, jnp.float32)
     for piece in total:
         own = own + piece.astype(jnp.float32)
     return own

time: 140 us -> 138 us (0.986)
  waiting for transfers between devices: 52.4 us -> 43.7 us
  starting transfers between devices: 23.7 us -> 30.1 us
  Pallas kernels: 52.2 us -> 54.7 us
  local copies, waits for them, and re-layouts: 8.21 us -> 5.72 us
    ppermute x20, waiting for transfers between devices: 42 us -> 34.2 us  [moved(): return lax.ppermute(value, BRICK, pairs)]
    ppermute x20, starting transfers between devices: 19.2 us -> 24.9 us  [moved(): return lax.ppermute(value, BRICK, pairs)]
    gather x4 -> x0, local copies, waits for them, and re-layouts: 2.22 us -> none  [the longest x2 1.11 us: find(): number = jnp.sum(jnp.where(hit, ids[bricks][:, None, :], 0), axis=-1)]
    pallas_call x1, Pallas kernels: 7.62 us -> 9.74 us  [collocate(): pl.pallas_call(kernel, out_shape=jax.ShapeDtypeStruct((8, points), jnp.fl...]
  transfers between devices with their start and end apart: 24 -> 24, of which waited for: 12 -> 9; matrix products, arithmetic and copies ran while one was open for 6% -> 4% of each run, Pallas kernels for 22% -> 23%
where the time goes in v6:
time: 138 us; the launch traced here: 137 us
  Pallas kernels  54.7 us (40%)
  waiting for transfers between devices  43.7 us (32%)
  starting transfers between devices  30.1 us (22%)
  local copies, waits for them, and re-layouts  5.72 us (4%)
  other arithmetic  2.59 us (2%)
    ppermute x20, waiting for transfers between devices, moved(): return lax.ppermute(value, BRICK, pairs)  34.2 us
    pallas_call x4, Pallas kernels, gather_tables(): pl.pallas_call(kernel, out_shape=pltpu.HBM((count, width, points), jnp.bf...  25.2 us
    ppermute x20, starting transfers between devices, moved(): return lax.ppermute(value, BRICK, pairs)  24.9 us
    pallas_call x1, Pallas kernels, collocate(): pl.pallas_call(kernel, out_shape=jax.ShapeDtypeStruct((8, points), jnp.fl...  9.74 us
    pallas_call x4, Pallas kernels, add_up(): pl.pallas_call(kernel, out_shape=jax.ShapeDtypeStruct((own_count, rows, c...  9.03 us
    pallas_call x1, Pallas kernels, integrate(): pl.pallas_call(kernel, out_shape=[pltpu.HBM((inner, width, width), jnp.bf...  8.36 us
    ppermute x1, waiting for transfers between devices, extended_pairs(): far = lax.ppermute(jnp.where(odd, high, low), axis, between)  4.59 us
    ppermute x1, waiting for transfers between devices, extended_ring(): above = lax.ppermute(low, axis, backward)  3.65 us
  transfers between devices with their start and end apart: 24, of which 9 were waited for; matrix products, arithmetic and copies ran while one was open for 4% of the time, Pallas kernels for 23%

profile of v6, /device:TPU:96, one launch (start us, length us, event | category | flops | bytes accessed | tf_op | source)
XLA Modules:
  0.0 137.1 jit_solution(16903831842366131704)
XLA Ops:
  0.0 1.5 %collective-permute-start = (bf16[3,256,256]{2,1,0:T(8,128)(2,1)}, bf16[3,256,256]{2,1,0:T(8,128)(2,1)S(1)}, u32[]{:S(2)}, u32[]{:S(2)}) collective-permute-start(bf16[3,256,256]{2,1,0:T(8,128)(2,1)} %refs_0_.1), channel_id=1, source_target_pairs={{0,8},{1,3},{2,10},{3,5},{4,12},{5,7},{6,14},{7,1},{8,16},{9,11},{... | collective-permute-start | bytes 1179656 | tf_op jit(solution)/shard_map/ppermute | solution.py:327
  1.5 2.7 %collective-permute-start.1 = (bf16[3,256,256]{2,1,0:T(8,128)(2,1)}, bf16[3,256,256]{2,1,0:T(8,128)(2,1)S(1)}, u32[]{:S(2)}, u32[]{:S(2)}) collective-permute-start(bf16[3,256,256]{2,1,0:T(8,128)(2,1)} %refs_0_.1), channel_id=1, source_target_pairs={{0,16},{1,5},{2,18},{3,7},{4,20},{5,1},{6,22},{7,3},{8,24},{9,13},... | collective-permute-start | bytes 1179656 | tf_op jit(solution)/shard_map/ppermute | solution.py:327
  4.2 1.4 %collective-permute-start.2 = (bf16[3,256,256]{2,1,0:T(8,128)(2,1)}, bf16[3,256,256]{2,1,0:T(8,128)(2,1)S(1)}, u32[]{:S(2)}, u32[]{:S(2)}) collective-permute-start(bf16[3,256,256]{2,1,0:T(8,128)(2,1)} %refs_0_.1), channel_id=1, source_target_pairs={{0,24},{1,7},{2,26},{3,1},{4,28},{5,3},{6,30},{7,5},{8,0},{9,15},{... | collective-permute-start | bytes 1179656 | tf_op jit(solution)/shard_map/ppermute | solution.py:327
  5.7 0.8 copy.20
  6.5 0.1 copy.23
  6.6 0.1 copy.24
  6.7 0.1 select_reduce_fusion
  6.8 0.1 copy.25.numbers_ref
  6.9 0.8 fusion.19
  7.7 2.9 %copy.26 = bf16[1024,1024]{0,1:T(8,128)(2,1)S(1)} copy(bf16[1024,1024]{1,0:T(8,128)(2,1)} %bitcast.18) | data formatting | bytes 4194304 | tf_op jit(solution)/shard_map/reshape | solution.py:361
  10.6 0.1 pad_add_fusion.4.bricks_ref
  10.7 0.0 copy-start.2
  10.7 6.3 %gather_tables.4.refs_8_.refs_0_ = bf16[4,512,1024]{2,1,0:T(8,128)(2,1)} custom-call(s32[4,1,512]{2,1,0:T(1,128)S(1)} %copy.27.index_ref, bf16[1024,1024]{1,0:T(8,128)(2,1)S(1)} %bitcast.14), custom_call_target="tpu_custom_call" | custom-call | flops 4294967296 | bytes 4194304 | tf_op jit(solution)/shard_map/gather_tables/pallas_call | solution.py:83
  17.0 0.0 collective-permute-done.refs_1_
  17.0 2.4 %select_blocks.1 = (bf16[4,256,256]{2,1,0:T(8,128)(2,1)}, bf16[4,256,256]{2,1,0:T(8,128)(2,1)}, bf16[4,256,256]{2,1,0:T(8,128)(2,1)}, bf16[4,256,256]{2,1,0:T(8,...) custom-call(s32[8]{0:T(128)S(1)} %pad_add_fusion.4.bricks_ref, ...), custom_call_target="tpu_custom_call" | custom-call | tf_op jit(solution)/shard_map/select_blocks/pallas_call | solution.py:50
  19.4 0.1 collective-permute-start.6
  19.5 1.7 %collective-permute-start.3 = (bf16[4,256,256]{2,1,0:T(8,128)(2,1)}, bf16[4,256,256]{2,1,0:T(8,128)(2,1)S(1)}, u32[]{:S(2)}, u32[]{:S(2)}) collective-permute-start(bf16[4,256,256]{2,1,0:T(8,128)(2,1)} %get-tuple-element.26), channel_id=1, source_target_pairs={{0,2},{1,9},{2,4},{3,11},{4,6},{5,13},{6,0},{7,15},{8,10},{9,17},{... | collective-permute-start | bytes 1572872 | tf_op jit(solution)/shard_map/ppermute | solution.py:327
  21.3 2.9 %collective-permute-start.4 = (bf16[4,256,256]{2,1,0:T(8,128)(2,1)}, bf16[4,256,256]{2,1,0:T(8,128)(2,1)S(1)}, u32[]{:S(2)}, u32[]{:S(2)}) collective-permute-start(bf16[4,256,256]{2,1,0:T(8,128)(2,1)} %get-tuple-element.27), channel_id=1, source_target_pairs={{0,4},{1,17},{2,6},{3,19},{4,0},{5,21},{6,2},{7,23},{8,12},{9,25},... | collective-permute-start | bytes 1572872 | tf_op jit(solution)/shard_map/ppermute | solution.py:327
  24.1 1.5 %collective-permute-start.5 = (bf16[4,256,256]{2,1,0:T(8,128)(2,1)}, bf16[4,256,256]{2,1,0:T(8,128)(2,1)S(1)}, u32[]{:S(2)}, u32[]{:S(2)}) collective-permute-start(bf16[4,256,256]{2,1,0:T(8,128)(2,1)} %get-tuple-element.28), channel_id=1, source_target_pairs={{0,6},{1,25},{2,0},{3,27},{4,2},{5,29},{6,4},{7,31},{8,14},{9,1},{... | collective-permute-start | bytes 1572872 | tf_op jit(solution)/shard_map/ppermute | solution.py:327
  25.6 6.4 %gather_tables.5.refs_9_.refs_1_ = bf16[4,512,1024]{2,1,0:T(8,128)(2,1)} custom-call(s32[4,1,512]{2,1,0:T(1,128)S(1)} %copy.28.index_ref, bf16[1024,1024]{1,0:T(8,128)(2,1)S(1)} %bitcast.15), custom_call_target="tpu_custom_call" | custom-call | flops 4294967296 | bytes 4194304 | tf_op jit(solution)/shard_map/gather_tables/pallas_call | solution.py:83
  32.0 0.6 collective-permute-start.8
  32.6 5.3 %collective-permute-start.9 = (bf16[4,256,256]{2,1,0:T(8,128)(2,1)S(1)}, bf16[4,256,256]{2,1,0:T(8,128)(2,1)S(1)}, u32[]{:S(2)}, u32[]{:S(2)}) collective-permute-start(bf16[4,256,256]{2,1,0:T(8,128)(2,1)S(1)} %copy-done.3), channel_id=1, source_target_pairs={{0,7},{1,24},{2,1},{3,26},{4,3},{5,28},{6,5},{7,30},{8,15},{9,0},{... | collective-permute-start | bytes 1572872 | tf_op jit(solution)/shard_map/ppermute | solution.py:327
  37.9 6.3 %gather_tables.6.refs_10_.refs_2_ = bf16[4,512,1024]{2,1,0:T(8,128)(2,1)} custom-call(s32[4,1,512]{2,1,0:T(1,128)S(1)} %copy.29.index_ref, bf16[1024,1024]{1,0:T(8,128)(2,1)S(1)} %bitcast.16), custom_call_target="tpu_custom_call" | custom-call | flops 4294967296 | bytes 4194304 | tf_op jit(solution)/shard_map/gather_tables/pallas_call | solution.py:83
  44.2 6.3 %gather_tables.7.refs_11_.refs_3_ = bf16[4,512,1024]{2,1,0:T(8,128)(2,1)} custom-call(s32[4,1,512]{2,1,0:T(1,128)S(1)} %slice.148.index_ref, bf16[1024,1024]{1,0:T(8,128)(2,1)S(1)} %bitcast.17), custom_call_target="tpu_custom_call" | custom-call | flops 4294967296 | bytes 4194304 | tf_op jit(solution)/shard_map/gather_tables/pallas_call | solution.py:83
  50.5 9.7 %collocate.1 = f32[8,1024]{1,0:T(8,128)S(1)} custom-call(s32[2,16]{1,0:T(2,128)S(1)} %pad_add_fusion.2.places_ref, bf16[4,256,256]{2,1,0:T(8,128)(2,1)S(1)} %copy-done.1, bf16[4,256,256]{2,1,0:T(8,128)(2,1)S(1)} %collective-permute-done.3.refs_1_, bf16[4,256,256]{2,1,0:T(8,128)(2,1)S(1)} %collective-permute-done.4.refs_2_, ...), custom_call_target="tpu_custom_call" | custom-call | tf_op jit(solution)/shard_map/collocate/pallas_call | solution.py:140
  60.3 0.1 slice.152
  60.4 3.2 %collective-permute-start.10 = (f32[2,8,16]{2,1,0:T(8,128)S(1)}, f32[2,8,16]{2,1,0:T(8,128)S(1)}, u32[]{:S(2)}, u32[]{:S(2)}) collective-permute-start(f32[2,8,16]{2,1,0:T(8,128)S(1)} %slice.152), channel_id=1, source_target_pairs={{0,32},{32,64},{64,96},{96,128},{128,160},{160,192},{192,224},{224... | collective-permute-start | bytes 3080 | tf_op jit(solution)/shard_map/ppermute | solution.py:266
  63.6 0.1 reshape.114
  63.6 0.1 slice.154
  63.7 0.0 collective-permute-start.11
  63.8 1.2 collective-permute-done.10
  64.9 3.7 %collective-permute-done.11 = f32[2,8,16]{2,1,0:T(8,128)S(1)} collective-permute-done((f32[2,8,16]{2,1,0:T(8,128)S(1)}, f32[2,8,16]{2,1,0:T(8,128)S(1)}, u32[]{:S(2)}, u32[]{:S(2)}) %collective-permute-start.11) | collective-permute-done | bytes 1056 | tf_op jit(solution)/shard_map/ppermute | solution.py:267
  68.6 0.1 collective-permute-start.12
  68.7 1.9 %collective-permute-start.13 = (f32[12,2,16]{2,1,0:T(2,128)S(1)}, f32[12,2,16]{2,1,0:T(2,128)S(1)}, u32[]{:S(2)}, u32[]{:S(2)}) collective-permute-start(f32[12,2,16]{2,1,0:T(2,128)S(1)} %get-tuple-element.79), channel_id=1, source_target_pairs={{0,31},{1,2},{2,1},{3,4},{4,3},{5,6},{6,5},{7,8},{8,7},{9,10},{10,... | collective-permute-start | bytes 4616 | tf_op jit(solution)/shard_map/ppermute | solution.py:277
  70.7 4.6 %collective-permute-done.13 = f32[12,2,16]{2,1,0:T(2,128)S(1)} collective-permute-done((f32[12,2,16]{2,1,0:T(2,128)S(1)}, f32[12,2,16]{2,1,0:T(2,128)S(1)}, u32[]{:S(2)}, u32[]{:S(2)}) %collective-permute-start.13) | collective-permute-done | bytes 1568 | tf_op jit(solution)/shard_map/ppermute | solution.py:277
  75.3 0.1 fusion.46
  75.4 0.1 fusion.47
  75.5 0.1 fusion.42
  75.6 0.1 fusion.48
  75.7 0.1 fusion.49
  75.8 0.1 fusion.12
  75.9 0.1 fusion.9
  76.0 0.1 mul.148.scaled_ref
  76.1 8.4 %integrate.1 = (bf16[4,256,256]{2,1,0:T(8,128)(2,1)}, bf16[4,256,256]{2,1,0:T(8,128)(2,1)}, bf16[4,256,256]{2,1,0:T(8,128)(2,1)}, bf16[4,256,256]{2,1,0:T(8,128)...) custom-call(s32[2,16]{1,0:T(2,128)S(1)} %pad_add_fusion.1.places_ref, ...), custom_call_target="tpu_custom_call" | custom-call | tf_op jit(solution)/shard_map/integrate/pallas_call | solution.py:196
  84.4 0.1 collective-permute-start.14
  84.5 0.1 collective-permute-start.15
  84.6 3.1 %collective-permute-start.16 = (bf16[4,256,256]{2,1,0:T(8,128)(2,1)}, bf16[4,256,256]{2,1,0:T(8,128)(2,1)S(1)}, u32[]{:S(2)}, u32[]{:S(2)}) collective-permute-start(bf16[4,256,256]{2,1,0:T(8,128)(2,1)} %get-tuple-element.40), channel_id=1, source_target_pairs={{0,6},{1,25},{2,0},{3,27},{4,2},{5,29},{6,4},{7,31},{8,14},{9,1},{... | collective-permute-start | bytes 1572872 | tf_op jit(solution)/shard_map/ppermute | solution.py:327
  87.8 17.6 %collective-permute-done.14.refs_1_ = bf16[4,256,256]{2,1,0:T(8,128)(2,1)S(1)} collective-permute-done((bf16[4,256,256]{2,1,0:T(8,128)(2,1)}, bf16[4,256,256]{2,1,0:T(8,128)(2,1)S(1)}, u32[]{:S(2)}, u32[]{:S(2)}) %collective-permute-start.14) | collective-permute-done | bytes 524320 | tf_op jit(solution)/shard_map/ppermute | solution.py:327
  105.3 0.1 copy.30.numbers_ref
  105.4 0.1 pad_add_fusion.3.bricks_ref
  105.5 0.8 collective-permute-done.18.refs_5_
  106.3 9.3 %collective-permute-done.19.refs_6_ = bf16[4,256,256]{2,1,0:T(8,128)(2,1)S(1)} collective-permute-done((bf16[4,256,256]{2,1,0:T(8,128)(2,1)}, bf16[4,256,256]{2,1,0:T(8,128)(2,1)S(1)}, u32[]{:S(2)}, u32[]{:S(2)}) %collective-permute-start.19) | collective-permute-done | bytes 524320 | tf_op jit(solution)/shard_map/ppermute | solution.py:327
  115.7 2.7 %collective-permute-done.20.refs_7_ = bf16[4,256,256]{2,1,0:T(8,128)(2,1)} collective-permute-done((bf16[4,256,256]{2,1,0:T(8,128)(2,1)}, bf16[4,256,256]{2,1,0:T(8,128)(2,1)}, u32[]{:S(2)}, u32[]{:S(2)}) %collective-permute-start.20) | collective-permute-done | bytes 524320 | tf_op jit(solution)/shard_map/ppermute | solution.py:327
  118.4 1.0 copy-done
  119.4 2.3 %add_up.5 = bf16[3,256,256]{2,1,0:T(8,128)(2,1)S(1)} custom-call(s32[8]{0:T(128)S(1)} %pad_add_fusion.3.bricks_ref, s32[32,4]{1,0:T(8,128)S(1)} %copy.30.numbers_ref, bf16[4,256,256]{2,1,0:T(8,128)(2,1)S(1)} %copy-done, bf16[4,256,256]{2,1,0:T(8,128)(2,1)S(1)} %collective-permute-done.14.refs_1_, bf16[4,256,256]{2,1,0:T(8,128)(2,1)S(1)} %collective-permute-done.15.refs_2_, ...), custom_call_target="tpu_custom_call" | custom-call | tf_op jit(solution)/shard_map/add_up/pallas_call | solution.py:238
  121.7 0.1 collective-permute-start.21
  121.8 2.3 %add_up.6 = bf16[3,256,256]{2,1,0:T(8,128)(2,1)S(1)} custom-call(s32[8]{0:T(128)S(1)} %pad_add_fusion.3.bricks_ref, s32[32,4]{1,0:T(8,128)S(1)} %copy.30.numbers_ref, bf16[4,256,256]{2,1,0:T(8,128)(2,1)S(1)} %copy-done, bf16[4,256,256]{2,1,0:T(8,128)(2,1)S(1)} %collective-permute-done.14.refs_1_, bf16[4,256,256]{2,1,0:T(8,128)(2,1)S(1)} %collective-permute-done.15.refs_2_, ...), custom_call_target="tpu_custom_call" | custom-call | tf_op jit(solution)/shard_map/add_up/pallas_call | solution.py:238
  124.1 0.1 collective-permute-start.22
  124.2 2.6 %add_up.7 = bf16[3,256,256]{2,1,0:T(8,128)(2,1)S(1)} custom-call(s32[8]{0:T(128)S(1)} %pad_add_fusion.3.bricks_ref, s32[32,4]{1,0:T(8,128)S(1)} %copy.30.numbers_ref, bf16[4,256,256]{2,1,0:T(8,128)(2,1)S(1)} %copy-done, bf16[4,256,256]{2,1,0:T(8,128)(2,1)S(1)} %collective-permute-done.14.refs_1_, bf16[4,256,256]{2,1,0:T(8,128)(2,1)S(1)} %collective-permute-done.15.refs_2_, ...), custom_call_target="tpu_custom_call" | custom-call | tf_op jit(solution)/shard_map/add_up/pallas_call | solution.py:238
  126.8 3.6 %collective-permute-start.23 = (bf16[3,256,256]{2,1,0:T(8,128)(2,1)S(1)}, bf16[3,256,256]{2,1,0:T(8,128)(2,1)S(1)}, u32[]{:S(2)}, u32[]{:S(2)}) collective-permute-start(bf16[3,256,256]{2,1,0:T(8,128)(2,1)S(1)} %add_up.7), channel_id=1, source_target_pairs={{0,24},{1,7},{2,26},{3,1},{4,28},{5,3},{6,30},{7,5},{8,0},{9,15},{... | collective-permute-start | bytes 1179656 | tf_op jit(solution)/shard_map/ppermute | solution.py:327
  130.4 1.9 %add_up.4 = f32[3,256,256]{2,1,0:T(8,128)S(1)} custom-call(s32[8]{0:T(128)S(1)} %pad_add_fusion.3.bricks_ref, s32[32,4]{1,0:T(8,128)S(1)} %copy.30.numbers_ref, bf16[4,256,256]{2,1,0:T(8,128)(2,1)S(1)} %copy-done, bf16[4,256,256]{2,1,0:T(8,128)(2,1)S(1)} %collective-permute-done.14.refs_1_, bf16[4,256,256]{2,1,0:T(8,128)(2,1)S(1)} %collective-permute-done.15.refs_2_, ...), custom_call_target="tpu_custom_call" | custom-call | tf_op jit(solution)/shard_map/add_up/pallas_call | solution.py:238
  132.3 3.0 %collective-permute-done.22 = bf16[3,256,256]{2,1,0:T(8,128)(2,1)S(1)} collective-permute-done((bf16[3,256,256]{2,1,0:T(8,128)(2,1)S(1)}, bf16[3,256,256]{2,1,0:T(8,128)(2,1)S(1)}, u32[]{:S(2)}, u32[]{:S(2)}) %collective-permute-start.22) | collective-permute-done | bytes 393248 | tf_op jit(solution)/shard_map/ppermute | solution.py:327
  135.3 0.8 collective-permute-done.23
  136.1 1.0 convert_add_fusion
  (52 shorter events, 0.3 us)
Async XLA Ops:
  0.0 17.0 %collective-permute-start = (bf16[3,256,256]{2,1,0:T(8,128)(2,1)}, bf16[3,256,256]{2,1,0:T(8,128)(2,1)S(1)}, u32[]{:S(2)}, u32[]{:S(2)}) collective-permute-start(bf16[3,256,256]{2,1,0:T(8,128)(2,1)} %refs_0_.1), channel_id=1, source_target_pairs={{0,8},{1,3},{2,10},{3,5},{4,12},{5,7},{6,14},{7,1},{8,16},{9,11},{... | collective-permute-start | bytes 1179656 | tf_op jit(solution)/shard_map/ppermute | solution.py:327
  1.5 15.5 %collective-permute-start.1 = (bf16[3,256,256]{2,1,0:T(8,128)(2,1)}, bf16[3,256,256]{2,1,0:T(8,128)(2,1)S(1)}, u32[]{:S(2)}, u32[]{:S(2)}) collective-permute-start(bf16[3,256,256]{2,1,0:T(8,128)(2,1)} %refs_0_.1), channel_id=1, source_target_pairs={{0,16},{1,5},{2,18},{3,7},{4,20},{5,1},{6,22},{7,3},{8,24},{9,13},... | collective-permute-start | bytes 1179656 | tf_op jit(solution)/shard_map/ppermute | solution.py:327
  4.2 12.8 %collective-permute-start.2 = (bf16[3,256,256]{2,1,0:T(8,128)(2,1)}, bf16[3,256,256]{2,1,0:T(8,128)(2,1)S(1)}, u32[]{:S(2)}, u32[]{:S(2)}) collective-permute-start(bf16[3,256,256]{2,1,0:T(8,128)(2,1)} %refs_0_.1), channel_id=1, source_target_pairs={{0,24},{1,7},{2,26},{3,1},{4,28},{5,3},{6,30},{7,5},{8,0},{9,15},{... | collective-permute-start | bytes 1179656 | tf_op jit(solution)/shard_map/ppermute | solution.py:327
  10.7 6.3 %copy-start.2 = (bf16[3,256,256]{2,1,0:T(8,128)(2,1)S(1)}, bf16[3,256,256]{2,1,0:T(8,128)(2,1)}, u32[]{:S(2)}) copy-start(bf16[3,256,256]{2,1,0:T(8,128)(2,1)} %refs_0_.1) | copy-start | bytes 1179652
  19.4 12.6 %collective-permute-start.6 = (bf16[4,256,256]{2,1,0:T(8,128)(2,1)}, bf16[4,256,256]{2,1,0:T(8,128)(2,1)S(1)}, u32[]{:S(2)}, u32[]{:S(2)}) collective-permute-start(bf16[4,256,256]{2,1,0:T(8,128)(2,1)} %get-tuple-element.30), channel_id=1, source_target_pairs={{0,1},{1,0},{2,3},{3,2},{4,5},{5,4},{6,7},{7,6},{8,9},{9,8},{10,11... | collective-permute-start | bytes 1572872 | tf_op jit(solution)/shard_map/ppermute | solution.py:327
  19.5 13.1 %collective-permute-start.3 = (bf16[4,256,256]{2,1,0:T(8,128)(2,1)}, bf16[4,256,256]{2,1,0:T(8,128)(2,1)S(1)}, u32[]{:S(2)}, u32[]{:S(2)}) collective-permute-start(bf16[4,256,256]{2,1,0:T(8,128)(2,1)} %get-tuple-element.26), channel_id=1, source_target_pairs={{0,2},{1,9},{2,4},{3,11},{4,6},{5,13},{6,0},{7,15},{8,10},{9,17},{... | collective-permute-start | bytes 1572872 | tf_op jit(solution)/shard_map/ppermute | solution.py:327
  21.3 29.2 %collective-permute-start.4 = (bf16[4,256,256]{2,1,0:T(8,128)(2,1)}, bf16[4,256,256]{2,1,0:T(8,128)(2,1)S(1)}, u32[]{:S(2)}, u32[]{:S(2)}) collective-permute-start(bf16[4,256,256]{2,1,0:T(8,128)(2,1)} %get-tuple-element.27), channel_id=1, source_target_pairs={{0,4},{1,17},{2,6},{3,19},{4,0},{5,21},{6,2},{7,23},{8,12},{9,25},... | collective-permute-start | bytes 1572872 | tf_op jit(solution)/shard_map/ppermute | solution.py:327
  24.1 26.3 %collective-permute-start.5 = (bf16[4,256,256]{2,1,0:T(8,128)(2,1)}, bf16[4,256,256]{2,1,0:T(8,128)(2,1)S(1)}, u32[]{:S(2)}, u32[]{:S(2)}) collective-permute-start(bf16[4,256,256]{2,1,0:T(8,128)(2,1)} %get-tuple-element.28), channel_id=1, source_target_pairs={{0,6},{1,25},{2,0},{3,27},{4,2},{5,29},{6,4},{7,31},{8,14},{9,1},{... | collective-permute-start | bytes 1572872 | tf_op jit(solution)/shard_map/ppermute | solution.py:327
  25.6 6.4 %copy-start.4 = (bf16[4,256,256]{2,1,0:T(8,128)(2,1)S(1)}, bf16[4,256,256]{2,1,0:T(8,128)(2,1)}, u32[]{:S(2)}) copy-start(bf16[4,256,256]{2,1,0:T(8,128)(2,1)} %get-tuple-element.32) | copy-start | bytes 1572868
  25.6 7.0 %copy-start.3 = (bf16[4,256,256]{2,1,0:T(8,128)(2,1)S(1)}, bf16[4,256,256]{2,1,0:T(8,128)(2,1)}, u32[]{:S(2)}) copy-start(bf16[4,256,256]{2,1,0:T(8,128)(2,1)} %get-tuple-element.33) | copy-start | bytes 1572868
  25.6 24.9 %collective-permute-start.7 = (bf16[4,256,256]{2,1,0:T(8,128)(2,1)}, bf16[4,256,256]{2,1,0:T(8,128)(2,1)S(1)}, u32[]{:S(2)}, u32[]{:S(2)}) collective-permute-start(bf16[4,256,256]{2,1,0:T(8,128)(2,1)} %get-tuple-element.31), channel_id=1, source_target_pairs={{0,3},{1,8},{2,5},{3,10},{4,7},{5,12},{6,1},{7,14},{8,11},{9,16},{... | collective-permute-start | bytes 1572872 | tf_op jit(solution)/shard_map/ppermute | solution.py:327
  32.0 18.5 %collective-permute-start.8 = (bf16[4,256,256]{2,1,0:T(8,128)(2,1)S(1)}, bf16[4,256,256]{2,1,0:T(8,128)(2,1)S(1)}, u32[]{:S(2)}, u32[]{:S(2)}) collective-permute-start(bf16[4,256,256]{2,1,0:T(8,128)(2,1)S(1)} %copy-done.4), channel_id=1, source_target_pairs={{0,5},{1,16},{2,7},{3,18},{4,1},{5,20},{6,3},{7,22},{8,13},{9,24},... | collective-permute-start | bytes 1572872 | tf_op jit(solution)/shard_map/ppermute | solution.py:327
  32.6 17.9 %collective-permute-start.9 = (bf16[4,256,256]{2,1,0:T(8,128)(2,1)S(1)}, bf16[4,256,256]{2,1,0:T(8,128)(2,1)S(1)}, u32[]{:S(2)}, u32[]{:S(2)}) collective-permute-start(bf16[4,256,256]{2,1,0:T(8,128)(2,1)S(1)} %copy-done.3), channel_id=1, source_target_pairs={{0,7},{1,24},{2,1},{3,26},{4,3},{5,28},{6,5},{7,30},{8,15},{9,0},{... | collective-permute-start | bytes 1572872 | tf_op jit(solution)/shard_map/ppermute | solution.py:327
  44.2 6.3 %copy-start.1 = (bf16[4,256,256]{2,1,0:T(8,128)(2,1)S(1)}, bf16[4,256,256]{2,1,0:T(8,128)(2,1)}, u32[]{:S(2)}) copy-start(bf16[4,256,256]{2,1,0:T(8,128)(2,1)} %get-tuple-element.25.refs_0_) | copy-start | bytes 1572868
  60.4 4.6 %collective-permute-start.10 = (f32[2,8,16]{2,1,0:T(8,128)S(1)}, f32[2,8,16]{2,1,0:T(8,128)S(1)}, u32[]{:S(2)}, u32[]{:S(2)}) collective-permute-start(f32[2,8,16]{2,1,0:T(8,128)S(1)} %slice.152), channel_id=1, source_target_pairs={{0,32},{32,64},{64,96},{96,128},{128,160},{160,192},{192,224},{224... | collective-permute-start | bytes 3080 | tf_op jit(solution)/shard_map/ppermute | solution.py:266
  63.7 4.9 %collective-permute-start.11 = (f32[2,8,16]{2,1,0:T(8,128)S(1)}, f32[2,8,16]{2,1,0:T(8,128)S(1)}, u32[]{:S(2)}, u32[]{:S(2)}) collective-permute-start(f32[2,8,16]{2,1,0:T(8,128)S(1)} %slice.154), channel_id=1, source_target_pairs={{32,0},{64,32},{96,64},{128,96},{160,128},{192,160},{224,192},{0,2... | collective-permute-start | bytes 3080 | tf_op jit(solution)/shard_map/ppermute | solution.py:267
  68.6 2.0 %collective-permute-start.12 = (f32[12,2,16]{2,1,0:T(2,128)S(1)}, f32[12,2,16]{2,1,0:T(2,128)S(1)}, u32[]{:S(2)}, u32[]{:S(2)}) collective-permute-start(f32[12,2,16]{2,1,0:T(2,128)S(1)} %get-tuple-element.78), channel_id=1, source_target_pairs={{0,1},{1,0},{2,3},{3,2},{4,5},{5,4},{6,7},{7,6},{8,9},{9,8},{10,11... | collective-permute-start | bytes 4616 | tf_op jit(solution)/shard_map/ppermute | solution.py:278
  68.7 6.5 %collective-permute-start.13 = (f32[12,2,16]{2,1,0:T(2,128)S(1)}, f32[12,2,16]{2,1,0:T(2,128)S(1)}, u32[]{:S(2)}, u32[]{:S(2)}) collective-permute-start(f32[12,2,16]{2,1,0:T(2,128)S(1)} %get-tuple-element.79), channel_id=1, source_target_pairs={{0,31},{1,2},{2,1},{3,4},{4,3},{5,6},{6,5},{7,8},{8,7},{9,10},{10,... | collective-permute-start | bytes 4616 | tf_op jit(solution)/shard_map/ppermute | solution.py:277
  84.4 20.9 %collective-permute-start.14 = (bf16[4,256,256]{2,1,0:T(8,128)(2,1)}, bf16[4,256,256]{2,1,0:T(8,128)(2,1)S(1)}, u32[]{:S(2)}, u32[]{:S(2)}) collective-permute-start(bf16[4,256,256]{2,1,0:T(8,128)(2,1)} %get-tuple-element.38), channel_id=1, source_target_pairs={{0,2},{1,9},{2,4},{3,11},{4,6},{5,13},{6,0},{7,15},{8,10},{9,17},{... | collective-permute-start | bytes 1572872 | tf_op jit(solution)/shard_map/ppermute | solution.py:327
  84.5 20.8 %collective-permute-start.15 = (bf16[4,256,256]{2,1,0:T(8,128)(2,1)}, bf16[4,256,256]{2,1,0:T(8,128)(2,1)S(1)}, u32[]{:S(2)}, u32[]{:S(2)}) collective-permute-start(bf16[4,256,256]{2,1,0:T(8,128)(2,1)} %get-tuple-element.39), channel_id=1, source_target_pairs={{0,4},{1,17},{2,6},{3,19},{4,0},{5,21},{6,2},{7,23},{8,12},{9,25},... | collective-permute-start | bytes 1572872 | tf_op jit(solution)/shard_map/ppermute | solution.py:327
  84.6 20.9 %collective-permute-start.16 = (bf16[4,256,256]{2,1,0:T(8,128)(2,1)}, bf16[4,256,256]{2,1,0:T(8,128)(2,1)S(1)}, u32[]{:S(2)}, u32[]{:S(2)}) collective-permute-start(bf16[4,256,256]{2,1,0:T(8,128)(2,1)} %get-tuple-element.40), channel_id=1, source_target_pairs={{0,6},{1,25},{2,0},{3,27},{4,2},{5,29},{6,4},{7,31},{8,14},{9,1},{... | collective-permute-start | bytes 1572872 | tf_op jit(solution)/shard_map/ppermute | solution.py:327
  87.7 17.8 %collective-permute-start.17 = (bf16[4,256,256]{2,1,0:T(8,128)(2,1)}, bf16[4,256,256]{2,1,0:T(8,128)(2,1)S(1)}, u32[]{:S(2)}, u32[]{:S(2)}) collective-permute-start(bf16[4,256,256]{2,1,0:T(8,128)(2,1)} %get-tuple-element.41), channel_id=1, source_target_pairs={{0,1},{1,0},{2,3},{3,2},{4,5},{5,4},{6,7},{7,6},{8,9},{9,8},{10,11... | collective-permute-start | bytes 1572872 | tf_op jit(solution)/shard_map/ppermute | solution.py:327
  87.7 18.6 %collective-permute-start.18 = (bf16[4,256,256]{2,1,0:T(8,128)(2,1)}, bf16[4,256,256]{2,1,0:T(8,128)(2,1)S(1)}, u32[]{:S(2)}, u32[]{:S(2)}) collective-permute-start(bf16[4,256,256]{2,1,0:T(8,128)(2,1)} %get-tuple-element.42), channel_id=1, source_target_pairs={{0,9},{1,2},{2,11},{3,4},{4,13},{5,6},{6,15},{7,0},{8,17},{9,10},{... | collective-permute-start | bytes 1572872 | tf_op jit(solution)/shard_map/ppermute | solution.py:327
  105.3 10.3 %collective-permute-start.19 = (bf16[4,256,256]{2,1,0:T(8,128)(2,1)}, bf16[4,256,256]{2,1,0:T(8,128)(2,1)S(1)}, u32[]{:S(2)}, u32[]{:S(2)}) collective-permute-start(bf16[4,256,256]{2,1,0:T(8,128)(2,1)} %get-tuple-element.43), channel_id=1, source_target_pairs={{0,17},{1,4},{2,19},{3,6},{4,21},{5,0},{6,23},{7,2},{8,25},{9,12},... | collective-permute-start | bytes 1572872 | tf_op jit(solution)/shard_map/ppermute | solution.py:327
  105.3 13.1 %collective-permute-start.20 = (bf16[4,256,256]{2,1,0:T(8,128)(2,1)}, bf16[4,256,256]{2,1,0:T(8,128)(2,1)}, u32[]{:S(2)}, u32[]{:S(2)}) collective-permute-start(bf16[4,256,256]{2,1,0:T(8,128)(2,1)} %get-tuple-element.44), channel_id=1, source_target_pairs={{0,25},{1,6},{2,27},{3,0},{4,29},{5,2},{6,31},{7,4},{8,1},{9,14},{... | collective-permute-start | bytes 1572872 | tf_op jit(solution)/shard_map/ppermute | solution.py:327
  118.4 1.0 copy-start
  121.7 10.6 %collective-permute-start.21 = (bf16[3,256,256]{2,1,0:T(8,128)(2,1)S(1)}, bf16[3,256,256]{2,1,0:T(8,128)(2,1)S(1)}, u32[]{:S(2)}, u32[]{:S(2)}) collective-permute-start(bf16[3,256,256]{2,1,0:T(8,128)(2,1)S(1)} %add_up.5), channel_id=1, source_target_pairs={{0,16},{1,5},{2,18},{3,7},{4,20},{5,1},{6,22},{7,3},{8,24},{9,13},... | collective-permute-start | bytes 1179656 | tf_op jit(solution)/shard_map/ppermute | solution.py:327
  124.1 11.2 %collective-permute-start.22 = (bf16[3,256,256]{2,1,0:T(8,128)(2,1)S(1)}, bf16[3,256,256]{2,1,0:T(8,128)(2,1)S(1)}, u32[]{:S(2)}, u32[]{:S(2)}) collective-permute-start(bf16[3,256,256]{2,1,0:T(8,128)(2,1)S(1)} %add_up.6), channel_id=1, source_target_pairs={{0,8},{1,3},{2,10},{3,5},{4,12},{5,7},{6,14},{7,1},{8,16},{9,11},{... | collective-permute-start | bytes 1179656 | tf_op jit(solution)/shard_map/ppermute | solution.py:327
  126.8 9.3 %collective-permute-start.23 = (bf16[3,256,256]{2,1,0:T(8,128)(2,1)S(1)}, bf16[3,256,256]{2,1,0:T(8,128)(2,1)S(1)}, u32[]{:S(2)}, u32[]{:S(2)}) collective-permute-start(bf16[3,256,256]{2,1,0:T(8,128)(2,1)S(1)} %add_up.7), channel_id=1, source_target_pairs={{0,24},{1,7},{2,26},{3,1},{4,28},{5,3},{6,30},{7,5},{8,0},{9,15},{... | collective-permute-start | bytes 1179656 | tf_op jit(solution)/shard_map/ppermute | solution.py:327

commit v7 on v6

--- a/solution.py
+++ b/solution.py
@@ -147,7 +147,7 @@
             pltpu.VMEM((count, both, points), jnp.bfloat16),
             pltpu.SemaphoreType.DMA((2, count)),
         ],
-        compiler_params=params(48),
+        compiler_params=params(52),
         name="collocate",
     )(places, *blocks, *tables)
 
@@ -328,9 +328,8 @@
 
 
 def turns(side):
-    near = [1, side - 1]
-    far = [k for k in range(side) if k not in (0, 1, side - 1)]
-    return [(o, k) for o in (0, 1) for k in near] + [(o, k) for k in far for o in (0, 1)] + [(1, 0)]
+    far = [(o, k) for k in range(side) if k not in (0, 1, side - 1) for o in (0, 1)]
+    return [(1, 0), (0, side - 1), (0, 1)] + far + [(1, 1), (1, side - 1)]
 
 
 def order(side):

time: 138 us -> 136 us (0.986)
  Pallas kernels: 54.7 us -> 51.9 us
    pallas_call x1, Pallas kernels: 9.74 us -> 7.6 us  [collocate(): pl.pallas_call(kernel, out_shape=jax.ShapeDtypeStruct((8, points), jnp.fl...]
    unnamed x13 -> x21, local copies, waits for them, and re-layouts: 1.84 us -> 3.1 us
where the time goes in v7:
time: 136 us; the launch traced here: 135 us
  Pallas kernels  51.9 us (38%)
  waiting for transfers between devices  43.4 us (32%)
  starting transfers between devices  29.8 us (22%)
  local copies, waits for them, and re-layouts  6.98 us (5%)
  other arithmetic  2.59 us (2%)
    ppermute x20, waiting for transfers between devices, moved(): return lax.ppermute(value, BRICK, pairs)  33.6 us
    ppermute x20, starting transfers between devices, moved(): return lax.ppermute(value, BRICK, pairs)  25.2 us
    pallas_call x4, Pallas kernels, gather_tables(): pl.pallas_call(kernel, out_shape=pltpu.HBM((count, width, points), jnp.bf...  25.1 us
    pallas_call x4, Pallas kernels, add_up(): pl.pallas_call(kernel, out_shape=jax.ShapeDtypeStruct((own_count, rows, c...  8.43 us
    pallas_call x1, Pallas kernels, integrate(): pl.pallas_call(kernel, out_shape=[pltpu.HBM((inner, width, width), jnp.bf...  8.37 us
    pallas_call x1, Pallas kernels, collocate(): pl.pallas_call(kernel, out_shape=jax.ShapeDtypeStruct((8, points), jnp.fl...  7.6 us
    ppermute x1, waiting for transfers between devices, extended_pairs(): far = lax.ppermute(jnp.where(odd, high, low), axis, between)  4.91 us
    ppermute x1, waiting for transfers between devices, extended_ring(): above = lax.ppermute(low, axis, backward)  3.65 us
  transfers between devices with their start and end apart: 24, of which 9 were waited for; matrix products, arithmetic and copies ran while one was open for 4% of the time, Pallas kernels for 23%

profile of v7, /device:TPU:96, one launch (start us, length us, event | category | flops | bytes accessed | tf_op | source)
XLA Modules:
  0.0 135.0 jit_solution(4158052029370681315)
XLA Ops:
  0.0 1.5 %collective-permute-start = (bf16[3,256,256]{2,1,0:T(8,128)(2,1)}, bf16[3,256,256]{2,1,0:T(8,128)(2,1)S(1)}, u32[]{:S(2)}, u32[]{:S(2)}) collective-permute-start(bf16[3,256,256]{2,1,0:T(8,128)(2,1)} %refs_0_.1), channel_id=1, source_target_pairs={{0,8},{1,3},{2,10},{3,5},{4,12},{5,7},{6,14},{7,1},{8,16},{9,11},{... | collective-permute-start | bytes 1179656 | tf_op jit(solution)/shard_map/ppermute | solution.py:327
  1.5 2.7 %collective-permute-start.1 = (bf16[3,256,256]{2,1,0:T(8,128)(2,1)}, bf16[3,256,256]{2,1,0:T(8,128)(2,1)S(1)}, u32[]{:S(2)}, u32[]{:S(2)}) collective-permute-start(bf16[3,256,256]{2,1,0:T(8,128)(2,1)} %refs_0_.1), channel_id=1, source_target_pairs={{0,16},{1,5},{2,18},{3,7},{4,20},{5,1},{6,22},{7,3},{8,24},{9,13},... | collective-permute-start | bytes 1179656 | tf_op jit(solution)/shard_map/ppermute | solution.py:327
  4.2 1.4 %collective-permute-start.2 = (bf16[3,256,256]{2,1,0:T(8,128)(2,1)}, bf16[3,256,256]{2,1,0:T(8,128)(2,1)S(1)}, u32[]{:S(2)}, u32[]{:S(2)}) collective-permute-start(bf16[3,256,256]{2,1,0:T(8,128)(2,1)} %refs_0_.1), channel_id=1, source_target_pairs={{0,24},{1,7},{2,26},{3,1},{4,28},{5,3},{6,30},{7,5},{8,0},{9,15},{... | collective-permute-start | bytes 1179656 | tf_op jit(solution)/shard_map/ppermute | solution.py:327
  5.7 0.8 copy.20
  6.5 0.1 copy.23
  6.6 0.1 copy.24
  6.7 0.1 select_reduce_fusion
  6.8 0.1 copy.25.numbers_ref
  6.9 0.8 fusion.19
  7.7 2.9 %copy.26 = bf16[1024,1024]{0,1:T(8,128)(2,1)S(1)} copy(bf16[1024,1024]{1,0:T(8,128)(2,1)} %bitcast.18) | data formatting | bytes 4194304 | tf_op jit(solution)/shard_map/reshape | solution.py:360
  10.6 0.1 pad_add_fusion.4.bricks_ref
  10.7 6.2 %gather_tables.4.refs_8_.refs_0_ = bf16[4,512,1024]{2,1,0:T(8,128)(2,1)} custom-call(s32[4,1,512]{2,1,0:T(1,128)S(1)} %copy.27.index_ref, bf16[1024,1024]{1,0:T(8,128)(2,1)S(1)} %bitcast.14), custom_call_target="tpu_custom_call" | custom-call | flops 4294967296 | bytes 4194304 | tf_op jit(solution)/shard_map/gather_tables/pallas_call | solution.py:83
  17.0 2.4 %select_blocks.1 = (bf16[4,256,256]{2,1,0:T(8,128)(2,1)}, bf16[4,256,256]{2,1,0:T(8,128)(2,1)}, bf16[4,256,256]{2,1,0:T(8,128)(2,1)}, bf16[4,256,256]{2,1,0:T(8,...) custom-call(s32[8]{0:T(128)S(1)} %pad_add_fusion.4.bricks_ref, ...), custom_call_target="tpu_custom_call" | custom-call | tf_op jit(solution)/shard_map/select_blocks/pallas_call | solution.py:50
  19.3 0.1 collective-permute-start.6
  19.4 1.6 %collective-permute-start.3 = (bf16[4,256,256]{2,1,0:T(8,128)(2,1)}, bf16[4,256,256]{2,1,0:T(8,128)(2,1)S(1)}, u32[]{:S(2)}, u32[]{:S(2)}) collective-permute-start(bf16[4,256,256]{2,1,0:T(8,128)(2,1)} %get-tuple-element.26), channel_id=1, source_target_pairs={{0,2},{1,9},{2,4},{3,11},{4,6},{5,13},{6,0},{7,15},{8,10},{9,17},{... | collective-permute-start | bytes 1572872 | tf_op jit(solution)/shard_map/ppermute | solution.py:327
  21.1 3.2 %collective-permute-start.4 = (bf16[4,256,256]{2,1,0:T(8,128)(2,1)}, bf16[4,256,256]{2,1,0:T(8,128)(2,1)S(1)}, u32[]{:S(2)}, u32[]{:S(2)}) collective-permute-start(bf16[4,256,256]{2,1,0:T(8,128)(2,1)} %get-tuple-element.27), channel_id=1, source_target_pairs={{0,4},{1,17},{2,6},{3,19},{4,0},{5,21},{6,2},{7,23},{8,12},{9,25},... | collective-permute-start | bytes 1572872 | tf_op jit(solution)/shard_map/ppermute | solution.py:327
  24.3 1.2 collective-permute-start.5
  25.5 6.4 %gather_tables.5.refs_9_.refs_1_ = bf16[4,512,1024]{2,1,0:T(8,128)(2,1)} custom-call(s32[4,1,512]{2,1,0:T(1,128)S(1)} %copy.28.index_ref, bf16[1024,1024]{1,0:T(8,128)(2,1)S(1)} %bitcast.15), custom_call_target="tpu_custom_call" | custom-call | flops 4294967296 | bytes 4194304 | tf_op jit(solution)/shard_map/gather_tables/pallas_call | solution.py:83
  31.9 0.7 collective-permute-start.8
  32.6 5.5 %collective-permute-start.9 = (bf16[4,256,256]{2,1,0:T(8,128)(2,1)S(1)}, bf16[4,256,256]{2,1,0:T(8,128)(2,1)S(1)}, u32[]{:S(2)}, u32[]{:S(2)}) collective-permute-start(bf16[4,256,256]{2,1,0:T(8,128)(2,1)S(1)} %copy-done.7), channel_id=1, source_target_pairs={{0,7},{1,24},{2,1},{3,26},{4,3},{5,28},{6,5},{7,30},{8,15},{9,0},{... | collective-permute-start | bytes 1572872 | tf_op jit(solution)/shard_map/ppermute | solution.py:327
  38.1 6.3 %gather_tables.6.refs_10_.refs_2_ = bf16[4,512,1024]{2,1,0:T(8,128)(2,1)} custom-call(s32[4,1,512]{2,1,0:T(1,128)S(1)} %copy.29.index_ref, bf16[1024,1024]{1,0:T(8,128)(2,1)S(1)} %bitcast.16), custom_call_target="tpu_custom_call" | custom-call | flops 4294967296 | bytes 4194304 | tf_op jit(solution)/shard_map/gather_tables/pallas_call | solution.py:83
  44.4 6.2 %gather_tables.7.refs_11_.refs_3_ = bf16[4,512,1024]{2,1,0:T(8,128)(2,1)} custom-call(s32[4,1,512]{2,1,0:T(1,128)S(1)} %slice.148.index_ref, bf16[1024,1024]{1,0:T(8,128)(2,1)S(1)} %bitcast.17), custom_call_target="tpu_custom_call" | custom-call | flops 4294967296 | bytes 4194304 | tf_op jit(solution)/shard_map/gather_tables/pallas_call | solution.py:83
  50.7 0.7 copy-done.3
  51.5 0.2 copy-done.4
  51.7 0.2 copy-done.5
  51.9 0.1 copy-done.6
  52.0 7.6 %collocate.1 = f32[8,1024]{1,0:T(8,128)S(1)} custom-call(s32[2,16]{1,0:T(2,128)S(1)} %pad_add_fusion.2.places_ref, bf16[4,256,256]{2,1,0:T(8,128)(2,1)S(1)} %copy-done.1, bf16[4,256,256]{2,1,0:T(8,128)(2,1)S(1)} %collective-permute-done.3.refs_1_, bf16[4,256,256]{2,1,0:T(8,128)(2,1)S(1)} %collective-permute-done.4.refs_2_, bf16[4,256,256]{2,1,0:T(8,128)(2,1)} %copy-done.3, ...), custom_call_target="tpu_custom_call" | custom-call | tf_op jit(solution)/shard_map/collocate/pallas_call | solution.py:140
  59.6 0.1 slice.152
  59.7 2.9 %collective-permute-start.10 = (f32[2,8,16]{2,1,0:T(8,128)S(1)}, f32[2,8,16]{2,1,0:T(8,128)S(1)}, u32[]{:S(2)}, u32[]{:S(2)}) collective-permute-start(f32[2,8,16]{2,1,0:T(8,128)S(1)} %slice.152), channel_id=1, source_target_pairs={{0,32},{32,64},{64,96},{96,128},{128,160},{160,192},{192,224},{224... | collective-permute-start | bytes 3080 | tf_op jit(solution)/shard_map/ppermute | solution.py:266
  62.6 0.1 reshape.114
  62.7 0.1 slice.154
  62.8 1.2 collective-permute-done.10
  64.0 3.7 %collective-permute-done.11 = f32[2,8,16]{2,1,0:T(8,128)S(1)} collective-permute-done((f32[2,8,16]{2,1,0:T(8,128)S(1)}, f32[2,8,16]{2,1,0:T(8,128)S(1)}, u32[]{:S(2)}, u32[]{:S(2)}) %collective-permute-start.11) | collective-permute-done | bytes 1056 | tf_op jit(solution)/shard_map/ppermute | solution.py:267
  67.7 0.1 collective-permute-start.12
  67.8 1.6 %collective-permute-start.13 = (f32[12,2,16]{2,1,0:T(2,128)S(1)}, f32[12,2,16]{2,1,0:T(2,128)S(1)}, u32[]{:S(2)}, u32[]{:S(2)}) collective-permute-start(f32[12,2,16]{2,1,0:T(2,128)S(1)} %get-tuple-element.79), channel_id=1, source_target_pairs={{0,31},{1,2},{2,1},{3,4},{4,3},{5,6},{6,5},{7,8},{8,7},{9,10},{10,... | collective-permute-start | bytes 4616 | tf_op jit(solution)/shard_map/ppermute | solution.py:277
  69.4 4.9 %collective-permute-done.13 = f32[12,2,16]{2,1,0:T(2,128)S(1)} collective-permute-done((f32[12,2,16]{2,1,0:T(2,128)S(1)}, f32[12,2,16]{2,1,0:T(2,128)S(1)}, u32[]{:S(2)}, u32[]{:S(2)}) %collective-permute-start.13) | collective-permute-done | bytes 1568 | tf_op jit(solution)/shard_map/ppermute | solution.py:277
  74.3 0.1 fusion.46
  74.4 0.1 fusion.47
  74.5 0.1 fusion.42
  74.7 0.1 fusion.48
  74.7 0.1 fusion.49
  74.9 0.1 fusion.9
  75.0 0.1 mul.148.scaled_ref
  75.1 8.4 %integrate.1 = (bf16[4,256,256]{2,1,0:T(8,128)(2,1)}, bf16[4,256,256]{2,1,0:T(8,128)(2,1)}, bf16[4,256,256]{2,1,0:T(8,128)(2,1)}, bf16[4,256,256]{2,1,0:T(8,128)...) custom-call(s32[2,16]{1,0:T(2,128)S(1)} %pad_add_fusion.1.places_ref, ...), custom_call_target="tpu_custom_call" | custom-call | tf_op jit(solution)/shard_map/integrate/pallas_call | solution.py:196
  83.5 0.1 collective-permute-start.14
  83.6 0.1 collective-permute-start.15
  83.7 3.1 %collective-permute-start.16 = (bf16[4,256,256]{2,1,0:T(8,128)(2,1)}, bf16[4,256,256]{2,1,0:T(8,128)(2,1)S(1)}, u32[]{:S(2)}, u32[]{:S(2)}) collective-permute-start(bf16[4,256,256]{2,1,0:T(8,128)(2,1)} %get-tuple-element.40), channel_id=1, source_target_pairs={{0,6},{1,25},{2,0},{3,27},{4,2},{5,29},{6,4},{7,31},{8,14},{9,1},{... | collective-permute-start | bytes 1572872 | tf_op jit(solution)/shard_map/ppermute | solution.py:327
  86.8 17.1 %collective-permute-done.14.refs_1_ = bf16[4,256,256]{2,1,0:T(8,128)(2,1)S(1)} collective-permute-done((bf16[4,256,256]{2,1,0:T(8,128)(2,1)}, bf16[4,256,256]{2,1,0:T(8,128)(2,1)S(1)}, u32[]{:S(2)}, u32[]{:S(2)}) %collective-permute-start.14) | collective-permute-done | bytes 524320 | tf_op jit(solution)/shard_map/ppermute | solution.py:327
  104.0 0.1 copy.30.numbers_ref
  104.1 0.1 pad_add_fusion.3.bricks_ref
  104.1 1.2 collective-permute-done.18.refs_5_
  105.4 8.9 %collective-permute-done.19.refs_6_ = bf16[4,256,256]{2,1,0:T(8,128)(2,1)S(1)} collective-permute-done((bf16[4,256,256]{2,1,0:T(8,128)(2,1)}, bf16[4,256,256]{2,1,0:T(8,128)(2,1)S(1)}, u32[]{:S(2)}, u32[]{:S(2)}) %collective-permute-start.19) | collective-permute-done | bytes 524320 | tf_op jit(solution)/shard_map/ppermute | solution.py:327
  114.3 2.7 %collective-permute-done.20.refs_7_ = bf16[4,256,256]{2,1,0:T(8,128)(2,1)} collective-permute-done((bf16[4,256,256]{2,1,0:T(8,128)(2,1)}, bf16[4,256,256]{2,1,0:T(8,128)(2,1)}, u32[]{:S(2)}, u32[]{:S(2)}) %collective-permute-start.20) | collective-permute-done | bytes 524320 | tf_op jit(solution)/shard_map/ppermute | solution.py:327
  117.0 1.0 copy-done
  118.1 2.1 %add_up.5 = bf16[3,256,256]{2,1,0:T(8,128)(2,1)S(1)} custom-call(s32[8]{0:T(128)S(1)} %pad_add_fusion.3.bricks_ref, s32[32,4]{1,0:T(8,128)S(1)} %copy.30.numbers_ref, bf16[4,256,256]{2,1,0:T(8,128)(2,1)S(1)} %copy-done, bf16[4,256,256]{2,1,0:T(8,128)(2,1)S(1)} %collective-permute-done.14.refs_1_, bf16[4,256,256]{2,1,0:T(8,128)(2,1)S(1)} %collective-permute-done.15.refs_2_, ...), custom_call_target="tpu_custom_call" | custom-call | tf_op jit(solution)/shard_map/add_up/pallas_call | solution.py:238
  120.2 0.1 collective-permute-start.21
  120.3 1.7 %add_up.6 = bf16[3,256,256]{2,1,0:T(8,128)(2,1)S(1)} custom-call(s32[8]{0:T(128)S(1)} %pad_add_fusion.3.bricks_ref, s32[32,4]{1,0:T(8,128)S(1)} %copy.30.numbers_ref, bf16[4,256,256]{2,1,0:T(8,128)(2,1)S(1)} %copy-done, bf16[4,256,256]{2,1,0:T(8,128)(2,1)S(1)} %collective-permute-done.14.refs_1_, bf16[4,256,256]{2,1,0:T(8,128)(2,1)S(1)} %collective-permute-done.15.refs_2_, ...), custom_call_target="tpu_custom_call" | custom-call | tf_op jit(solution)/shard_map/add_up/pallas_call | solution.py:238
  122.0 0.1 collective-permute-start.22
  122.1 1.5 %add_up.7 = bf16[3,256,256]{2,1,0:T(8,128)(2,1)S(1)} custom-call(s32[8]{0:T(128)S(1)} %pad_add_fusion.3.bricks_ref, s32[32,4]{1,0:T(8,128)S(1)} %copy.30.numbers_ref, bf16[4,256,256]{2,1,0:T(8,128)(2,1)S(1)} %copy-done, bf16[4,256,256]{2,1,0:T(8,128)(2,1)S(1)} %collective-permute-done.14.refs_1_, bf16[4,256,256]{2,1,0:T(8,128)(2,1)S(1)} %collective-permute-done.15.refs_2_, ...), custom_call_target="tpu_custom_call" | custom-call | tf_op jit(solution)/shard_map/add_up/pallas_call | solution.py:238
  123.6 3.7 %collective-permute-start.23 = (bf16[3,256,256]{2,1,0:T(8,128)(2,1)S(1)}, bf16[3,256,256]{2,1,0:T(8,128)(2,1)S(1)}, u32[]{:S(2)}, u32[]{:S(2)}) collective-permute-start(bf16[3,256,256]{2,1,0:T(8,128)(2,1)S(1)} %add_up.7), channel_id=1, source_target_pairs={{0,24},{1,7},{2,26},{3,1},{4,28},{5,3},{6,30},{7,5},{8,0},{9,15},{... | collective-permute-start | bytes 1179656 | tf_op jit(solution)/shard_map/ppermute | solution.py:327
  127.3 3.1 %add_up.4 = f32[3,256,256]{2,1,0:T(8,128)S(1)} custom-call(s32[8]{0:T(128)S(1)} %pad_add_fusion.3.bricks_ref, s32[32,4]{1,0:T(8,128)S(1)} %copy.30.numbers_ref, bf16[4,256,256]{2,1,0:T(8,128)(2,1)S(1)} %copy-done, bf16[4,256,256]{2,1,0:T(8,128)(2,1)S(1)} %collective-permute-done.14.refs_1_, bf16[4,256,256]{2,1,0:T(8,128)(2,1)S(1)} %collective-permute-done.15.refs_2_, ...), custom_call_target="tpu_custom_call" | custom-call | tf_op jit(solution)/shard_map/add_up/pallas_call | solution.py:238
  130.4 3.4 %collective-permute-done.22 = bf16[3,256,256]{2,1,0:T(8,128)(2,1)S(1)} collective-permute-done((bf16[3,256,256]{2,1,0:T(8,128)(2,1)S(1)}, bf16[3,256,256]{2,1,0:T(8,128)(2,1)S(1)}, u32[]{:S(2)}, u32[]{:S(2)}) %collective-permute-start.22) | collective-permute-done | bytes 393248 | tf_op jit(solution)/shard_map/ppermute | solution.py:327
  133.8 0.2 collective-permute-done.23
  134.0 1.0 convert_add_fusion
  (60 shorter events, 0.4 us)
Async XLA Ops:
  0.0 17.0 %collective-permute-start = (bf16[3,256,256]{2,1,0:T(8,128)(2,1)}, bf16[3,256,256]{2,1,0:T(8,128)(2,1)S(1)}, u32[]{:S(2)}, u32[]{:S(2)}) collective-permute-start(bf16[3,256,256]{2,1,0:T(8,128)(2,1)} %refs_0_.1), channel_id=1, source_target_pairs={{0,8},{1,3},{2,10},{3,5},{4,12},{5,7},{6,14},{7,1},{8,16},{9,11},{... | collective-permute-start | bytes 1179656 | tf_op jit(solution)/shard_map/ppermute | solution.py:327
  1.5 15.5 %collective-permute-start.1 = (bf16[3,256,256]{2,1,0:T(8,128)(2,1)}, bf16[3,256,256]{2,1,0:T(8,128)(2,1)S(1)}, u32[]{:S(2)}, u32[]{:S(2)}) collective-permute-start(bf16[3,256,256]{2,1,0:T(8,128)(2,1)} %refs_0_.1), channel_id=1, source_target_pairs={{0,16},{1,5},{2,18},{3,7},{4,20},{5,1},{6,22},{7,3},{8,24},{9,13},... | collective-permute-start | bytes 1179656 | tf_op jit(solution)/shard_map/ppermute | solution.py:327
  4.2 12.8 %collective-permute-start.2 = (bf16[3,256,256]{2,1,0:T(8,128)(2,1)}, bf16[3,256,256]{2,1,0:T(8,128)(2,1)S(1)}, u32[]{:S(2)}, u32[]{:S(2)}) collective-permute-start(bf16[3,256,256]{2,1,0:T(8,128)(2,1)} %refs_0_.1), channel_id=1, source_target_pairs={{0,24},{1,7},{2,26},{3,1},{4,28},{5,3},{6,30},{7,5},{8,0},{9,15},{... | collective-permute-start | bytes 1179656 | tf_op jit(solution)/shard_map/ppermute | solution.py:327
  10.7 6.3 %copy-start.2 = (bf16[3,256,256]{2,1,0:T(8,128)(2,1)S(1)}, bf16[3,256,256]{2,1,0:T(8,128)(2,1)}, u32[]{:S(2)}) copy-start(bf16[3,256,256]{2,1,0:T(8,128)(2,1)} %refs_0_.1) | copy-start | bytes 1179652
  19.3 12.5 %collective-permute-start.6 = (bf16[4,256,256]{2,1,0:T(8,128)(2,1)}, bf16[4,256,256]{2,1,0:T(8,128)(2,1)}, u32[]{:S(2)}, u32[]{:S(2)}) collective-permute-start(bf16[4,256,256]{2,1,0:T(8,128)(2,1)} %get-tuple-element.30), channel_id=1, source_target_pairs={{0,1},{1,0},{2,3},{3,2},{4,5},{5,4},{6,7},{7,6},{8,9},{9,8},{10,11... | collective-permute-start | bytes 1572872 | tf_op jit(solution)/shard_map/ppermute | solution.py:327
  19.4 13.2 %collective-permute-start.3 = (bf16[4,256,256]{2,1,0:T(8,128)(2,1)}, bf16[4,256,256]{2,1,0:T(8,128)(2,1)S(1)}, u32[]{:S(2)}, u32[]{:S(2)}) collective-permute-start(bf16[4,256,256]{2,1,0:T(8,128)(2,1)} %get-tuple-element.26), channel_id=1, source_target_pairs={{0,2},{1,9},{2,4},{3,11},{4,6},{5,13},{6,0},{7,15},{8,10},{9,17},{... | collective-permute-start | bytes 1572872 | tf_op jit(solution)/shard_map/ppermute | solution.py:327
  21.1 29.5 %collective-permute-start.4 = (bf16[4,256,256]{2,1,0:T(8,128)(2,1)}, bf16[4,256,256]{2,1,0:T(8,128)(2,1)S(1)}, u32[]{:S(2)}, u32[]{:S(2)}) collective-permute-start(bf16[4,256,256]{2,1,0:T(8,128)(2,1)} %get-tuple-element.27), channel_id=1, source_target_pairs={{0,4},{1,17},{2,6},{3,19},{4,0},{5,21},{6,2},{7,23},{8,12},{9,25},... | collective-permute-start | bytes 1572872 | tf_op jit(solution)/shard_map/ppermute | solution.py:327
  24.3 26.3 %collective-permute-start.5 = (bf16[4,256,256]{2,1,0:T(8,128)(2,1)}, bf16[4,256,256]{2,1,0:T(8,128)(2,1)S(1)}, u32[]{:S(2)}, u32[]{:S(2)}) collective-permute-start(bf16[4,256,256]{2,1,0:T(8,128)(2,1)} %get-tuple-element.28), channel_id=1, source_target_pairs={{0,6},{1,25},{2,0},{3,27},{4,2},{5,29},{6,4},{7,31},{8,14},{9,1},{... | collective-permute-start | bytes 1572872 | tf_op jit(solution)/shard_map/ppermute | solution.py:327
  25.5 6.4 %copy-start.8 = (bf16[4,256,256]{2,1,0:T(8,128)(2,1)S(1)}, bf16[4,256,256]{2,1,0:T(8,128)(2,1)}, u32[]{:S(2)}) copy-start(bf16[4,256,256]{2,1,0:T(8,128)(2,1)} %get-tuple-element.32) | copy-start | bytes 1572868
  25.5 7.1 %copy-start.7 = (bf16[4,256,256]{2,1,0:T(8,128)(2,1)S(1)}, bf16[4,256,256]{2,1,0:T(8,128)(2,1)}, u32[]{:S(2)}) copy-start(bf16[4,256,256]{2,1,0:T(8,128)(2,1)} %get-tuple-element.33) | copy-start | bytes 1572868
  25.5 25.1 %collective-permute-start.7 = (bf16[4,256,256]{2,1,0:T(8,128)(2,1)}, bf16[4,256,256]{2,1,0:T(8,128)(2,1)S(1)}, u32[]{:S(2)}, u32[]{:S(2)}) collective-permute-start(bf16[4,256,256]{2,1,0:T(8,128)(2,1)} %get-tuple-element.31), channel_id=1, source_target_pairs={{0,3},{1,8},{2,5},{3,10},{4,7},{5,12},{6,1},{7,14},{8,11},{9,16},{... | collective-permute-start | bytes 1572872 | tf_op jit(solution)/shard_map/ppermute | solution.py:327
  31.9 18.8 %collective-permute-start.8 = (bf16[4,256,256]{2,1,0:T(8,128)(2,1)S(1)}, bf16[4,256,256]{2,1,0:T(8,128)(2,1)S(1)}, u32[]{:S(2)}, u32[]{:S(2)}) collective-permute-start(bf16[4,256,256]{2,1,0:T(8,128)(2,1)S(1)} %copy-done.8), channel_id=1, source_target_pairs={{0,5},{1,16},{2,7},{3,18},{4,1},{5,20},{6,3},{7,22},{8,13},{9,24},... | collective-permute-start | bytes 1572872 | tf_op jit(solution)/shard_map/ppermute | solution.py:327
  32.6 18.1 %collective-permute-start.9 = (bf16[4,256,256]{2,1,0:T(8,128)(2,1)S(1)}, bf16[4,256,256]{2,1,0:T(8,128)(2,1)S(1)}, u32[]{:S(2)}, u32[]{:S(2)}) collective-permute-start(bf16[4,256,256]{2,1,0:T(8,128)(2,1)S(1)} %copy-done.7), channel_id=1, source_target_pairs={{0,7},{1,24},{2,1},{3,26},{4,3},{5,28},{6,5},{7,30},{8,15},{9,0},{... | collective-permute-start | bytes 1572872 | tf_op jit(solution)/shard_map/ppermute | solution.py:327
  44.4 7.6 %copy-start.1 = (bf16[4,256,256]{2,1,0:T(8,128)(2,1)S(1)}, bf16[4,256,256]{2,1,0:T(8,128)(2,1)}, u32[]{:S(2)}) copy-start(bf16[4,256,256]{2,1,0:T(8,128)(2,1)} %get-tuple-element.25.refs_0_) | copy-start | bytes 1572868
  50.7 0.8 copy-start.3
  50.7 1.0 copy-start.4
  50.7 1.1 copy-start.5
  50.7 1.3 copy-start.6
  59.7 4.3 %collective-permute-start.10 = (f32[2,8,16]{2,1,0:T(8,128)S(1)}, f32[2,8,16]{2,1,0:T(8,128)S(1)}, u32[]{:S(2)}, u32[]{:S(2)}) collective-permute-start(f32[2,8,16]{2,1,0:T(8,128)S(1)} %slice.152), channel_id=1, source_target_pairs={{0,32},{32,64},{64,96},{96,128},{128,160},{160,192},{192,224},{224... | collective-permute-start | bytes 3080 | tf_op jit(solution)/shard_map/ppermute | solution.py:266
  62.8 4.9 %collective-permute-start.11 = (f32[2,8,16]{2,1,0:T(8,128)S(1)}, f32[2,8,16]{2,1,0:T(8,128)S(1)}, u32[]{:S(2)}, u32[]{:S(2)}) collective-permute-start(f32[2,8,16]{2,1,0:T(8,128)S(1)} %slice.154), channel_id=1, source_target_pairs={{32,0},{64,32},{96,64},{128,96},{160,128},{192,160},{224,192},{0,2... | collective-permute-start | bytes 3080 | tf_op jit(solution)/shard_map/ppermute | solution.py:267
  67.7 1.7 %collective-permute-start.12 = (f32[12,2,16]{2,1,0:T(2,128)S(1)}, f32[12,2,16]{2,1,0:T(2,128)S(1)}, u32[]{:S(2)}, u32[]{:S(2)}) collective-permute-start(f32[12,2,16]{2,1,0:T(2,128)S(1)} %get-tuple-element.78), channel_id=1, source_target_pairs={{0,1},{1,0},{2,3},{3,2},{4,5},{5,4},{6,7},{7,6},{8,9},{9,8},{10,11... | collective-permute-start | bytes 4616 | tf_op jit(solution)/shard_map/ppermute | solution.py:278
  67.8 6.5 %collective-permute-start.13 = (f32[12,2,16]{2,1,0:T(2,128)S(1)}, f32[12,2,16]{2,1,0:T(2,128)S(1)}, u32[]{:S(2)}, u32[]{:S(2)}) collective-permute-start(f32[12,2,16]{2,1,0:T(2,128)S(1)} %get-tuple-element.79), channel_id=1, source_target_pairs={{0,31},{1,2},{2,1},{3,4},{4,3},{5,6},{6,5},{7,8},{8,7},{9,10},{10,... | collective-permute-start | bytes 4616 | tf_op jit(solution)/shard_map/ppermute | solution.py:277
  83.5 20.5 %collective-permute-start.14 = (bf16[4,256,256]{2,1,0:T(8,128)(2,1)}, bf16[4,256,256]{2,1,0:T(8,128)(2,1)S(1)}, u32[]{:S(2)}, u32[]{:S(2)}) collective-permute-start(bf16[4,256,256]{2,1,0:T(8,128)(2,1)} %get-tuple-element.38), channel_id=1, source_target_pairs={{0,2},{1,9},{2,4},{3,11},{4,6},{5,13},{6,0},{7,15},{8,10},{9,17},{... | collective-permute-start | bytes 1572872 | tf_op jit(solution)/shard_map/ppermute | solution.py:327
  83.6 20.4 %collective-permute-start.15 = (bf16[4,256,256]{2,1,0:T(8,128)(2,1)}, bf16[4,256,256]{2,1,0:T(8,128)(2,1)S(1)}, u32[]{:S(2)}, u32[]{:S(2)}) collective-permute-start(bf16[4,256,256]{2,1,0:T(8,128)(2,1)} %get-tuple-element.39), channel_id=1, source_target_pairs={{0,4},{1,17},{2,6},{3,19},{4,0},{5,21},{6,2},{7,23},{8,12},{9,25},... | collective-permute-start | bytes 1572872 | tf_op jit(solution)/shard_map/ppermute | solution.py:327
  83.7 20.5 %collective-permute-start.16 = (bf16[4,256,256]{2,1,0:T(8,128)(2,1)}, bf16[4,256,256]{2,1,0:T(8,128)(2,1)S(1)}, u32[]{:S(2)}, u32[]{:S(2)}) collective-permute-start(bf16[4,256,256]{2,1,0:T(8,128)(2,1)} %get-tuple-element.40), channel_id=1, source_target_pairs={{0,6},{1,25},{2,0},{3,27},{4,2},{5,29},{6,4},{7,31},{8,14},{9,1},{... | collective-permute-start | bytes 1572872 | tf_op jit(solution)/shard_map/ppermute | solution.py:327
  86.8 17.3 %collective-permute-start.17 = (bf16[4,256,256]{2,1,0:T(8,128)(2,1)}, bf16[4,256,256]{2,1,0:T(8,128)(2,1)S(1)}, u32[]{:S(2)}, u32[]{:S(2)}) collective-permute-start(bf16[4,256,256]{2,1,0:T(8,128)(2,1)} %get-tuple-element.41), channel_id=1, source_target_pairs={{0,1},{1,0},{2,3},{3,2},{4,5},{5,4},{6,7},{7,6},{8,9},{9,8},{10,11... | collective-permute-start | bytes 1572872 | tf_op jit(solution)/shard_map/ppermute | solution.py:327
  86.8 18.6 %collective-permute-start.18 = (bf16[4,256,256]{2,1,0:T(8,128)(2,1)}, bf16[4,256,256]{2,1,0:T(8,128)(2,1)S(1)}, u32[]{:S(2)}, u32[]{:S(2)}) collective-permute-start(bf16[4,256,256]{2,1,0:T(8,128)(2,1)} %get-tuple-element.42), channel_id=1, source_target_pairs={{0,9},{1,2},{2,11},{3,4},{4,13},{5,6},{6,15},{7,0},{8,17},{9,10},{... | collective-permute-start | bytes 1572872 | tf_op jit(solution)/shard_map/ppermute | solution.py:327
  104.0 10.3 %collective-permute-start.19 = (bf16[4,256,256]{2,1,0:T(8,128)(2,1)}, bf16[4,256,256]{2,1,0:T(8,128)(2,1)S(1)}, u32[]{:S(2)}, u32[]{:S(2)}) collective-permute-start(bf16[4,256,256]{2,1,0:T(8,128)(2,1)} %get-tuple-element.43), channel_id=1, source_target_pairs={{0,17},{1,4},{2,19},{3,6},{4,21},{5,0},{6,23},{7,2},{8,25},{9,12},... | collective-permute-start | bytes 1572872 | tf_op jit(solution)/shard_map/ppermute | solution.py:327
  104.0 13.1 %collective-permute-start.20 = (bf16[4,256,256]{2,1,0:T(8,128)(2,1)}, bf16[4,256,256]{2,1,0:T(8,128)(2,1)}, u32[]{:S(2)}, u32[]{:S(2)}) collective-permute-start(bf16[4,256,256]{2,1,0:T(8,128)(2,1)} %get-tuple-element.44), channel_id=1, source_target_pairs={{0,25},{1,6},{2,27},{3,0},{4,29},{5,2},{6,31},{7,4},{8,1},{9,14},{... | collective-permute-start | bytes 1572872 | tf_op jit(solution)/shard_map/ppermute | solution.py:327
  117.0 1.0 copy-start
  120.2 10.2 %collective-permute-start.21 = (bf16[3,256,256]{2,1,0:T(8,128)(2,1)S(1)}, bf16[3,256,256]{2,1,0:T(8,128)(2,1)S(1)}, u32[]{:S(2)}, u32[]{:S(2)}) collective-permute-start(bf16[3,256,256]{2,1,0:T(8,128)(2,1)S(1)} %add_up.5), channel_id=1, source_target_pairs={{0,16},{1,5},{2,18},{3,7},{4,20},{5,1},{6,22},{7,3},{8,24},{9,13},... | collective-permute-start | bytes 1179656 | tf_op jit(solution)/shard_map/ppermute | solution.py:327
  122.0 11.8 %collective-permute-start.22 = (bf16[3,256,256]{2,1,0:T(8,128)(2,1)S(1)}, bf16[3,256,256]{2,1,0:T(8,128)(2,1)S(1)}, u32[]{:S(2)}, u32[]{:S(2)}) collective-permute-start(bf16[3,256,256]{2,1,0:T(8,128)(2,1)S(1)} %add_up.6), channel_id=1, source_target_pairs={{0,8},{1,3},{2,10},{3,5},{4,12},{5,7},{6,14},{7,1},{8,16},{9,11},{... | collective-permute-start | bytes 1179656 | tf_op jit(solution)/shard_map/ppermute | solution.py:327
  123.6 10.4 %collective-permute-start.23 = (bf16[3,256,256]{2,1,0:T(8,128)(2,1)S(1)}, bf16[3,256,256]{2,1,0:T(8,128)(2,1)S(1)}, u32[]{:S(2)}, u32[]{:S(2)}) collective-permute-start(bf16[3,256,256]{2,1,0:T(8,128)(2,1)S(1)} %add_up.7), channel_id=1, source_target_pairs={{0,24},{1,7},{2,26},{3,1},{4,28},{5,3},{6,30},{7,5},{8,0},{9,15},{... | collective-permute-start | bytes 1179656 | tf_op jit(solution)/shard_map/ppermute | solution.py:327

commit v8 on v7

--- a/solution.py
+++ b/solution.py
@@ -392,6 +392,9 @@
     sources = jnp.concatenate([behind + c, behind + (1 - c)]).astype(jnp.int32)
     wanted = jnp.where(c == 0, ((x + steps) % nx) * ny + y, x * ny + (y + steps) % ny) * nc + c
     numbers = find(owners, ids, wanted)
+    ranks = [0] + [other * side + step for other, step in turns(side)]
+    parts = [parts[i] for i in ranks]
+    sources = jnp.stack([sources[i] for i in ranks])
     total = []
     for step in order(side):
         summed = add_up(sources, numbers, parts, step, own_count, jnp.bfloat16)

time: 136 us -> 132 us (0.971)
  waiting for transfers between devices: 43.4 us -> 33.9 us
  local copies, waits for them, and re-layouts: 6.98 us -> 12.1 us
    ppermute x20, waiting for transfers between devices: 33.6 us -> 23.9 us  [moved(): return lax.ppermute(value, BRICK, pairs)]
    another operation x0 -> x1, local copies, waits for them, and re-layouts: none -> 3.76 us  [local(): sources = jnp.stack([sources[i] for i in ranks])]
  transfers between devices with their start and end apart: 24 -> 24, of which waited for: 9 -> 9; matrix products, arithmetic and copies ran while one was open for 4% -> 8% of each run, Pallas kernels for 23% -> 24%
where the time goes in v8:
time: 132 us; the launch traced here: 131 us
  Pallas kernels  51.7 us (39%)
  waiting for transfers between devices  33.9 us (26%)
  starting transfers between devices  30.2 us (23%)
  local copies, waits for them, and re-layouts  12.1 us (9%)
  other arithmetic  2.54 us (2%)
    ppermute x20, starting transfers between devices, moved(): return lax.ppermute(value, BRICK, pairs)  25.6 us
    pallas_call x4, Pallas kernels, gather_tables(): pl.pallas_call(kernel, out_shape=pltpu.HBM((count, width, points), jnp.bf...  25.2 us
    ppermute x20, waiting for transfers between devices, moved(): return lax.ppermute(value, BRICK, pairs)  23.9 us
    pallas_call x1, Pallas kernels, integrate(): pl.pallas_call(kernel, out_shape=[pltpu.HBM((inner, width, width), jnp.bf...  8.36 us
    pallas_call x4, Pallas kernels, add_up(): pl.pallas_call(kernel, out_shape=jax.ShapeDtypeStruct((own_count, rows, c...  8.28 us
    pallas_call x1, Pallas kernels, collocate(): pl.pallas_call(kernel, out_shape=jax.ShapeDtypeStruct((8, points), jnp.fl...  7.55 us
    ppermute x1, waiting for transfers between devices, extended_pairs(): far = lax.ppermute(jnp.where(odd, high, low), axis, between)  5.12 us
    another operation x1, local copies, waits for them, and re-layouts, local(): sources = jnp.stack([sources[i] for i in ranks])  3.76 us
  transfers between devices with their start and end apart: 24, of which 9 were waited for; matrix products, arithmetic and copies ran while one was open for 8% of the time, Pallas kernels for 24%

profile of v8, /device:TPU:96, one launch (start us, length us, event | category | flops | bytes accessed | tf_op | source)
XLA Modules:
  0.0 130.7 jit_solution(16040658139028255051)
XLA Ops:
  0.0 1.5 %collective-permute-start = (bf16[3,256,256]{2,1,0:T(8,128)(2,1)}, bf16[3,256,256]{2,1,0:T(8,128)(2,1)S(1)}, u32[]{:S(2)}, u32[]{:S(2)}) collective-permute-start(bf16[3,256,256]{2,1,0:T(8,128)(2,1)} %refs_0_.1), channel_id=1, source_target_pairs={{0,8},{1,3},{2,10},{3,5},{4,12},{5,7},{6,14},{7,1},{8,16},{9,11},{... | collective-permute-start | bytes 1179656 | tf_op jit(solution)/shard_map/ppermute | solution.py:327
  1.5 2.7 %collective-permute-start.1 = (bf16[3,256,256]{2,1,0:T(8,128)(2,1)}, bf16[3,256,256]{2,1,0:T(8,128)(2,1)S(1)}, u32[]{:S(2)}, u32[]{:S(2)}) collective-permute-start(bf16[3,256,256]{2,1,0:T(8,128)(2,1)} %refs_0_.1), channel_id=1, source_target_pairs={{0,16},{1,5},{2,18},{3,7},{4,20},{5,1},{6,22},{7,3},{8,24},{9,13},... | collective-permute-start | bytes 1179656 | tf_op jit(solution)/shard_map/ppermute | solution.py:327
  4.2 1.4 %collective-permute-start.2 = (bf16[3,256,256]{2,1,0:T(8,128)(2,1)}, bf16[3,256,256]{2,1,0:T(8,128)(2,1)S(1)}, u32[]{:S(2)}, u32[]{:S(2)}) collective-permute-start(bf16[3,256,256]{2,1,0:T(8,128)(2,1)} %refs_0_.1), channel_id=1, source_target_pairs={{0,24},{1,7},{2,26},{3,1},{4,28},{5,3},{6,30},{7,5},{8,0},{9,15},{... | collective-permute-start | bytes 1179656 | tf_op jit(solution)/shard_map/ppermute | solution.py:327
  5.7 0.8 copy.20
  6.7 0.1 select_reduce_fusion
  6.8 0.1 copy.25.numbers_ref
  6.9 0.8 fusion.19
  7.7 2.9 %copy.26 = bf16[1024,1024]{0,1:T(8,128)(2,1)S(1)} copy(bf16[1024,1024]{1,0:T(8,128)(2,1)} %bitcast.18) | data formatting | bytes 4194304 | tf_op jit(solution)/shard_map/reshape | solution.py:360
  10.6 0.1 pad_add_fusion.3.bricks_ref
  10.7 6.3 %gather_tables.4.refs_8_.refs_0_ = bf16[4,512,1024]{2,1,0:T(8,128)(2,1)} custom-call(s32[4,1,512]{2,1,0:T(1,128)S(1)} %copy.27.index_ref, bf16[1024,1024]{1,0:T(8,128)(2,1)S(1)} %bitcast.14), custom_call_target="tpu_custom_call" | custom-call | flops 4294967296 | bytes 4194304 | tf_op jit(solution)/shard_map/gather_tables/pallas_call | solution.py:83
  17.0 2.3 %select_blocks.1 = (bf16[4,256,256]{2,1,0:T(8,128)(2,1)}, bf16[4,256,256]{2,1,0:T(8,128)(2,1)}, bf16[4,256,256]{2,1,0:T(8,128)(2,1)}, bf16[4,256,256]{2,1,0:T(8,...) custom-call(s32[8]{0:T(128)S(1)} %pad_add_fusion.3.bricks_ref, ...), custom_call_target="tpu_custom_call" | custom-call | tf_op jit(solution)/shard_map/select_blocks/pallas_call | solution.py:50
  19.4 0.1 collective-permute-start.6
  19.5 1.8 %collective-permute-start.3 = (bf16[4,256,256]{2,1,0:T(8,128)(2,1)}, bf16[4,256,256]{2,1,0:T(8,128)(2,1)S(1)}, u32[]{:S(2)}, u32[]{:S(2)}) collective-permute-start(bf16[4,256,256]{2,1,0:T(8,128)(2,1)} %get-tuple-element.26), channel_id=1, source_target_pairs={{0,2},{1,9},{2,4},{3,11},{4,6},{5,13},{6,0},{7,15},{8,10},{9,17},{... | collective-permute-start | bytes 1572872 | tf_op jit(solution)/shard_map/ppermute | solution.py:327
  21.3 2.9 %collective-permute-start.4 = (bf16[4,256,256]{2,1,0:T(8,128)(2,1)}, bf16[4,256,256]{2,1,0:T(8,128)(2,1)S(1)}, u32[]{:S(2)}, u32[]{:S(2)}) collective-permute-start(bf16[4,256,256]{2,1,0:T(8,128)(2,1)} %get-tuple-element.27), channel_id=1, source_target_pairs={{0,4},{1,17},{2,6},{3,19},{4,0},{5,21},{6,2},{7,23},{8,12},{9,25},... | collective-permute-start | bytes 1572872 | tf_op jit(solution)/shard_map/ppermute | solution.py:327
  24.2 1.3 collective-permute-start.5
  25.5 6.3 %gather_tables.5.refs_9_.refs_1_ = bf16[4,512,1024]{2,1,0:T(8,128)(2,1)} custom-call(s32[4,1,512]{2,1,0:T(1,128)S(1)} %copy.28.index_ref, bf16[1024,1024]{1,0:T(8,128)(2,1)S(1)} %bitcast.15), custom_call_target="tpu_custom_call" | custom-call | flops 4294967296 | bytes 4194304 | tf_op jit(solution)/shard_map/gather_tables/pallas_call | solution.py:83
  31.8 0.6 collective-permute-start.8
  32.5 5.6 %collective-permute-start.9 = (bf16[4,256,256]{2,1,0:T(8,128)(2,1)S(1)}, bf16[4,256,256]{2,1,0:T(8,128)(2,1)S(1)}, u32[]{:S(2)}, u32[]{:S(2)}) collective-permute-start(bf16[4,256,256]{2,1,0:T(8,128)(2,1)S(1)} %copy-done.7), channel_id=1, source_target_pairs={{0,7},{1,24},{2,1},{3,26},{4,3},{5,28},{6,5},{7,30},{8,15},{9,0},{... | collective-permute-start | bytes 1572872 | tf_op jit(solution)/shard_map/ppermute | solution.py:327
  38.0 6.3 %gather_tables.6.refs_10_.refs_2_ = bf16[4,512,1024]{2,1,0:T(8,128)(2,1)} custom-call(s32[4,1,512]{2,1,0:T(1,128)S(1)} %copy.29.index_ref, bf16[1024,1024]{1,0:T(8,128)(2,1)S(1)} %bitcast.16), custom_call_target="tpu_custom_call" | custom-call | flops 4294967296 | bytes 4194304 | tf_op jit(solution)/shard_map/gather_tables/pallas_call | solution.py:83
  44.3 6.3 %gather_tables.7.refs_11_.refs_3_ = bf16[4,512,1024]{2,1,0:T(8,128)(2,1)} custom-call(s32[4,1,512]{2,1,0:T(1,128)S(1)} %slice.178.index_ref, bf16[1024,1024]{1,0:T(8,128)(2,1)S(1)} %bitcast.17), custom_call_target="tpu_custom_call" | custom-call | flops 4294967296 | bytes 4194304 | tf_op jit(solution)/shard_map/gather_tables/pallas_call | solution.py:83
  50.7 0.7 copy-done.3
  51.4 0.2 copy-done.4
  51.6 0.1 copy-done.5
  51.8 0.2 copy-done.6
  51.9 7.5 %collocate.1 = f32[8,1024]{1,0:T(8,128)S(1)} custom-call(s32[2,16]{1,0:T(2,128)S(1)} %pad_add_fusion.2.places_ref, bf16[4,256,256]{2,1,0:T(8,128)(2,1)S(1)} %copy-done.1, bf16[4,256,256]{2,1,0:T(8,128)(2,1)S(1)} %collective-permute-done.3.refs_1_, bf16[4,256,256]{2,1,0:T(8,128)(2,1)S(1)} %collective-permute-done.4.refs_2_, bf16[4,256,256]{2,1,0:T(8,128)(2,1)} %copy-done.3, ...), custom_call_target="tpu_custom_call" | custom-call | tf_op jit(solution)/shard_map/collocate/pallas_call | solution.py:140
  59.5 0.1 slice.182
  59.6 3.1 %collective-permute-start.10 = (f32[2,8,16]{2,1,0:T(8,128)S(1)}, f32[2,8,16]{2,1,0:T(8,128)S(1)}, u32[]{:S(2)}, u32[]{:S(2)}) collective-permute-start(f32[2,8,16]{2,1,0:T(8,128)S(1)} %slice.182), channel_id=1, source_target_pairs={{0,32},{32,64},{64,96},{96,128},{128,160},{160,192},{192,224},{224... | collective-permute-start | bytes 3080 | tf_op jit(solution)/shard_map/ppermute | solution.py:266
  62.8 0.1 slice.184
  62.9 1.2 collective-permute-done.10
  64.1 3.7 %collective-permute-done.11 = f32[2,8,16]{2,1,0:T(8,128)S(1)} collective-permute-done((f32[2,8,16]{2,1,0:T(8,128)S(1)}, f32[2,8,16]{2,1,0:T(8,128)S(1)}, u32[]{:S(2)}, u32[]{:S(2)}) %collective-permute-start.11) | collective-permute-done | bytes 1056 | tf_op jit(solution)/shard_map/ppermute | solution.py:267
  67.7 0.1 collective-permute-start.12
  67.8 1.4 %collective-permute-start.13 = (f32[12,2,16]{2,1,0:T(2,128)S(1)}, f32[12,2,16]{2,1,0:T(2,128)S(1)}, u32[]{:S(2)}, u32[]{:S(2)}) collective-permute-start(f32[12,2,16]{2,1,0:T(2,128)S(1)} %get-tuple-element.79), channel_id=1, source_target_pairs={{0,31},{1,2},{2,1},{3,4},{4,3},{5,6},{6,5},{7,8},{8,7},{9,10},{10,... | collective-permute-start | bytes 4616 | tf_op jit(solution)/shard_map/ppermute | solution.py:277
  69.2 5.1 %collective-permute-done.13 = f32[12,2,16]{2,1,0:T(2,128)S(1)} collective-permute-done((f32[12,2,16]{2,1,0:T(2,128)S(1)}, f32[12,2,16]{2,1,0:T(2,128)S(1)}, u32[]{:S(2)}, u32[]{:S(2)}) %collective-permute-start.13) | collective-permute-done | bytes 1568 | tf_op jit(solution)/shard_map/ppermute | solution.py:277
  74.4 0.1 fusion.46
  74.5 0.1 fusion.47
  74.6 0.1 fusion.42
  74.7 0.1 fusion.48
  74.8 0.1 fusion.49
  75.0 0.1 fusion.9
  75.1 0.1 mul.148.scaled_ref
  75.2 8.4 %integrate.1 = (bf16[4,256,256]{2,1,0:T(8,128)(2,1)}, bf16[4,256,256]{2,1,0:T(8,128)(2,1)}, bf16[4,256,256]{2,1,0:T(8,128)(2,1)}, bf16[4,256,256]{2,1,0:T(8,128)...) custom-call(s32[2,16]{1,0:T(2,128)S(1)} %pad_add_fusion.1.places_ref, ...), custom_call_target="tpu_custom_call" | custom-call | tf_op jit(solution)/shard_map/integrate/pallas_call | solution.py:196
  83.5 0.1 collective-permute-start.14
  83.6 0.1 collective-permute-start.15
  83.7 2.0 %collective-permute-start.16 = (bf16[4,256,256]{2,1,0:T(8,128)(2,1)}, bf16[4,256,256]{2,1,0:T(8,128)(2,1)S(1)}, u32[]{:S(2)}, u32[]{:S(2)}) collective-permute-start(bf16[4,256,256]{2,1,0:T(8,128)(2,1)} %get-tuple-element.40), channel_id=1, source_target_pairs={{0,2},{1,9},{2,4},{3,11},{4,6},{5,13},{6,0},{7,15},{8,10},{9,17},{... | collective-permute-start | bytes 1572872 | tf_op jit(solution)/shard_map/ppermute | solution.py:327
  85.7 2.7 %collective-permute-start.18 = (bf16[4,256,256]{2,1,0:T(8,128)(2,1)}, bf16[4,256,256]{2,1,0:T(8,128)(2,1)S(1)}, u32[]{:S(2)}, u32[]{:S(2)}) collective-permute-start(bf16[4,256,256]{2,1,0:T(8,128)(2,1)} %get-tuple-element.42), channel_id=1, source_target_pairs={{0,17},{1,4},{2,19},{3,6},{4,21},{5,0},{6,23},{7,2},{8,25},{9,12},... | collective-permute-start | bytes 1572872 | tf_op jit(solution)/shard_map/ppermute | solution.py:327
  88.5 7.2 %collective-permute-done.15.refs_2_ = bf16[4,256,256]{2,1,0:T(8,128)(2,1)S(1)} collective-permute-done((bf16[4,256,256]{2,1,0:T(8,128)(2,1)}, bf16[4,256,256]{2,1,0:T(8,128)(2,1)S(1)}, u32[]{:S(2)}, u32[]{:S(2)}) %collective-permute-start.15) | collective-permute-done | bytes 524320 | tf_op jit(solution)/shard_map/ppermute | solution.py:327
  95.8 0.1 copy.30.numbers_ref
  95.9 0.6 fusion.54
  96.5 0.7 fusion.53
  97.1 3.8 %stack.6.bricks_ref = s32[8]{0:T(128)S(1)} concatenate(s32[1]{0:T(128)} %get-tuple-element.96, s32[1]{0:T(128)} %get-tuple-element.94, s32[1]{0:T(128)} %get-tuple-element.95, s32[2]{0:T(128)S(1)} %slice.169, s32[1]{0:T(128)} %get-tuple-element.93, s32[1]{0:T(128)} %get-tuple-element.92, s32[1]{0:T(128)} %get-tuple-element.91), dimensions={0} | concatenate | bytes 64 | tf_op jit(solution)/shard_map/stack | solution.py:397
  100.9 7.4 %collective-permute-done.16.refs_3_ = bf16[4,256,256]{2,1,0:T(8,128)(2,1)S(1)} collective-permute-done((bf16[4,256,256]{2,1,0:T(8,128)(2,1)}, bf16[4,256,256]{2,1,0:T(8,128)(2,1)S(1)}, u32[]{:S(2)}, u32[]{:S(2)}) %collective-permute-start.16) | collective-permute-done | bytes 524320 | tf_op jit(solution)/shard_map/ppermute | solution.py:327
  108.3 3.0 %collective-permute-done.19.refs_6_ = bf16[4,256,256]{2,1,0:T(8,128)(2,1)S(1)} collective-permute-done((bf16[4,256,256]{2,1,0:T(8,128)(2,1)}, bf16[4,256,256]{2,1,0:T(8,128)(2,1)S(1)}, u32[]{:S(2)}, u32[]{:S(2)}) %collective-permute-start.19) | collective-permute-done | bytes 524320 | tf_op jit(solution)/shard_map/ppermute | solution.py:327
  111.3 1.0 copy-done
  112.3 2.3 %add_up.5 = bf16[3,256,256]{2,1,0:T(8,128)(2,1)S(1)} custom-call(s32[8]{0:T(128)S(1)} %stack.6.bricks_ref, s32[32,4]{1,0:T(8,128)S(1)} %copy.30.numbers_ref, bf16[4,256,256]{2,1,0:T(8,128)(2,1)S(1)} %copy-done, bf16[4,256,256]{2,1,0:T(8,128)(2,1)S(1)} %collective-permute-done.14.refs_1_, bf16[4,256,256]{2,1,0:T(8,128)(2,1)S(1)} %collective-permute-done.15.refs_2_, ...), custom_call_target="tpu_custom_call" | custom-call | tf_op jit(solution)/shard_map/add_up/pallas_call | solution.py:238
  114.6 0.1 collective-permute-start.21
  114.7 1.9 %add_up.6 = bf16[3,256,256]{2,1,0:T(8,128)(2,1)S(1)} custom-call(s32[8]{0:T(128)S(1)} %stack.6.bricks_ref, s32[32,4]{1,0:T(8,128)S(1)} %copy.30.numbers_ref, bf16[4,256,256]{2,1,0:T(8,128)(2,1)S(1)} %copy-done, bf16[4,256,256]{2,1,0:T(8,128)(2,1)S(1)} %collective-permute-done.14.refs_1_, bf16[4,256,256]{2,1,0:T(8,128)(2,1)S(1)} %collective-permute-done.15.refs_2_, ...), custom_call_target="tpu_custom_call" | custom-call | tf_op jit(solution)/shard_map/add_up/pallas_call | solution.py:238
  116.6 2.6 %collective-permute-start.22 = (bf16[3,256,256]{2,1,0:T(8,128)(2,1)S(1)}, bf16[3,256,256]{2,1,0:T(8,128)(2,1)S(1)}, u32[]{:S(2)}, u32[]{:S(2)}) collective-permute-start(bf16[3,256,256]{2,1,0:T(8,128)(2,1)S(1)} %add_up.6), channel_id=1, source_target_pairs={{0,8},{1,3},{2,10},{3,5},{4,12},{5,7},{6,14},{7,1},{8,16},{9,11},{... | collective-permute-start | bytes 1179656 | tf_op jit(solution)/shard_map/ppermute | solution.py:327
  119.2 2.6 %add_up.7 = bf16[3,256,256]{2,1,0:T(8,128)(2,1)S(1)} custom-call(s32[8]{0:T(128)S(1)} %stack.6.bricks_ref, s32[32,4]{1,0:T(8,128)S(1)} %copy.30.numbers_ref, bf16[4,256,256]{2,1,0:T(8,128)(2,1)S(1)} %copy-done, bf16[4,256,256]{2,1,0:T(8,128)(2,1)S(1)} %collective-permute-done.14.refs_1_, bf16[4,256,256]{2,1,0:T(8,128)(2,1)S(1)} %collective-permute-done.15.refs_2_, ...), custom_call_target="tpu_custom_call" | custom-call | tf_op jit(solution)/shard_map/add_up/pallas_call | solution.py:238
  121.8 0.1 collective-permute-start.23
  121.9 1.5 %add_up.4 = f32[3,256,256]{2,1,0:T(8,128)S(1)} custom-call(s32[8]{0:T(128)S(1)} %stack.6.bricks_ref, s32[32,4]{1,0:T(8,128)S(1)} %copy.30.numbers_ref, bf16[4,256,256]{2,1,0:T(8,128)(2,1)S(1)} %copy-done, bf16[4,256,256]{2,1,0:T(8,128)(2,1)S(1)} %collective-permute-done.14.refs_1_, bf16[4,256,256]{2,1,0:T(8,128)(2,1)S(1)} %collective-permute-done.15.refs_2_, ...), custom_call_target="tpu_custom_call" | custom-call | tf_op jit(solution)/shard_map/add_up/pallas_call | solution.py:238
  123.4 0.6 collective-permute-done.21
  124.1 4.1 %collective-permute-done.22 = bf16[3,256,256]{2,1,0:T(8,128)(2,1)S(1)} collective-permute-done((bf16[3,256,256]{2,1,0:T(8,128)(2,1)S(1)}, bf16[3,256,256]{2,1,0:T(8,128)(2,1)S(1)}, u32[]{:S(2)}, u32[]{:S(2)}) %collective-permute-start.22) | collective-permute-done | bytes 393248 | tf_op jit(solution)/shard_map/ppermute | solution.py:327
  128.2 1.5 %collective-permute-done.23 = bf16[3,256,256]{2,1,0:T(8,128)(2,1)S(1)} collective-permute-done((bf16[3,256,256]{2,1,0:T(8,128)(2,1)S(1)}, bf16[3,256,256]{2,1,0:T(8,128)(2,1)S(1)}, u32[]{:S(2)}, u32[]{:S(2)}) %collective-permute-start.23) | collective-permute-done | bytes 393248 | tf_op jit(solution)/shard_map/ppermute | solution.py:327
  129.7 1.0 convert_add_fusion
  (63 shorter events, 0.7 us)
Async XLA Ops:
  0.0 17.0 %collective-permute-start = (bf16[3,256,256]{2,1,0:T(8,128)(2,1)}, bf16[3,256,256]{2,1,0:T(8,128)(2,1)S(1)}, u32[]{:S(2)}, u32[]{:S(2)}) collective-permute-start(bf16[3,256,256]{2,1,0:T(8,128)(2,1)} %refs_0_.1), channel_id=1, source_target_pairs={{0,8},{1,3},{2,10},{3,5},{4,12},{5,7},{6,14},{7,1},{8,16},{9,11},{... | collective-permute-start | bytes 1179656 | tf_op jit(solution)/shard_map/ppermute | solution.py:327
  1.5 15.5 %collective-permute-start.1 = (bf16[3,256,256]{2,1,0:T(8,128)(2,1)}, bf16[3,256,256]{2,1,0:T(8,128)(2,1)S(1)}, u32[]{:S(2)}, u32[]{:S(2)}) collective-permute-start(bf16[3,256,256]{2,1,0:T(8,128)(2,1)} %refs_0_.1), channel_id=1, source_target_pairs={{0,16},{1,5},{2,18},{3,7},{4,20},{5,1},{6,22},{7,3},{8,24},{9,13},... | collective-permute-start | bytes 1179656 | tf_op jit(solution)/shard_map/ppermute | solution.py:327
  4.2 12.8 %collective-permute-start.2 = (bf16[3,256,256]{2,1,0:T(8,128)(2,1)}, bf16[3,256,256]{2,1,0:T(8,128)(2,1)S(1)}, u32[]{:S(2)}, u32[]{:S(2)}) collective-permute-start(bf16[3,256,256]{2,1,0:T(8,128)(2,1)} %refs_0_.1), channel_id=1, source_target_pairs={{0,24},{1,7},{2,26},{3,1},{4,28},{5,3},{6,30},{7,5},{8,0},{9,15},{... | collective-permute-start | bytes 1179656 | tf_op jit(solution)/shard_map/ppermute | solution.py:327
  10.7 6.3 %copy-start.2 = (bf16[3,256,256]{2,1,0:T(8,128)(2,1)S(1)}, bf16[3,256,256]{2,1,0:T(8,128)(2,1)}, u32[]{:S(2)}) copy-start(bf16[3,256,256]{2,1,0:T(8,128)(2,1)} %refs_0_.1) | copy-start | bytes 1179652
  19.4 12.5 %collective-permute-start.6 = (bf16[4,256,256]{2,1,0:T(8,128)(2,1)}, bf16[4,256,256]{2,1,0:T(8,128)(2,1)}, u32[]{:S(2)}, u32[]{:S(2)}) collective-permute-start(bf16[4,256,256]{2,1,0:T(8,128)(2,1)} %get-tuple-element.30), channel_id=1, source_target_pairs={{0,1},{1,0},{2,3},{3,2},{4,5},{5,4},{6,7},{7,6},{8,9},{9,8},{10,11... | collective-permute-start | bytes 1572872 | tf_op jit(solution)/shard_map/ppermute | solution.py:327
  19.5 13.0 %collective-permute-start.3 = (bf16[4,256,256]{2,1,0:T(8,128)(2,1)}, bf16[4,256,256]{2,1,0:T(8,128)(2,1)S(1)}, u32[]{:S(2)}, u32[]{:S(2)}) collective-permute-start(bf16[4,256,256]{2,1,0:T(8,128)(2,1)} %get-tuple-element.26), channel_id=1, source_target_pairs={{0,2},{1,9},{2,4},{3,11},{4,6},{5,13},{6,0},{7,15},{8,10},{9,17},{... | collective-permute-start | bytes 1572872 | tf_op jit(solution)/shard_map/ppermute | solution.py:327
  21.3 29.3 %collective-permute-start.4 = (bf16[4,256,256]{2,1,0:T(8,128)(2,1)}, bf16[4,256,256]{2,1,0:T(8,128)(2,1)S(1)}, u32[]{:S(2)}, u32[]{:S(2)}) collective-permute-start(bf16[4,256,256]{2,1,0:T(8,128)(2,1)} %get-tuple-element.27), channel_id=1, source_target_pairs={{0,4},{1,17},{2,6},{3,19},{4,0},{5,21},{6,2},{7,23},{8,12},{9,25},... | collective-permute-start | bytes 1572872 | tf_op jit(solution)/shard_map/ppermute | solution.py:327
  24.2 26.4 %collective-permute-start.5 = (bf16[4,256,256]{2,1,0:T(8,128)(2,1)}, bf16[4,256,256]{2,1,0:T(8,128)(2,1)S(1)}, u32[]{:S(2)}, u32[]{:S(2)}) collective-permute-start(bf16[4,256,256]{2,1,0:T(8,128)(2,1)} %get-tuple-element.28), channel_id=1, source_target_pairs={{0,6},{1,25},{2,0},{3,27},{4,2},{5,29},{6,4},{7,31},{8,14},{9,1},{... | collective-permute-start | bytes 1572872 | tf_op jit(solution)/shard_map/ppermute | solution.py:327
  25.5 6.4 %copy-start.8 = (bf16[4,256,256]{2,1,0:T(8,128)(2,1)S(1)}, bf16[4,256,256]{2,1,0:T(8,128)(2,1)}, u32[]{:S(2)}) copy-start(bf16[4,256,256]{2,1,0:T(8,128)(2,1)} %get-tuple-element.32) | copy-start | bytes 1572868
  25.5 7.0 %copy-start.7 = (bf16[4,256,256]{2,1,0:T(8,128)(2,1)S(1)}, bf16[4,256,256]{2,1,0:T(8,128)(2,1)}, u32[]{:S(2)}) copy-start(bf16[4,256,256]{2,1,0:T(8,128)(2,1)} %get-tuple-element.33) | copy-start | bytes 1572868
  25.5 25.1 %collective-permute-start.7 = (bf16[4,256,256]{2,1,0:T(8,128)(2,1)}, bf16[4,256,256]{2,1,0:T(8,128)(2,1)S(1)}, u32[]{:S(2)}, u32[]{:S(2)}) collective-permute-start(bf16[4,256,256]{2,1,0:T(8,128)(2,1)} %get-tuple-element.31), channel_id=1, source_target_pairs={{0,3},{1,8},{2,5},{3,10},{4,7},{5,12},{6,1},{7,14},{8,11},{9,16},{... | collective-permute-start | bytes 1572872 | tf_op jit(solution)/shard_map/ppermute | solution.py:327
  31.8 18.8 %collective-permute-start.8 = (bf16[4,256,256]{2,1,0:T(8,128)(2,1)S(1)}, bf16[4,256,256]{2,1,0:T(8,128)(2,1)S(1)}, u32[]{:S(2)}, u32[]{:S(2)}) collective-permute-start(bf16[4,256,256]{2,1,0:T(8,128)(2,1)S(1)} %copy-done.8), channel_id=1, source_target_pairs={{0,5},{1,16},{2,7},{3,18},{4,1},{5,20},{6,3},{7,22},{8,13},{9,24},... | collective-permute-start | bytes 1572872 | tf_op jit(solution)/shard_map/ppermute | solution.py:327
  32.5 18.2 %collective-permute-start.9 = (bf16[4,256,256]{2,1,0:T(8,128)(2,1)S(1)}, bf16[4,256,256]{2,1,0:T(8,128)(2,1)S(1)}, u32[]{:S(2)}, u32[]{:S(2)}) collective-permute-start(bf16[4,256,256]{2,1,0:T(8,128)(2,1)S(1)} %copy-done.7), channel_id=1, source_target_pairs={{0,7},{1,24},{2,1},{3,26},{4,3},{5,28},{6,5},{7,30},{8,15},{9,0},{... | collective-permute-start | bytes 1572872 | tf_op jit(solution)/shard_map/ppermute | solution.py:327
  44.3 7.6 %copy-start.1 = (bf16[4,256,256]{2,1,0:T(8,128)(2,1)S(1)}, bf16[4,256,256]{2,1,0:T(8,128)(2,1)}, u32[]{:S(2)}) copy-start(bf16[4,256,256]{2,1,0:T(8,128)(2,1)} %get-tuple-element.25.refs_0_) | copy-start | bytes 1572868
  50.6 0.8 copy-start.3
  50.6 1.0 copy-start.4
  50.6 1.1 copy-start.5
  50.6 1.3 copy-start.6
  59.6 4.5 %collective-permute-start.10 = (f32[2,8,16]{2,1,0:T(8,128)S(1)}, f32[2,8,16]{2,1,0:T(8,128)S(1)}, u32[]{:S(2)}, u32[]{:S(2)}) collective-permute-start(f32[2,8,16]{2,1,0:T(8,128)S(1)} %slice.182), channel_id=1, source_target_pairs={{0,32},{32,64},{64,96},{96,128},{128,160},{160,192},{192,224},{224... | collective-permute-start | bytes 3080 | tf_op jit(solution)/shard_map/ppermute | solution.py:266
  62.8 4.9 %collective-permute-start.11 = (f32[2,8,16]{2,1,0:T(8,128)S(1)}, f32[2,8,16]{2,1,0:T(8,128)S(1)}, u32[]{:S(2)}, u32[]{:S(2)}) collective-permute-start(f32[2,8,16]{2,1,0:T(8,128)S(1)} %slice.184), channel_id=1, source_target_pairs={{32,0},{64,32},{96,64},{128,96},{160,128},{192,160},{224,192},{0,2... | collective-permute-start | bytes 3080 | tf_op jit(solution)/shard_map/ppermute | solution.py:267
  67.7 1.5 %collective-permute-start.12 = (f32[12,2,16]{2,1,0:T(2,128)S(1)}, f32[12,2,16]{2,1,0:T(2,128)S(1)}, u32[]{:S(2)}, u32[]{:S(2)}) collective-permute-start(f32[12,2,16]{2,1,0:T(2,128)S(1)} %get-tuple-element.78), channel_id=1, source_target_pairs={{0,1},{1,0},{2,3},{3,2},{4,5},{5,4},{6,7},{7,6},{8,9},{9,8},{10,11... | collective-permute-start | bytes 4616 | tf_op jit(solution)/shard_map/ppermute | solution.py:278
  67.8 6.5 %collective-permute-start.13 = (f32[12,2,16]{2,1,0:T(2,128)S(1)}, f32[12,2,16]{2,1,0:T(2,128)S(1)}, u32[]{:S(2)}, u32[]{:S(2)}) collective-permute-start(f32[12,2,16]{2,1,0:T(2,128)S(1)} %get-tuple-element.79), channel_id=1, source_target_pairs={{0,31},{1,2},{2,1},{3,4},{4,3},{5,6},{6,5},{7,8},{8,7},{9,10},{10,... | collective-permute-start | bytes 4616 | tf_op jit(solution)/shard_map/ppermute | solution.py:277
  83.5 4.9 %collective-permute-start.14 = (bf16[4,256,256]{2,1,0:T(8,128)(2,1)}, bf16[4,256,256]{2,1,0:T(8,128)(2,1)S(1)}, u32[]{:S(2)}, u32[]{:S(2)}) collective-permute-start(bf16[4,256,256]{2,1,0:T(8,128)(2,1)} %get-tuple-element.38), channel_id=1, source_target_pairs={{0,1},{1,0},{2,3},{3,2},{4,5},{5,4},{6,7},{7,6},{8,9},{9,8},{10,11... | collective-permute-start | bytes 1572872 | tf_op jit(solution)/shard_map/ppermute | solution.py:327
  83.6 12.1 %collective-permute-start.15 = (bf16[4,256,256]{2,1,0:T(8,128)(2,1)}, bf16[4,256,256]{2,1,0:T(8,128)(2,1)S(1)}, u32[]{:S(2)}, u32[]{:S(2)}) collective-permute-start(bf16[4,256,256]{2,1,0:T(8,128)(2,1)} %get-tuple-element.39), channel_id=1, source_target_pairs={{0,6},{1,25},{2,0},{3,27},{4,2},{5,29},{6,4},{7,31},{8,14},{9,1},{... | collective-permute-start | bytes 1572872 | tf_op jit(solution)/shard_map/ppermute | solution.py:327
  83.7 24.5 %collective-permute-start.16 = (bf16[4,256,256]{2,1,0:T(8,128)(2,1)}, bf16[4,256,256]{2,1,0:T(8,128)(2,1)S(1)}, u32[]{:S(2)}, u32[]{:S(2)}) collective-permute-start(bf16[4,256,256]{2,1,0:T(8,128)(2,1)} %get-tuple-element.40), channel_id=1, source_target_pairs={{0,2},{1,9},{2,4},{3,11},{4,6},{5,13},{6,0},{7,15},{8,10},{9,17},{... | collective-permute-start | bytes 1572872 | tf_op jit(solution)/shard_map/ppermute | solution.py:327
  85.7 22.5 %collective-permute-start.17 = (bf16[4,256,256]{2,1,0:T(8,128)(2,1)}, bf16[4,256,256]{2,1,0:T(8,128)(2,1)S(1)}, u32[]{:S(2)}, u32[]{:S(2)}) collective-permute-start(bf16[4,256,256]{2,1,0:T(8,128)(2,1)} %get-tuple-element.41), channel_id=1, source_target_pairs={{0,4},{1,17},{2,6},{3,19},{4,0},{5,21},{6,2},{7,23},{8,12},{9,25},... | collective-permute-start | bytes 1572872 | tf_op jit(solution)/shard_map/ppermute | solution.py:327
  85.7 22.5 %collective-permute-start.18 = (bf16[4,256,256]{2,1,0:T(8,128)(2,1)}, bf16[4,256,256]{2,1,0:T(8,128)(2,1)S(1)}, u32[]{:S(2)}, u32[]{:S(2)}) collective-permute-start(bf16[4,256,256]{2,1,0:T(8,128)(2,1)} %get-tuple-element.42), channel_id=1, source_target_pairs={{0,17},{1,4},{2,19},{3,6},{4,21},{5,0},{6,23},{7,2},{8,25},{9,12},... | collective-permute-start | bytes 1572872 | tf_op jit(solution)/shard_map/ppermute | solution.py:327
  88.5 22.8 %collective-permute-start.19 = (bf16[4,256,256]{2,1,0:T(8,128)(2,1)}, bf16[4,256,256]{2,1,0:T(8,128)(2,1)S(1)}, u32[]{:S(2)}, u32[]{:S(2)}) collective-permute-start(bf16[4,256,256]{2,1,0:T(8,128)(2,1)} %get-tuple-element.43), channel_id=1, source_target_pairs={{0,9},{1,2},{2,11},{3,4},{4,13},{5,6},{6,15},{7,0},{8,17},{9,10},{... | collective-permute-start | bytes 1572872 | tf_op jit(solution)/shard_map/ppermute | solution.py:327
  95.7 15.6 %collective-permute-start.20 = (bf16[4,256,256]{2,1,0:T(8,128)(2,1)}, bf16[4,256,256]{2,1,0:T(8,128)(2,1)}, u32[]{:S(2)}, u32[]{:S(2)}) collective-permute-start(bf16[4,256,256]{2,1,0:T(8,128)(2,1)} %get-tuple-element.44), channel_id=1, source_target_pairs={{0,25},{1,6},{2,27},{3,0},{4,29},{5,2},{6,31},{7,4},{8,1},{9,14},{... | collective-permute-start | bytes 1572872 | tf_op jit(solution)/shard_map/ppermute | solution.py:327
  111.3 1.0 copy-start
  114.6 9.5 %collective-permute-start.21 = (bf16[3,256,256]{2,1,0:T(8,128)(2,1)S(1)}, bf16[3,256,256]{2,1,0:T(8,128)(2,1)S(1)}, u32[]{:S(2)}, u32[]{:S(2)}) collective-permute-start(bf16[3,256,256]{2,1,0:T(8,128)(2,1)S(1)} %add_up.5), channel_id=1, source_target_pairs={{0,16},{1,5},{2,18},{3,7},{4,20},{5,1},{6,22},{7,3},{8,24},{9,13},... | collective-permute-start | bytes 1179656 | tf_op jit(solution)/shard_map/ppermute | solution.py:327
  116.6 11.6 %collective-permute-start.22 = (bf16[3,256,256]{2,1,0:T(8,128)(2,1)S(1)}, bf16[3,256,256]{2,1,0:T(8,128)(2,1)S(1)}, u32[]{:S(2)}, u32[]{:S(2)}) collective-permute-start(bf16[3,256,256]{2,1,0:T(8,128)(2,1)S(1)} %add_up.6), channel_id=1, source_target_pairs={{0,8},{1,3},{2,10},{3,5},{4,12},{5,7},{6,14},{7,1},{8,16},{9,11},{... | collective-permute-start | bytes 1179656 | tf_op jit(solution)/shard_map/ppermute | solution.py:327
  121.8 7.9 %collective-permute-start.23 = (bf16[3,256,256]{2,1,0:T(8,128)(2,1)S(1)}, bf16[3,256,256]{2,1,0:T(8,128)(2,1)S(1)}, u32[]{:S(2)}, u32[]{:S(2)}) collective-permute-start(bf16[3,256,256]{2,1,0:T(8,128)(2,1)S(1)} %add_up.7), channel_id=1, source_target_pairs={{0,24},{1,7},{2,26},{3,1},{4,28},{5,3},{6,30},{7,5},{8,0},{9,15},{... | collective-permute-start | bytes 1179656 | tf_op jit(solution)/shard_map/ppermute | solution.py:327

commit v9 on v8

--- a/solution.py
+++ b/solution.py
@@ -388,13 +388,14 @@
     for other, step in turns(side):
         i = other * side + step
         parts[i] = moved(parts[i], step, bool(other), lambda c, to: to == 0)
-    behind = jnp.where(c == 0, x * ny + (y - steps) % ny, ((x - steps) % nx) * ny + y) * nc
-    sources = jnp.concatenate([behind + c, behind + (1 - c)]).astype(jnp.int32)
     wanted = jnp.where(c == 0, ((x + steps) % nx) * ny + y, x * ny + (y + steps) % ny) * nc + c
     numbers = find(owners, ids, wanted)
     ranks = [0] + [other * side + step for other, step in turns(side)]
     parts = [parts[i] for i in ranks]
-    sources = jnp.stack([sources[i] for i in ranks])
+    back = jnp.array([i % side for i in ranks], jnp.int32)
+    core = jnp.where(jnp.array([i >= side for i in ranks]), 1 - c, c)
+    behind = jnp.where(c == 0, x * ny + (y - back) % ny, ((x - back) % nx) * ny + y)
+    sources = (behind * nc + core).astype(jnp.int32)
     total = []
     for step in order(side):
         summed = add_up(sources, numbers, parts, step, own_count, jnp.bfloat16)

time: 132 us -> 134 us (1.015)
  the two profiles are of different devices: /device:TPU:96 before, /device:TPU:120 now
where the time goes in v9:
time: 134 us; the launch traced here: 133 us
  Pallas kernels  52.4 us (39%)
  starting transfers between devices  45.2 us (34%)
  waiting for transfers between devices  25.7 us (19%)
  local copies, waits for them, and re-layouts  6.99 us (5%)
  other arithmetic  2.54 us (2%)
    ppermute x20, starting transfers between devices, moved(): return lax.ppermute(value, BRICK, pairs)  41.2 us
    pallas_call x4, Pallas kernels, gather_tables(): pl.pallas_call(kernel, out_shape=pltpu.HBM((count, width, points), jnp.bf...  25 us
    ppermute x20, waiting for transfers between devices, moved(): return lax.ppermute(value, BRICK, pairs)  18.4 us
    pallas_call x4, Pallas kernels, add_up(): pl.pallas_call(kernel, out_shape=jax.ShapeDtypeStruct((own_count, rows, c...  8.99 us
    pallas_call x1, Pallas kernels, integrate(): pl.pallas_call(kernel, out_shape=[pltpu.HBM((inner, width, width), jnp.bf...  8.37 us
    pallas_call x1, Pallas kernels, collocate(): pl.pallas_call(kernel, out_shape=jax.ShapeDtypeStruct((8, points), jnp.fl...  7.55 us
    ppermute x1, waiting for transfers between devices, extended_ring(): above = lax.ppermute(low, axis, backward)  3.65 us
    unnamed x25, local copies, waits for them, and re-layouts  3.11 us
  transfers between devices with their start and end apart: 24, of which 9 were waited for; matrix products, arithmetic and copies ran while one was open for 4% of the time, Pallas kernels for 24%

profile of v9, /device:TPU:120, one launch (start us, length us, event | category | flops | bytes accessed | tf_op | source)
XLA Modules:
  0.0 133.2 jit_solution(2964309519918483553)
XLA Ops:
  0.0 1.5 %collective-permute-start = (bf16[3,256,256]{2,1,0:T(8,128)(2,1)}, bf16[3,256,256]{2,1,0:T(8,128)(2,1)S(1)}, u32[]{:S(2)}, u32[]{:S(2)}) collective-permute-start(bf16[3,256,256]{2,1,0:T(8,128)(2,1)} %refs_0_.1), channel_id=1, source_target_pairs={{0,8},{1,3},{2,10},{3,5},{4,12},{5,7},{6,14},{7,1},{8,16},{9,11},{... | collective-permute-start | bytes 1179656 | tf_op jit(solution)/shard_map/ppermute | solution.py:327
  1.5 2.7 %collective-permute-start.1 = (bf16[3,256,256]{2,1,0:T(8,128)(2,1)}, bf16[3,256,256]{2,1,0:T(8,128)(2,1)S(1)}, u32[]{:S(2)}, u32[]{:S(2)}) collective-permute-start(bf16[3,256,256]{2,1,0:T(8,128)(2,1)} %refs_0_.1), channel_id=1, source_target_pairs={{0,16},{1,5},{2,18},{3,7},{4,20},{5,1},{6,22},{7,3},{8,24},{9,13},... | collective-permute-start | bytes 1179656 | tf_op jit(solution)/shard_map/ppermute | solution.py:327
  4.2 1.4 %collective-permute-start.2 = (bf16[3,256,256]{2,1,0:T(8,128)(2,1)}, bf16[3,256,256]{2,1,0:T(8,128)(2,1)S(1)}, u32[]{:S(2)}, u32[]{:S(2)}) collective-permute-start(bf16[3,256,256]{2,1,0:T(8,128)(2,1)} %refs_0_.1), channel_id=1, source_target_pairs={{0,24},{1,7},{2,26},{3,1},{4,28},{5,3},{6,30},{7,5},{8,0},{9,15},{... | collective-permute-start | bytes 1179656 | tf_op jit(solution)/shard_map/ppermute | solution.py:327
  5.7 0.8 copy.22
  6.6 0.1 select_reduce_fusion
  6.7 0.1 copy.27.numbers_ref
  6.8 0.8 fusion.19
  7.7 2.9 %copy.28 = bf16[1024,1024]{0,1:T(8,128)(2,1)S(1)} copy(bf16[1024,1024]{1,0:T(8,128)(2,1)} %bitcast.18) | data formatting | bytes 4194304 | tf_op jit(solution)/shard_map/reshape | solution.py:360
  10.6 0.1 pad_add_fusion.3.bricks_ref
  10.7 6.3 %gather_tables.4.refs_8_.refs_0_ = bf16[4,512,1024]{2,1,0:T(8,128)(2,1)} custom-call(s32[4,1,512]{2,1,0:T(1,128)S(1)} %copy.29.index_ref, bf16[1024,1024]{1,0:T(8,128)(2,1)S(1)} %bitcast.14), custom_call_target="tpu_custom_call" | custom-call | flops 4294967296 | bytes 4194304 | tf_op jit(solution)/shard_map/gather_tables/pallas_call | solution.py:83
  17.0 2.5 %select_blocks.1 = (bf16[4,256,256]{2,1,0:T(8,128)(2,1)}, bf16[4,256,256]{2,1,0:T(8,128)(2,1)}, bf16[4,256,256]{2,1,0:T(8,128)(2,1)}, bf16[4,256,256]{2,1,0:T(8,...) custom-call(s32[8]{0:T(128)S(1)} %pad_add_fusion.3.bricks_ref, ...), custom_call_target="tpu_custom_call" | custom-call | tf_op jit(solution)/shard_map/select_blocks/pallas_call | solution.py:50
  19.5 0.1 collective-permute-start.6
  19.6 0.1 collective-permute-start.3
  19.8 2.9 %collective-permute-start.4 = (bf16[4,256,256]{2,1,0:T(8,128)(2,1)}, bf16[4,256,256]{2,1,0:T(8,128)(2,1)S(1)}, u32[]{:S(2)}, u32[]{:S(2)}) collective-permute-start(bf16[4,256,256]{2,1,0:T(8,128)(2,1)} %get-tuple-element.27), channel_id=1, source_target_pairs={{0,4},{1,17},{2,6},{3,19},{4,0},{5,21},{6,2},{7,23},{8,12},{9,25},... | collective-permute-start | bytes 1572872 | tf_op jit(solution)/shard_map/ppermute | solution.py:327
  22.7 0.8 collective-permute-start.7
  23.5 6.3 %gather_tables.5.refs_9_.refs_1_ = bf16[4,512,1024]{2,1,0:T(8,128)(2,1)} custom-call(s32[4,1,512]{2,1,0:T(1,128)S(1)} %copy.30.index_ref, bf16[1024,1024]{1,0:T(8,128)(2,1)S(1)} %bitcast.15), custom_call_target="tpu_custom_call" | custom-call | flops 4294967296 | bytes 4194304 | tf_op jit(solution)/shard_map/gather_tables/pallas_call | solution.py:83
  29.8 2.9 %collective-permute-start.8 = (bf16[4,256,256]{2,1,0:T(8,128)(2,1)S(1)}, bf16[4,256,256]{2,1,0:T(8,128)(2,1)S(1)}, u32[]{:S(2)}, u32[]{:S(2)}) collective-permute-start(bf16[4,256,256]{2,1,0:T(8,128)(2,1)S(1)} %copy-done.10), channel_id=1, source_target_pairs={{0,5},{1,16},{2,7},{3,18},{4,1},{5,20},{6,3},{7,22},{8,13},{9,24},... | collective-permute-start | bytes 1572872 | tf_op jit(solution)/shard_map/ppermute | solution.py:327
  32.7 2.9 %collective-permute-start.9 = (bf16[4,256,256]{2,1,0:T(8,128)(2,1)S(1)}, bf16[4,256,256]{2,1,0:T(8,128)(2,1)S(1)}, u32[]{:S(2)}, u32[]{:S(2)}) collective-permute-start(bf16[4,256,256]{2,1,0:T(8,128)(2,1)S(1)} %copy-done.9), channel_id=1, source_target_pairs={{0,7},{1,24},{2,1},{3,26},{4,3},{5,28},{6,5},{7,30},{8,15},{9,0},{... | collective-permute-start | bytes 1572872 | tf_op jit(solution)/shard_map/ppermute | solution.py:327
  35.6 6.2 %gather_tables.6.refs_10_.refs_2_ = bf16[4,512,1024]{2,1,0:T(8,128)(2,1)} custom-call(s32[4,1,512]{2,1,0:T(1,128)S(1)} %copy.31.index_ref, bf16[1024,1024]{1,0:T(8,128)(2,1)S(1)} %bitcast.16), custom_call_target="tpu_custom_call" | custom-call | flops 4294967296 | bytes 4194304 | tf_op jit(solution)/shard_map/gather_tables/pallas_call | solution.py:83
  41.8 6.2 %gather_tables.7.refs_11_.refs_3_ = bf16[4,512,1024]{2,1,0:T(8,128)(2,1)} custom-call(s32[4,1,512]{2,1,0:T(1,128)S(1)} %slice.148.index_ref, bf16[1024,1024]{1,0:T(8,128)(2,1)S(1)} %bitcast.17), custom_call_target="tpu_custom_call" | custom-call | flops 4294967296 | bytes 4194304 | tf_op jit(solution)/shard_map/gather_tables/pallas_call | solution.py:83
  48.1 0.7 copy-done.3
  48.8 0.2 copy-done.4
  49.0 0.2 copy-done.5
  49.2 0.2 copy-done.6
  49.3 7.5 %collocate.1 = f32[8,1024]{1,0:T(8,128)S(1)} custom-call(s32[2,16]{1,0:T(2,128)S(1)} %pad_add_fusion.2.places_ref, bf16[4,256,256]{2,1,0:T(8,128)(2,1)S(1)} %copy-done.1, bf16[4,256,256]{2,1,0:T(8,128)(2,1)S(1)} %collective-permute-done.3.refs_1_, bf16[4,256,256]{2,1,0:T(8,128)(2,1)S(1)} %collective-permute-done.4.refs_2_, bf16[4,256,256]{2,1,0:T(8,128)(2,1)} %copy-done.3, ...), custom_call_target="tpu_custom_call" | custom-call | tf_op jit(solution)/shard_map/collocate/pallas_call | solution.py:140
  56.9 0.1 slice.152
  57.0 3.1 %collective-permute-start.10 = (f32[2,8,16]{2,1,0:T(8,128)S(1)}, f32[2,8,16]{2,1,0:T(8,128)S(1)}, u32[]{:S(2)}, u32[]{:S(2)}) collective-permute-start(f32[2,8,16]{2,1,0:T(8,128)S(1)} %slice.152), channel_id=1, source_target_pairs={{0,32},{32,64},{64,96},{96,128},{128,160},{160,192},{192,224},{224... | collective-permute-start | bytes 3080 | tf_op jit(solution)/shard_map/ppermute | solution.py:266
  60.1 0.1 reshape.114
  60.2 0.1 slice.154
  60.3 1.2 collective-permute-done.10
  61.5 3.7 %collective-permute-done.11 = f32[2,8,16]{2,1,0:T(8,128)S(1)} collective-permute-done((f32[2,8,16]{2,1,0:T(8,128)S(1)}, f32[2,8,16]{2,1,0:T(8,128)S(1)}, u32[]{:S(2)}, u32[]{:S(2)}) %collective-permute-start.11) | collective-permute-done | bytes 1056 | tf_op jit(solution)/shard_map/ppermute | solution.py:267
  65.1 0.1 collective-permute-start.12
  65.2 0.8 collective-permute-start.13
  66.1 0.3 collective-permute-done.12
  66.4 2.0 %collective-permute-done.13 = f32[12,2,16]{2,1,0:T(2,128)S(1)} collective-permute-done((f32[12,2,16]{2,1,0:T(2,128)S(1)}, f32[12,2,16]{2,1,0:T(2,128)S(1)}, u32[]{:S(2)}, u32[]{:S(2)}) %collective-permute-start.13) | collective-permute-done | bytes 1568 | tf_op jit(solution)/shard_map/ppermute | solution.py:277
  68.5 0.1 fusion.51
  68.6 0.1 fusion.52
  68.7 0.1 fusion.48
  68.8 0.1 fusion.53
  68.9 0.1 fusion.54
  69.1 0.1 fusion.9
  69.2 0.1 mul.151.scaled_ref
  69.3 8.4 %integrate.1 = (bf16[4,256,256]{2,1,0:T(8,128)(2,1)}, bf16[4,256,256]{2,1,0:T(8,128)(2,1)}, bf16[4,256,256]{2,1,0:T(8,128)(2,1)}, bf16[4,256,256]{2,1,0:T(8,128)...) custom-call(s32[2,16]{1,0:T(2,128)S(1)} %pad_add_fusion.1.places_ref, ...), custom_call_target="tpu_custom_call" | custom-call | tf_op jit(solution)/shard_map/integrate/pallas_call | solution.py:196
  77.6 2.6 %collective-permute-start.14 = (bf16[4,256,256]{2,1,0:T(8,128)(2,1)}, bf16[4,256,256]{2,1,0:T(8,128)(2,1)S(1)}, u32[]{:S(2)}, u32[]{:S(2)}) collective-permute-start(bf16[4,256,256]{2,1,0:T(8,128)(2,1)} %get-tuple-element.38), channel_id=1, source_target_pairs={{0,1},{1,0},{2,3},{3,2},{4,5},{5,4},{6,7},{7,6},{8,9},{9,8},{10,11... | collective-permute-start | bytes 1572872 | tf_op jit(solution)/shard_map/ppermute | solution.py:327
  80.2 3.8 %collective-permute-start.16 = (bf16[4,256,256]{2,1,0:T(8,128)(2,1)}, bf16[4,256,256]{2,1,0:T(8,128)(2,1)S(1)}, u32[]{:S(2)}, u32[]{:S(2)}) collective-permute-start(bf16[4,256,256]{2,1,0:T(8,128)(2,1)} %get-tuple-element.40), channel_id=1, source_target_pairs={{0,2},{1,9},{2,4},{3,11},{4,6},{5,13},{6,0},{7,15},{8,10},{9,17},{... | collective-permute-start | bytes 1572872 | tf_op jit(solution)/shard_map/ppermute | solution.py:327
  84.1 1.4 %collective-permute-start.17 = (bf16[4,256,256]{2,1,0:T(8,128)(2,1)}, bf16[4,256,256]{2,1,0:T(8,128)(2,1)S(1)}, u32[]{:S(2)}, u32[]{:S(2)}) collective-permute-start(bf16[4,256,256]{2,1,0:T(8,128)(2,1)} %get-tuple-element.41), channel_id=1, source_target_pairs={{0,4},{1,17},{2,6},{3,19},{4,0},{5,21},{6,2},{7,23},{8,12},{9,25},... | collective-permute-start | bytes 1572872 | tf_op jit(solution)/shard_map/ppermute | solution.py:327
  85.5 0.2 collective-permute-start.18
  85.6 0.3 collective-permute-start.19
  85.9 6.6 %collective-permute-done.15.refs_2_ = bf16[4,256,256]{2,1,0:T(8,128)(2,1)S(1)} collective-permute-done((bf16[4,256,256]{2,1,0:T(8,128)(2,1)}, bf16[4,256,256]{2,1,0:T(8,128)(2,1)S(1)}, u32[]{:S(2)}, u32[]{:S(2)}) %collective-permute-start.15) | collective-permute-done | bytes 524320 | tf_op jit(solution)/shard_map/ppermute | solution.py:327
  92.5 11.2 %collective-permute-start.20 = (bf16[4,256,256]{2,1,0:T(8,128)(2,1)}, bf16[4,256,256]{2,1,0:T(8,128)(2,1)}, u32[]{:S(2)}, u32[]{:S(2)}) collective-permute-start(bf16[4,256,256]{2,1,0:T(8,128)(2,1)} %get-tuple-element.44), channel_id=1, source_target_pairs={{0,25},{1,6},{2,27},{3,0},{4,29},{5,2},{6,31},{7,4},{8,1},{9,14},{... | collective-permute-start | bytes 1572872 | tf_op jit(solution)/shard_map/ppermute | solution.py:327
  103.6 0.1 copy.32.numbers_ref
  103.8 1.2 collective-permute-done.16.refs_3_
  105.0 1.7 %collective-permute-done.17.refs_4_ = bf16[4,256,256]{2,1,0:T(8,128)(2,1)S(1)} collective-permute-done((bf16[4,256,256]{2,1,0:T(8,128)(2,1)}, bf16[4,256,256]{2,1,0:T(8,128)(2,1)S(1)}, u32[]{:S(2)}, u32[]{:S(2)}) %collective-permute-start.17) | collective-permute-done | bytes 524320 | tf_op jit(solution)/shard_map/ppermute | solution.py:327
  106.7 4.0 %collective-permute-done.20.refs_7_ = bf16[4,256,256]{2,1,0:T(8,128)(2,1)} collective-permute-done((bf16[4,256,256]{2,1,0:T(8,128)(2,1)}, bf16[4,256,256]{2,1,0:T(8,128)(2,1)}, u32[]{:S(2)}, u32[]{:S(2)}) %collective-permute-start.20) | collective-permute-done | bytes 524320 | tf_op jit(solution)/shard_map/ppermute | solution.py:327
  110.7 1.0 copy-done
  111.7 1.5 %add_up.5 = bf16[3,256,256]{2,1,0:T(8,128)(2,1)S(1)} custom-call(s32[8]{0:T(128)S(1)} %fusion.26.bricks_ref, s32[32,4]{1,0:T(8,128)S(1)} %copy.32.numbers_ref, bf16[4,256,256]{2,1,0:T(8,128)(2,1)S(1)} %copy-done, bf16[4,256,256]{2,1,0:T(8,128)(2,1)S(1)} %collective-permute-done.14.refs_1_, bf16[4,256,256]{2,1,0:T(8,128)(2,1)S(1)} %collective-permute-done.15.refs_2_, ...), custom_call_target="tpu_custom_call" | custom-call | tf_op jit(solution)/shard_map/add_up/pallas_call | solution.py:238
  113.2 0.1 collective-permute-start.21
  113.3 2.1 %add_up.6 = bf16[3,256,256]{2,1,0:T(8,128)(2,1)S(1)} custom-call(s32[8]{0:T(128)S(1)} %fusion.26.bricks_ref, s32[32,4]{1,0:T(8,128)S(1)} %copy.32.numbers_ref, bf16[4,256,256]{2,1,0:T(8,128)(2,1)S(1)} %copy-done, bf16[4,256,256]{2,1,0:T(8,128)(2,1)S(1)} %collective-permute-done.14.refs_1_, bf16[4,256,256]{2,1,0:T(8,128)(2,1)S(1)} %collective-permute-done.15.refs_2_, ...), custom_call_target="tpu_custom_call" | custom-call | tf_op jit(solution)/shard_map/add_up/pallas_call | solution.py:238
  115.4 6.2 %collective-permute-start.22 = (bf16[3,256,256]{2,1,0:T(8,128)(2,1)S(1)}, bf16[3,256,256]{2,1,0:T(8,128)(2,1)S(1)}, u32[]{:S(2)}, u32[]{:S(2)}) collective-permute-start(bf16[3,256,256]{2,1,0:T(8,128)(2,1)S(1)} %add_up.6), channel_id=1, source_target_pairs={{0,8},{1,3},{2,10},{3,5},{4,12},{5,7},{6,14},{7,1},{8,16},{9,11},{... | collective-permute-start | bytes 1179656 | tf_op jit(solution)/shard_map/ppermute | solution.py:327
  121.7 2.6 %add_up.7 = bf16[3,256,256]{2,1,0:T(8,128)(2,1)S(1)} custom-call(s32[8]{0:T(128)S(1)} %fusion.26.bricks_ref, s32[32,4]{1,0:T(8,128)S(1)} %copy.32.numbers_ref, bf16[4,256,256]{2,1,0:T(8,128)(2,1)S(1)} %copy-done, bf16[4,256,256]{2,1,0:T(8,128)(2,1)S(1)} %collective-permute-done.14.refs_1_, bf16[4,256,256]{2,1,0:T(8,128)(2,1)S(1)} %collective-permute-done.15.refs_2_, ...), custom_call_target="tpu_custom_call" | custom-call | tf_op jit(solution)/shard_map/add_up/pallas_call | solution.py:238
  124.3 0.1 collective-permute-start.23
  124.4 2.8 %add_up.4 = f32[3,256,256]{2,1,0:T(8,128)S(1)} custom-call(s32[8]{0:T(128)S(1)} %fusion.26.bricks_ref, s32[32,4]{1,0:T(8,128)S(1)} %copy.32.numbers_ref, bf16[4,256,256]{2,1,0:T(8,128)(2,1)S(1)} %copy-done, bf16[4,256,256]{2,1,0:T(8,128)(2,1)S(1)} %collective-permute-done.14.refs_1_, bf16[4,256,256]{2,1,0:T(8,128)(2,1)S(1)} %collective-permute-done.15.refs_2_, ...), custom_call_target="tpu_custom_call" | custom-call | tf_op jit(solution)/shard_map/add_up/pallas_call | solution.py:238
  127.2 5.0 %collective-permute-done.23 = bf16[3,256,256]{2,1,0:T(8,128)(2,1)S(1)} collective-permute-done((bf16[3,256,256]{2,1,0:T(8,128)(2,1)S(1)}, bf16[3,256,256]{2,1,0:T(8,128)(2,1)S(1)}, u32[]{:S(2)}, u32[]{:S(2)}) %collective-permute-start.23) | collective-permute-done | bytes 393248 | tf_op jit(solution)/shard_map/ppermute | solution.py:327
  132.1 1.0 convert_add_fusion
  (63 shorter events, 0.6 us)
Async XLA Ops:
  0.0 17.0 %collective-permute-start = (bf16[3,256,256]{2,1,0:T(8,128)(2,1)}, bf16[3,256,256]{2,1,0:T(8,128)(2,1)S(1)}, u32[]{:S(2)}, u32[]{:S(2)}) collective-permute-start(bf16[3,256,256]{2,1,0:T(8,128)(2,1)} %refs_0_.1), channel_id=1, source_target_pairs={{0,8},{1,3},{2,10},{3,5},{4,12},{5,7},{6,14},{7,1},{8,16},{9,11},{... | collective-permute-start | bytes 1179656 | tf_op jit(solution)/shard_map/ppermute | solution.py:327
  1.5 15.5 %collective-permute-start.1 = (bf16[3,256,256]{2,1,0:T(8,128)(2,1)}, bf16[3,256,256]{2,1,0:T(8,128)(2,1)S(1)}, u32[]{:S(2)}, u32[]{:S(2)}) collective-permute-start(bf16[3,256,256]{2,1,0:T(8,128)(2,1)} %refs_0_.1), channel_id=1, source_target_pairs={{0,16},{1,5},{2,18},{3,7},{4,20},{5,1},{6,22},{7,3},{8,24},{9,13},... | collective-permute-start | bytes 1179656 | tf_op jit(solution)/shard_map/ppermute | solution.py:327
  4.2 12.8 %collective-permute-start.2 = (bf16[3,256,256]{2,1,0:T(8,128)(2,1)}, bf16[3,256,256]{2,1,0:T(8,128)(2,1)S(1)}, u32[]{:S(2)}, u32[]{:S(2)}) collective-permute-start(bf16[3,256,256]{2,1,0:T(8,128)(2,1)} %refs_0_.1), channel_id=1, source_target_pairs={{0,24},{1,7},{2,26},{3,1},{4,28},{5,3},{6,30},{7,5},{8,0},{9,15},{... | collective-permute-start | bytes 1179656 | tf_op jit(solution)/shard_map/ppermute | solution.py:327
  10.7 6.3 %copy-start.2 = (bf16[3,256,256]{2,1,0:T(8,128)(2,1)S(1)}, bf16[3,256,256]{2,1,0:T(8,128)(2,1)}, u32[]{:S(2)}) copy-start(bf16[3,256,256]{2,1,0:T(8,128)(2,1)} %refs_0_.1) | copy-start | bytes 1179652
  19.5 10.3 %collective-permute-start.6 = (bf16[4,256,256]{2,1,0:T(8,128)(2,1)}, bf16[4,256,256]{2,1,0:T(8,128)(2,1)}, u32[]{:S(2)}, u32[]{:S(2)}) collective-permute-start(bf16[4,256,256]{2,1,0:T(8,128)(2,1)} %get-tuple-element.30), channel_id=1, source_target_pairs={{0,1},{1,0},{2,3},{3,2},{4,5},{5,4},{6,7},{7,6},{8,9},{9,8},{10,11... | collective-permute-start | bytes 1572872 | tf_op jit(solution)/shard_map/ppermute | solution.py:327
  19.6 13.1 %collective-permute-start.3 = (bf16[4,256,256]{2,1,0:T(8,128)(2,1)}, bf16[4,256,256]{2,1,0:T(8,128)(2,1)S(1)}, u32[]{:S(2)}, u32[]{:S(2)}) collective-permute-start(bf16[4,256,256]{2,1,0:T(8,128)(2,1)} %get-tuple-element.26), channel_id=1, source_target_pairs={{0,2},{1,9},{2,4},{3,11},{4,6},{5,13},{6,0},{7,15},{8,10},{9,17},{... | collective-permute-start | bytes 1572872 | tf_op jit(solution)/shard_map/ppermute | solution.py:327
  19.8 28.2 %collective-permute-start.4 = (bf16[4,256,256]{2,1,0:T(8,128)(2,1)}, bf16[4,256,256]{2,1,0:T(8,128)(2,1)S(1)}, u32[]{:S(2)}, u32[]{:S(2)}) collective-permute-start(bf16[4,256,256]{2,1,0:T(8,128)(2,1)} %get-tuple-element.27), channel_id=1, source_target_pairs={{0,4},{1,17},{2,6},{3,19},{4,0},{5,21},{6,2},{7,23},{8,12},{9,25},... | collective-permute-start | bytes 1572872 | tf_op jit(solution)/shard_map/ppermute | solution.py:327
  22.7 25.3 %collective-permute-start.5 = (bf16[4,256,256]{2,1,0:T(8,128)(2,1)}, bf16[4,256,256]{2,1,0:T(8,128)(2,1)S(1)}, u32[]{:S(2)}, u32[]{:S(2)}) collective-permute-start(bf16[4,256,256]{2,1,0:T(8,128)(2,1)} %get-tuple-element.28), channel_id=1, source_target_pairs={{0,6},{1,25},{2,0},{3,27},{4,2},{5,29},{6,4},{7,31},{8,14},{9,1},{... | collective-permute-start | bytes 1572872 | tf_op jit(solution)/shard_map/ppermute | solution.py:327
  22.7 7.1 %copy-start.10 = (bf16[4,256,256]{2,1,0:T(8,128)(2,1)S(1)}, bf16[4,256,256]{2,1,0:T(8,128)(2,1)}, u32[]{:S(2)}) copy-start(bf16[4,256,256]{2,1,0:T(8,128)(2,1)} %get-tuple-element.32) | copy-start | bytes 1572868
  22.7 10.0 %copy-start.9 = (bf16[4,256,256]{2,1,0:T(8,128)(2,1)S(1)}, bf16[4,256,256]{2,1,0:T(8,128)(2,1)}, u32[]{:S(2)}) copy-start(bf16[4,256,256]{2,1,0:T(8,128)(2,1)} %get-tuple-element.33) | copy-start | bytes 1572868
  22.7 25.3 %collective-permute-start.7 = (bf16[4,256,256]{2,1,0:T(8,128)(2,1)}, bf16[4,256,256]{2,1,0:T(8,128)(2,1)S(1)}, u32[]{:S(2)}, u32[]{:S(2)}) collective-permute-start(bf16[4,256,256]{2,1,0:T(8,128)(2,1)} %get-tuple-element.31), channel_id=1, source_target_pairs={{0,3},{1,8},{2,5},{3,10},{4,7},{5,12},{6,1},{7,14},{8,11},{9,16},{... | collective-permute-start | bytes 1572872 | tf_op jit(solution)/shard_map/ppermute | solution.py:327
  29.8 18.3 %collective-permute-start.8 = (bf16[4,256,256]{2,1,0:T(8,128)(2,1)S(1)}, bf16[4,256,256]{2,1,0:T(8,128)(2,1)S(1)}, u32[]{:S(2)}, u32[]{:S(2)}) collective-permute-start(bf16[4,256,256]{2,1,0:T(8,128)(2,1)S(1)} %copy-done.10), channel_id=1, source_target_pairs={{0,5},{1,16},{2,7},{3,18},{4,1},{5,20},{6,3},{7,22},{8,13},{9,24},... | collective-permute-start | bytes 1572872 | tf_op jit(solution)/shard_map/ppermute | solution.py:327
  32.7 15.4 %collective-permute-start.9 = (bf16[4,256,256]{2,1,0:T(8,128)(2,1)S(1)}, bf16[4,256,256]{2,1,0:T(8,128)(2,1)S(1)}, u32[]{:S(2)}, u32[]{:S(2)}) collective-permute-start(bf16[4,256,256]{2,1,0:T(8,128)(2,1)S(1)} %copy-done.9), channel_id=1, source_target_pairs={{0,7},{1,24},{2,1},{3,26},{4,3},{5,28},{6,5},{7,30},{8,15},{9,0},{... | collective-permute-start | bytes 1572872 | tf_op jit(solution)/shard_map/ppermute | solution.py:327
  41.8 7.5 %copy-start.1 = (bf16[4,256,256]{2,1,0:T(8,128)(2,1)S(1)}, bf16[4,256,256]{2,1,0:T(8,128)(2,1)}, u32[]{:S(2)}) copy-start(bf16[4,256,256]{2,1,0:T(8,128)(2,1)} %get-tuple-element.25.refs_0_) | copy-start | bytes 1572868
  48.0 0.8 copy-start.3
  48.0 1.0 copy-start.4
  48.0 1.1 copy-start.5
  48.1 1.3 copy-start.6
  57.0 4.5 %collective-permute-start.10 = (f32[2,8,16]{2,1,0:T(8,128)S(1)}, f32[2,8,16]{2,1,0:T(8,128)S(1)}, u32[]{:S(2)}, u32[]{:S(2)}) collective-permute-start(f32[2,8,16]{2,1,0:T(8,128)S(1)} %slice.152), channel_id=1, source_target_pairs={{0,32},{32,64},{64,96},{96,128},{128,160},{160,192},{192,224},{224... | collective-permute-start | bytes 3080 | tf_op jit(solution)/shard_map/ppermute | solution.py:266
  60.2 4.9 %collective-permute-start.11 = (f32[2,8,16]{2,1,0:T(8,128)S(1)}, f32[2,8,16]{2,1,0:T(8,128)S(1)}, u32[]{:S(2)}, u32[]{:S(2)}) collective-permute-start(f32[2,8,16]{2,1,0:T(8,128)S(1)} %slice.154), channel_id=1, source_target_pairs={{32,0},{64,32},{96,64},{128,96},{160,128},{192,160},{224,192},{0,2... | collective-permute-start | bytes 3080 | tf_op jit(solution)/shard_map/ppermute | solution.py:267
  65.1 1.3 collective-permute-start.12
  65.2 3.2 %collective-permute-start.13 = (f32[12,2,16]{2,1,0:T(2,128)S(1)}, f32[12,2,16]{2,1,0:T(2,128)S(1)}, u32[]{:S(2)}, u32[]{:S(2)}) collective-permute-start(f32[12,2,16]{2,1,0:T(2,128)S(1)} %get-tuple-element.77), channel_id=1, source_target_pairs={{0,31},{1,2},{2,1},{3,4},{4,3},{5,6},{6,5},{7,8},{8,7},{9,10},{10,... | collective-permute-start | bytes 4616 | tf_op jit(solution)/shard_map/ppermute | solution.py:277
  69.3 34.5 %copy-start.7 = (pred[8]{0:T(512)(128)(4,1)S(1)}, pred[8]{0:T(512)(128)(4,1)}, u32[]{:S(2)}) copy-start(pred[8]{0:T(512)(128)(4,1)} %constant.184.clone) | copy-start | bytes 28
  69.3 34.5 %copy-start.8 = (s32[8]{0:T(128)S(1)}, s32[8]{0:T(128)}, u32[]{:S(2)}) copy-start(s32[8]{0:T(128)} %constant.189) | copy-start | bytes 100
  77.6 8.0 %collective-permute-start.14 = (bf16[4,256,256]{2,1,0:T(8,128)(2,1)}, bf16[4,256,256]{2,1,0:T(8,128)(2,1)S(1)}, u32[]{:S(2)}, u32[]{:S(2)}) collective-permute-start(bf16[4,256,256]{2,1,0:T(8,128)(2,1)} %get-tuple-element.38), channel_id=1, source_target_pairs={{0,1},{1,0},{2,3},{3,2},{4,5},{5,4},{6,7},{7,6},{8,9},{9,8},{10,11... | collective-permute-start | bytes 1572872 | tf_op jit(solution)/shard_map/ppermute | solution.py:327
  80.2 12.2 %collective-permute-start.15 = (bf16[4,256,256]{2,1,0:T(8,128)(2,1)}, bf16[4,256,256]{2,1,0:T(8,128)(2,1)S(1)}, u32[]{:S(2)}, u32[]{:S(2)}) collective-permute-start(bf16[4,256,256]{2,1,0:T(8,128)(2,1)} %get-tuple-element.39), channel_id=1, source_target_pairs={{0,6},{1,25},{2,0},{3,27},{4,2},{5,29},{6,4},{7,31},{8,14},{9,1},{... | collective-permute-start | bytes 1572872 | tf_op jit(solution)/shard_map/ppermute | solution.py:327
  80.2 24.7 %collective-permute-start.16 = (bf16[4,256,256]{2,1,0:T(8,128)(2,1)}, bf16[4,256,256]{2,1,0:T(8,128)(2,1)S(1)}, u32[]{:S(2)}, u32[]{:S(2)}) collective-permute-start(bf16[4,256,256]{2,1,0:T(8,128)(2,1)} %get-tuple-element.40), channel_id=1, source_target_pairs={{0,2},{1,9},{2,4},{3,11},{4,6},{5,13},{6,0},{7,15},{8,10},{9,17},{... | collective-permute-start | bytes 1572872 | tf_op jit(solution)/shard_map/ppermute | solution.py:327
  84.1 22.6 %collective-permute-start.17 = (bf16[4,256,256]{2,1,0:T(8,128)(2,1)}, bf16[4,256,256]{2,1,0:T(8,128)(2,1)S(1)}, u32[]{:S(2)}, u32[]{:S(2)}) collective-permute-start(bf16[4,256,256]{2,1,0:T(8,128)(2,1)} %get-tuple-element.41), channel_id=1, source_target_pairs={{0,4},{1,17},{2,6},{3,19},{4,0},{5,21},{6,2},{7,23},{8,12},{9,25},... | collective-permute-start | bytes 1572872 | tf_op jit(solution)/shard_map/ppermute | solution.py:327
  85.5 21.2 %collective-permute-start.18 = (bf16[4,256,256]{2,1,0:T(8,128)(2,1)}, bf16[4,256,256]{2,1,0:T(8,128)(2,1)S(1)}, u32[]{:S(2)}, u32[]{:S(2)}) collective-permute-start(bf16[4,256,256]{2,1,0:T(8,128)(2,1)} %get-tuple-element.42), channel_id=1, source_target_pairs={{0,17},{1,4},{2,19},{3,6},{4,21},{5,0},{6,23},{7,2},{8,25},{9,12},... | collective-permute-start | bytes 1572872 | tf_op jit(solution)/shard_map/ppermute | solution.py:327
  85.6 21.0 %collective-permute-start.19 = (bf16[4,256,256]{2,1,0:T(8,128)(2,1)}, bf16[4,256,256]{2,1,0:T(8,128)(2,1)S(1)}, u32[]{:S(2)}, u32[]{:S(2)}) collective-permute-start(bf16[4,256,256]{2,1,0:T(8,128)(2,1)} %get-tuple-element.43), channel_id=1, source_target_pairs={{0,9},{1,2},{2,11},{3,4},{4,13},{5,6},{6,15},{7,0},{8,17},{9,10},{... | collective-permute-start | bytes 1572872 | tf_op jit(solution)/shard_map/ppermute | solution.py:327
  92.5 18.2 %collective-permute-start.20 = (bf16[4,256,256]{2,1,0:T(8,128)(2,1)}, bf16[4,256,256]{2,1,0:T(8,128)(2,1)}, u32[]{:S(2)}, u32[]{:S(2)}) collective-permute-start(bf16[4,256,256]{2,1,0:T(8,128)(2,1)} %get-tuple-element.44), channel_id=1, source_target_pairs={{0,25},{1,6},{2,27},{3,0},{4,29},{5,2},{6,31},{7,4},{8,1},{9,14},{... | collective-permute-start | bytes 1572872 | tf_op jit(solution)/shard_map/ppermute | solution.py:327
  110.7 1.0 copy-start
  113.2 13.9 %collective-permute-start.21 = (bf16[3,256,256]{2,1,0:T(8,128)(2,1)S(1)}, bf16[3,256,256]{2,1,0:T(8,128)(2,1)S(1)}, u32[]{:S(2)}, u32[]{:S(2)}) collective-permute-start(bf16[3,256,256]{2,1,0:T(8,128)(2,1)S(1)} %add_up.5), channel_id=1, source_target_pairs={{0,16},{1,5},{2,18},{3,7},{4,20},{5,1},{6,22},{7,3},{8,24},{9,13},... | collective-permute-start | bytes 1179656 | tf_op jit(solution)/shard_map/ppermute | solution.py:327
  115.4 11.7 %collective-permute-start.22 = (bf16[3,256,256]{2,1,0:T(8,128)(2,1)S(1)}, bf16[3,256,256]{2,1,0:T(8,128)(2,1)S(1)}, u32[]{:S(2)}, u32[]{:S(2)}) collective-permute-start(bf16[3,256,256]{2,1,0:T(8,128)(2,1)S(1)} %add_up.6), channel_id=1, source_target_pairs={{0,8},{1,3},{2,10},{3,5},{4,12},{5,7},{6,14},{7,1},{8,16},{9,11},{... | collective-permute-start | bytes 1179656 | tf_op jit(solution)/shard_map/ppermute | solution.py:327
  124.3 7.9 %collective-permute-start.23 = (bf16[3,256,256]{2,1,0:T(8,128)(2,1)S(1)}, bf16[3,256,256]{2,1,0:T(8,128)(2,1)S(1)}, u32[]{:S(2)}, u32[]{:S(2)}) collective-permute-start(bf16[3,256,256]{2,1,0:T(8,128)(2,1)S(1)} %add_up.7), channel_id=1, source_target_pairs={{0,24},{1,7},{2,26},{3,1},{4,28},{5,3},{6,30},{7,5},{8,0},{9,15},{... | collective-permute-start | bytes 1179656 | tf_op jit(solution)/shard_map/ppermute | solution.py:327
